TPU v7x, 32 devices: a whole 2x2x4 slice. The times are simulated.
32 devices in a mesh: row: 4 (over y, x), col: 8 (over z, core).
Axes of the slice: x: 2, y: 2, z: 4, core: 2. Of those that a mesh axis runs over, the one named last changes fastest.
Arguments:
- slip: float32 [65536, 256], P(('row', 'col')), may hold values from -2 to 2
- state: float32 [65536, 256], P(('row', 'col')), may hold values from 0.4 to 0.9
- tau_load: float32 [65536], P(('row', 'col')), may hold values from 1 to 2
- normal_stress: float32 [65536], P(('row', 'col')), may hold values from 6 to 8
- direct_effect: float32 [65536], P(('row', 'col')), may hold values from 0.8 to 1.6
- evolution_effect: float32 [65536], P(('row', 'col')), may hold values from 0.5 to 1
- slip_distance: float32 [65536], P(('row', 'col')), may hold values from 0.5 to 2
- self_stiffness: float32 [65536], P(('row', 'col')), may hold values from 0.5 to 2
- near_blocks: bfloat16 [3, 65536, 256], P(None, ('row', 'col')), may hold values from -0.21875 to 0.21875
- basis_in: bfloat16 [32, 65536], P(None, ('row', 'col')), may hold values from -0.375 to 0.375
- basis_out: bfloat16 [32, 65536], P(None, ('row', 'col')), may hold values from -1 to 1
- coupling: bfloat16 [8192, 4, 2048], P('row', None, 'col'), may hold values from -0.09375 to 0.09375
- block_rank: int32 [256, 4, 64], P('row', None, 'col'), may hold values from 8 to 32
- adj_bricks: int32 [8, 65536], P(None, ('row', 'col')), may hold values from 0 to 1023
- adj_count: int32 [65536], P(('row', 'col')), may hold values from 1 to 8
- adj_weight: float32 [8, 65536], P(None, ('row', 'col')), may hold values from 0.05 to 1
- pressure_now: bfloat16 [1024, 256], P('col'), may hold values from 0.099609375 to 1
- pressure_rate: bfloat16 [1024, 256], P('col'), may hold values from 0.5 to 5
Outputs:
- slip_out: float32 [65536, 256], P(('row', 'col'))
- state_out: float32 [65536, 256], P(('row', 'col'))
Inputs may be any that keep to these rules, and one draw needn't show every extreme that they name: Only the first adj_count entries of a patch's brick list are read. `adj_bricks`: brick numbers index the whole reservoir. `block_rank`: ranks of pairs with |i - j| <= 1 are not read.
All inputs are finite; a program needn't handle non-finite values.
Results may differ from a plain program's by a relative error of at most 0.0007.
Values may be sent and summed in bfloat16 or wider, within the bound.
No kernel may reach another device: no remote copies, remote signals or barrier semaphores. Data moves between devices by JAX's collectives and lax.ppermute only.
A program may use at most 192 MiB of HBM per device.

v0:
```python
import functools

import jax
import jax.numpy as jnp
from jax import lax
from jax.experimental import pallas as pl
from jax.experimental.pallas import tpu as pltpu
from jax.sharding import PartitionSpec as P

BS = 256
R = 32

STEP_SIZE = 0.5
REF_FRICTION = 0.6
LIMIT = 16 * 1024 * 1024
F32 = jnp.float32
BF16 = jnp.bfloat16


def dot(a, b):
    return jnp.dot(a, b, preferred_element_type=F32)


def dot_t(a, b):
    return lax.dot_general(a, b, (((0,), (0,)), ((), ())), preferred_element_type=F32)


VMEM = pl.BlockSpec(memory_space=pltpu.VMEM)


def call(kernel, outs, *operands, specs=None, **grid):
    return pl.pallas_call(
        kernel,
        in_specs=specs or [VMEM] * len(operands),
        out_shape=outs,
        compiler_params=pltpu.CompilerParams(vmem_limit_bytes=LIMIT),
        **grid,
    )(*operands)


def rows_at(n, size):
    return pl.ds(pl.multiple_of(n * size, size), size)


HBM = pl.BlockSpec(memory_space=pl.ANY)


def in_hbm(*arrays):
    return [pltpu.with_memory_space_constraint(array, pltpu.HBM) for array in arrays]


def start_copies(pairs, sems, first=0):
    copies = [pltpu.make_async_copy(a, b, sems.at[first + k]) for k, (a, b) in enumerate(pairs)]
    for copy in copies:
        copy.start()
    return copies


def fill_edges(rounded_ref, pair_ref, cross_ref):
    even = lax.rem(lax.axis_index("col"), 2) == 0
    first, last = rounded_ref[:BS], rounded_ref[-BS:]
    pair_ref[...] = jnp.where(even, last, first)
    cross_ref[...] = jnp.where(even, first, last)


def project_kernel(slip_hbm, basis_hbm, coeff_ref, rounded_ref, pair_ref, cross_ref, slip_ref, basis_ref, sems):
    count = slip_ref.shape[0] // BS
    blocks = [pl.ds(n * BS, BS) for n in range(count)]
    copies = start_copies(
        [(basis_hbm, basis_ref)] + [(slip_hbm.at[at, :], slip_ref.at[at, :]) for at in blocks], sems
    )
    copies[0].wait()
    for n, at in enumerate(blocks):
        copies[1 + n].wait()
        rounded = slip_ref[at, :].astype(BF16)
        rounded_ref[at, :] = rounded
        coeff_ref[n * R : (n + 1) * R, :] = dot(basis_ref[:, at], rounded).astype(BF16)
    fill_edges(rounded_ref, pair_ref, cross_ref)


def project(slip, basis_in):
    patches, ens = slip.shape
    count = patches // BS
    edge = jax.ShapeDtypeStruct((BS, ens), BF16)
    return call(
        project_kernel,
        [
            jax.ShapeDtypeStruct((count * R, ens), BF16),
            jax.ShapeDtypeStruct((patches, ens), BF16),
            edge,
            edge,
            jax.ShapeDtypeStruct((patches, ens), F32),
        ],
        *in_hbm(slip, basis_in),
        specs=[HBM] * 2,
        scratch_shapes=[pltpu.VMEM(basis_in.shape, BF16), pltpu.SemaphoreType.DMA((1 + count,))],
    )


def ranks_kernel(
    col_count, rank_hbm, now_hbm, rate_hbm, wide_ref, joined_ref, rank_ref, sems
):
    sources, share, blocks = rank_ref.shape
    ens = now_hbm.shape[1]
    copies = start_copies(
        [
            (rank_hbm, rank_ref),
            (now_hbm, joined_ref.at[:, pl.ds(0, ens)]),
            (rate_hbm, joined_ref.at[:, pl.ds(ens, ens)]),
        ],
        sems,
    )
    width = share * R
    column = lax.broadcasted_iota(jnp.int32, (share, width), 1)
    spread = (lax.div(column, R) == lax.broadcasted_iota(jnp.int32, (share, width), 0)).astype(F32).astype(BF16)
    level = lax.rem(lax.broadcasted_iota(jnp.int32, (blocks, width), 1), R).astype(F32)
    receiver = lax.axis_index("row") * blocks + lax.broadcasted_iota(jnp.int32, (share, blocks), 1)
    copies[0].wait()
    for source in range(sources):
        own = (source * col_count + lax.axis_index("col")) * share + lax.broadcasted_iota(jnp.int32, (share, blocks), 0)
        rank = jnp.where(jnp.abs(receiver - own) > 1, rank_ref[source], 0).astype(F32)
        wide = dot_t(rank.astype(BF16), spread)
        wide_ref[source] = jnp.where(level < wide, wide, 0.0)
    copies[1].wait()
    copies[2].wait()


def side_by_side_kernel(*refs):
    pieces, out_ref = refs[:-1], refs[-1]
    size = pieces[0].shape[0]
    for k, piece in enumerate(pieces):
        out_ref[k * size : (k + 1) * size, :] = piece[...]


def weights_kernel(heights, size, start, *refs):
    begun = start > 0
    sources, rest = refs[:9], refs[9:]
    near_hbm, state_hbm, begun_ref = rest[:3] if begun else (None, None, None)
    rest = rest[4:] if begun else rest[1:]
    numbers_ref, matrix_ref = rest[:2]
    near_ref, state_ref = rest[2:4] if begun else (None, None)
    vectors, lists, sems = rest[-5], rest[-4:-1], rest[-1]
    targets = [vectors.at[k] for k in range(6)] + list(lists)
    copies = start_copies(list(zip(sources, targets)), sems)
    large = [(near_hbm, near_ref), (state_hbm, state_ref)] if begun else []
    large = start_copies(large, sems, len(targets))
    if begun:
        numbers_ref[:start, :] = begun_ref[...]
    count_ref, bricks_ref, weight_ref = lists
    slots = bricks_ref.shape[0]
    col = lax.axis_index("col")
    height, core = lax.div(col, 2).astype(F32), lax.rem(col, 2).astype(F32)
    group, lanes, unrolled = 16, 128, 8
    for copy in copies:
        copy.wait()

    @pl.loop(0, matrix_ref.shape[1] // lanes)
    def _(n):
        own_at = rows_at(n, lanes)
        at = pl.ds(pl.multiple_of(start + n * lanes, lanes), lanes)
        load, normal, direct, evolution, distance, stiffness = (vectors[k, :, at] for k in range(6))
        rows = [load, normal, 1.0 / direct, 1.0 / evolution, evolution / distance, stiffness, load, normal]
        numbers_ref[at if begun else own_at, :] = jnp.concatenate(rows, axis=0).T
        bricks = bricks_ref[:, at].astype(F32)
        live = lax.broadcasted_iota(jnp.int32, (slots, lanes), 0) < count_ref[:, at]
        weights = jnp.where(live, weight_ref[:, at], 0.0)
        merged = jnp.zeros((slots, lanes), F32)
        for k in range(slots):
            merged = merged + jnp.where(bricks == bricks[k : k + 1], weights[k : k + 1], 0.0)
        shares = merged / jnp.sum(weights, axis=0, keepdims=True)
        owner = jnp.floor((bricks + 0.5) * (1.0 / size))
        chip = jnp.floor(owner * 0.5 + 0.25)
        away = height - chip
        away = jnp.where(away < 0, away + heights, away)
        other = jnp.where(owner - 2.0 * chip == core, 0.0, float(heights))
        place = jnp.where(live, (other + away - owner) * size + bricks, -1.0)
        high = jnp.floor((place + 0.5) * (1.0 / group))
        low = place - high * group
        spread = lambda rows, k: jnp.broadcast_to(rows[k : k + 1], (group, lanes)).astype(BF16)
        line = lax.broadcasted_iota(jnp.int32, (group, lanes), 0).astype(F32).astype(BF16)
        none = jnp.full((group, lanes), -1.0, BF16)
        highs = [jnp.where(spread(low, k) == line, spread(high, k), none) for k in range(slots)]
        values = [spread(shares, k) for k in range(slots)]

        @pl.loop(0, matrix_ref.shape[0] // (group * unrolled))
        def _(m):
            first = jnp.full((group, lanes), (m * unrolled).astype(F32)).astype(BF16)
            for step in range(unrolled):
                here = first + jnp.asarray(step, BF16)
                tile = jnp.zeros((group, lanes), BF16)
                for k in range(slots):
                    tile = jnp.where(highs[k] == here, values[k], tile)
                to = pl.ds(pl.multiple_of((m * unrolled + step) * group, group), group)
                matrix_ref[to, own_at] = tile

    for copy in large:
        copy.wait()


def couple_kernel(sources, heights, flip, matrix_ref, *refs):
    coeffs, edges, out_ref = refs[:sources], refs[sources:-1], refs[-1]
    share = coeffs[0].shape[0]
    row, col = lax.axis_index("row"), lax.axis_index("col")
    height, core = lax.div(col, 2), lax.rem(col + flip, 2)

    @pl.loop(0, heights)
    def _(d):
        at = rows_at(2 * lax.rem(height + d, heights) + core, share)
        total = None
        for step in range(sources):
            term = dot(matrix_ref[lax.rem(row + (sources - step), sources), at, :], coeffs[step][...])
            total = term if total is None else total + term
        out_ref[rows_at(d, share), :] = total.astype(out_ref.dtype)

    for edge in edges:
        out_ref[heights * share :, :] = edge[...]


def couple(flip, matrix, coeffs, heights, kind, *edges):
    share, ens = coeffs[0].shape
    return call(
        functools.partial(couple_kernel, len(coeffs), heights, flip),
        jax.ShapeDtypeStruct((heights * share + len(edges) * BS, ens), kind),
        matrix,
        *coeffs,
        *edges,
    )


def chip_sum_kernel(kept_ref, sent_ref, *outs):
    share = outs[0].shape[0]
    for d, out_ref in enumerate(outs):

        @pl.loop(0, share // 32)
        def _(n):
            at = pl.ds(pl.multiple_of(d * share + n * 32, 32), 32)
            out_ref[rows_at(n, 32), :] = (kept_ref[at, :] + sent_ref[at, :].astype(F32)).astype(BF16)


def chip_sum(kept, sent, heights):
    rows, ens = kept.shape
    return list(call(chip_sum_kernel, [jax.ShapeDtypeStruct((rows // heights, ens), BF16)] * heights, kept, sent))


def near_tau(n, slip, numbers, near_ref, rounded_ref):
    count = rounded_ref.shape[0] // BS
    at = rows_at(n, BS)
    none = jnp.zeros((BS, rounded_ref.shape[1]), BF16)
    before = jnp.where(n == 0, none, rounded_ref[rows_at(jnp.maximum(n - 1, 0), BS), :])
    after = jnp.where(n == count - 1, none, rounded_ref[rows_at(jnp.minimum(n + 1, count - 1), BS), :])
    near = dot(near_ref[0, at, :], before) + dot(near_ref[1, at, :], rounded_ref[at, :]) + dot(near_ref[2, at, :], after)
    return numbers[:, 0:1] - numbers[:, 5:6] * slip - near


def prepare_first_kernel(
    low_ref, high_ref, own_ref, other_ref, slip_ref, state_ref, numbers_ref, near_ref, rounded_ref,
    shift_ref, scale_ref, rest_ref, scale_mid_ref,
):
    half = own_ref.shape[0]
    ens = slip_ref.shape[1]
    blocks = low_ref.shape[1] // BS

    def block(matrix_ref, m, n):
        at, own_at = rows_at(n, BS), rows_at(m, BS)
        total = dot_t(matrix_ref[:half, own_at], own_ref[...]) + dot_t(matrix_ref[half:, own_at], other_ref[...])
        numbers = numbers_ref[at, :]
        normal, inv_direct, inv_evolution, ratio = (numbers[:, k : k + 1] for k in range(1, 5))
        base = total[:, :ens]
        scale = inv_direct / (normal - base)
        scale_ref[at, :] = scale
        scale_mid_ref[at, :] = inv_direct / (normal - (base + STEP_SIZE * total[:, ens:]))
        state = state_ref[at, :]
        tau = near_tau(n, slip_ref[at, :], numbers, near_ref, rounded_ref)
        shift_ref[at, :] = tau * scale - state * inv_direct
        rest_ref[at, :] = state + (STEP_SIZE * ratio) * jnp.exp((REF_FRICTION - state) * inv_evolution)

    @pl.loop(0, blocks)
    def _(m):
        block(low_ref, m, m)

    @pl.loop(0, blocks)
    def _(m):
        block(high_ref, m, blocks + m)


def over_blocks(block, basis_ref, near_ref, parts, pair_ref, cross_ref):
    count = near_ref.shape[1] // BS

    def far(n):
        levels = rows_at(n, R)
        total = parts[0][levels, :].astype(F32)
        for part in parts[1:]:
            total = total + part[levels, :].astype(F32)
        return dot_t(basis_ref[:, rows_at(n, BS)], total.astype(BF16))

    even = lax.rem(lax.axis_index("col"), 2) == 0
    pair, cross = pair_ref[-BS:], cross_ref[...]
    block(0, far(0) + dot(near_ref[0, :BS, :], jnp.where(even, cross, pair)))

    @pl.loop(1, count - 1, unroll=2)
    def _(n):
        block(n, far(n))

    block(count - 1, far(count - 1) + dot(near_ref[2, -BS:, :], jnp.where(even, pair, cross)))


def finish_first_kernel(
    heights, shift_ref, scale_ref, rest_ref, slip_ref, numbers_ref, basis_out_ref, basis_in_ref, near_ref, *refs
):
    parts, pair_ref, cross_ref = refs[:heights], refs[heights], refs[heights + 1]
    slip_mid_ref, state_mid_ref, rounded_ref, coeff_ref, pair_out, cross_out = refs[heights + 2 :]

    def block(n, outer):
        at = rows_at(n, BS)
        speed = jnp.exp(shift_ref[at, :] - scale_ref[at, :] * outer)
        slip_mid = slip_ref[at, :] + STEP_SIZE * speed
        slip_mid_ref[at, :] = slip_mid
        state_mid_ref[at, :] = rest_ref[at, :] - (STEP_SIZE * numbers_ref[at, 4:5]) * speed
        rounded = slip_mid.astype(BF16)
        rounded_ref[at, :] = rounded
        coeff_ref[rows_at(n, R), :] = dot(basis_in_ref[:, at], rounded).astype(BF16)

    over_blocks(block, basis_out_ref, near_ref, parts, pair_ref, cross_ref)
    fill_edges(rounded_ref, pair_out, cross_out)


def prepare_second_kernel(
    slip_ref, state_ref, slip_mid_ref, state_mid_ref, scale_ref, numbers_ref, near_ref, rounded_ref,
    shift_ref, slip_rest_ref, rest_ref,
):
    @pl.loop(0, slip_ref.shape[0] // BS)
    def _(n):
        at = rows_at(n, BS)
        numbers = numbers_ref[at, :]
        inv_direct, inv_evolution, ratio = (numbers[:, k : k + 1] for k in range(2, 5))
        slip = slip_mid_ref[at, :]
        state = state_mid_ref[at, :]
        tau = near_tau(n, slip, numbers, near_ref, rounded_ref)
        shift_ref[at, :] = tau * scale_ref[at, :] - state * inv_direct
        slip_rest_ref[at, :] = 0.5 * (slip_ref[at, :] + slip)
        friction = jnp.exp((REF_FRICTION - state) * inv_evolution)
        rest_ref[at, :] = 0.5 * (state_ref[at, :] + state) + (0.5 * STEP_SIZE * ratio) * friction


def finish_second_kernel(
    heights, shift_ref, scale_ref, rest_ref, slip_rest_ref, numbers_ref, basis_out_ref, near_ref, *refs
):
    parts, pair_ref, cross_ref = refs[:heights], refs[heights], refs[heights + 1]
    slip_hbm, state_hbm, slip_ref, state_ref, sems = refs[heights + 2 :]

    def copies(n):
        at = rows_at(n, BS)
        return [
            pltpu.make_async_copy(slip_ref.at[at, :], slip_hbm.at[at, :], sems.at[0, n]),
            pltpu.make_async_copy(state_ref.at[at, :], state_hbm.at[at, :], sems.at[1, n]),
        ]

    def block(n, outer):
        at = rows_at(n, BS)
        speed = jnp.exp(shift_ref[at, :] - scale_ref[at, :] * outer)
        slip_ref[at, :] = slip_rest_ref[at, :] + (0.5 * STEP_SIZE) * speed
        state_ref[at, :] = rest_ref[at, :] - (0.5 * STEP_SIZE * numbers_ref[at, 4:5]) * speed
        for copy in copies(n):
            copy.start()

    over_blocks(block, basis_out_ref, near_ref, parts, pair_ref, cross_ref)

    @pl.loop(0, slip_ref.shape[0] // BS)
    def _(n):
        for copy in copies(n):
            copy.wait()


def masked_coupling(coupling, wide):
    rows, sources, width = coupling.shape
    blocks = rows // R
    keep = jnp.arange(R, dtype=jnp.int32).astype(F32)[None, None, :, None] < wide[:, :, None, :]
    matrix = jnp.transpose(coupling, (1, 0, 2)).reshape(sources, blocks, R, width)
    masked = jnp.where(keep, matrix, jnp.zeros((), BF16)).reshape(sources, rows, width)
    return pltpu.with_memory_space_constraint(masked, pltpu.VMEM)


def per_device(
    slip,
    state,
    tau_load,
    normal_stress,
    direct_effect,
    evolution_effect,
    slip_distance,
    self_stiffness,
    near_blocks,
    basis_in,
    basis_out,
    coupling,
    block_rank,
    adj_bricks,
    adj_count,
    adj_weight,
    pressure_now,
    pressure_rate,
):
    row_count = lax.axis_size("row")
    col_count = lax.axis_size("col")
    row_index = lax.axis_index("row")
    col_index = lax.axis_index("col")
    heights = col_count // 2
    height, core = col_index // 2, col_index % 2
    both = ("row", "col")
    devices = row_count * col_count

    def to_row(array, d):
        return lax.ppermute(array, "row", [(i, (i + d) % row_count) for i in range(row_count)])

    def to_height(array, d):
        pairs = [(2 * z + k, 2 * ((z + d) % heights) + k) for z in range(heights) for k in range(2)]
        return lax.ppermute(array, "col", pairs)

    def to_core(array):
        return lax.ppermute(array, "col", [(2 * z + k, 2 * z + 1 - k) for z in range(heights) for k in range(2)])

    def to_chip(array):
        ends = [(i, i + 1) for i in range(1, devices - 1, 2)]
        return lax.ppermute(array, both, ends + [(j, i) for i, j in ends])

    patches, ens = slip.shape
    slots = adj_bricks.shape[0]
    size = pressure_now.shape[0]
    share = coupling.shape[2]
    def far_parts(coeffs, pair, cross):
        sent = to_core(couple(1, masked, coeffs, heights, BF16, pair))
        kept = couple(0, masked, coeffs, heights, F32)
        pieces = chip_sum(kept, sent, heights)
        pieces, cross = lax.optimization_barrier((pieces, cross))
        parts = pieces[:1] + [to_height(pieces[d], d) for d in range(1, heights)]
        return parts + [sent, to_chip(cross)]

    def row_coeffs(coeff):
        return [coeff] + [to_row(coeff, d) for d in range(1, row_count)]

    full = jax.ShapeDtypeStruct((patches, ens), F32)
    half = jax.ShapeDtypeStruct((patches, ens), BF16)
    edge = jax.ShapeDtypeStruct((BS, ens), BF16)
    per_patch = [tau_load, normal_stress, direct_effect, evolution_effect, slip_distance, self_stiffness]

    ranks = jnp.transpose(block_rank, (1, 2, 0))
    wide, joined = call(
        functools.partial(ranks_kernel, col_count),
        [
            jax.ShapeDtypeStruct((ranks.shape[0], ranks.shape[2], share), F32),
            jax.ShapeDtypeStruct((size, 2 * ens), BF16),
        ],
        *in_hbm(ranks, pressure_now, pressure_rate),
        specs=[HBM] * 3,
        scratch_shapes=[pltpu.VMEM(ranks.shape, jnp.int32), pltpu.SemaphoreType.DMA((3,))],
    )
    fields = [joined] + [to_height(joined, d) for d in range(1, heights)]
    masked = masked_coupling(coupling, wide)
    masked, slip = lax.optimization_barrier((masked, slip))
    coeff, rounded, pair, cross, slip = project(slip, basis_in)
    coeffs = row_coeffs(coeff)
    brick_lists = [adj_count[None], adj_bricks, adj_weight]
    columns = [array[None] for array in per_patch] + brick_lists
    start = patches // 2
    part = jax.ShapeDtypeStruct((2 * heights * size, start), BF16)
    scratch = [
        pltpu.VMEM((6, 1, patches), F32),
        pltpu.VMEM((1, patches), jnp.int32),
        pltpu.VMEM(adj_bricks.shape, jnp.int32),
        pltpu.VMEM(adj_weight.shape, F32),
        pltpu.SemaphoreType.DMA((11,)),
    ]
    numbers, low = call(
        functools.partial(weights_kernel, heights, size, 0),
        [jax.ShapeDtypeStruct((start, 8), F32), part],
        *in_hbm(*columns),
        coeff,
        specs=[HBM] * 9 + [VMEM],
        scratch_shapes=scratch,
    )
    fields, coeffs, low = lax.optimization_barrier((fields, coeffs, low))
    own = call(
        side_by_side_kernel, jax.ShapeDtypeStruct((heights * size, 2 * ens), BF16), *fields
    )
    other = to_core(own)
    outer = far_parts(coeffs, pair, cross)
    numbers, high, near, state = call(
        functools.partial(weights_kernel, heights, size, start),
        [jax.ShapeDtypeStruct((patches, 8), F32), part, jax.ShapeDtypeStruct(near_blocks.shape, BF16), full],
        *in_hbm(*columns, near_blocks, state),
        numbers,
        outer[0],
        specs=[HBM] * 11 + [VMEM] * 2,
        scratch_shapes=scratch,
    )
    shift, scale, rest, scale_mid = call(
        prepare_first_kernel, [full] * 4, low, high, own, other, slip, state, numbers, near, rounded
    )
    slip_mid, state_mid, rounded, coeff, pair, cross = call(
        functools.partial(finish_first_kernel, heights),
        [full, full, half, jax.ShapeDtypeStruct((patches // BS * R, ens), BF16), edge, edge],
        shift, scale, rest, slip, numbers, basis_out, basis_in, near, *outer,
    )
    coeffs = row_coeffs(coeff)
    outer = far_parts(coeffs, pair, cross)
    shift, slip_rest, rest = call(
        prepare_second_kernel, [full] * 3,
        slip, state, slip_mid, state_mid, scale_mid, numbers, near, rounded,
    )
    slip_out, state_out = call(
        functools.partial(finish_second_kernel, heights),
        [full] * 2,
        shift, scale_mid, rest, slip_rest, numbers, basis_out, near, *outer,
        out_specs=[HBM] * 2,
        scratch_shapes=[
            pltpu.VMEM((patches, ens), F32),
            pltpu.VMEM((patches, ens), F32),
            pltpu.SemaphoreType.DMA((2, patches // BS)),
        ],
    )
    return (slip_out, state_out)


def solution(mesh):
    in_specs = (
        P(("row", "col"), None),
        P(("row", "col"), None),
        P(("row", "col")),
        P(("row", "col")),
        P(("row", "col")),
        P(("row", "col")),
        P(("row", "col")),
        P(("row", "col")),
        P(None, ("row", "col"), None),
        P(None, ("row", "col")),
        P(None, ("row", "col")),
        P("row", None, "col"),
        P("row", None, "col"),
        P(None, ("row", "col")),
        P(("row", "col")),
        P(None, ("row", "col")),
        P("col", None),
        P("col", None),
    )
    out_specs = (P(("row", "col"), None), P(("row", "col"), None))
    return jax.shard_map(
        per_device, mesh=mesh, in_specs=in_specs, out_specs=out_specs, check_vma=False
    )
```

profile of v0, /device:TPU:9, one launch (start us, length us, event | category | flops | bytes accessed | tf_op | source)
XLA Modules:
  0.0 77.5 jit_solution(8944170256723883662)
XLA Ops:
  0.6 1.0 %shard_map.185 = (f32[4,64,256]{2,1,0:T(8,128)S(1)}, bf16[128,512]{1,0:T(8,128)(2,1)S(1)}) custom-call(s32[4,8,64]{2,1,0:T(8,128)} %bitcast.28, bf16[128,256]{1,0:T(8,128)(2,1)} %now_hbm.1, bf16[128,256]{1,0:T(8,128)(2,1)} %rate_hbm.1), custom_call_target="tpu_custom_call" | custom-call | tf_op jit(solution)/shard_map/pallas_call | solution.py:32
  1.6 0.1 collective-permute-start.2
  1.7 2.5 %collective-permute-start.1 = (bf16[128,512]{1,0:T(8,128)(2,1)S(1)}, bf16[128,512]{1,0:T(8,128)(2,1)S(1)}, u32[]{:S(2)}, u32[]{:S(2)}) collective-permute-start(bf16[128,512]{1,0:T(8,128)(2,1)S(1)} %get-tuple-element.79.refs_0_), channel_id=1, source_target_pairs={{0,4},{1,5},{2,6},{3,7},{4,0},{5,1},{6,2},{7,3},{8,12},{9,13},{10,... | collective-permute-start | bytes 393224 | tf_op jit(solution)/shard_map/ppermute | solution.py:417
  4.1 2.2 %collective-permute-start = (bf16[128,512]{1,0:T(8,128)(2,1)S(1)}, bf16[128,512]{1,0:T(8,128)(2,1)S(1)}, u32[]{:S(2)}, u32[]{:S(2)}) collective-permute-start(bf16[128,512]{1,0:T(8,128)(2,1)S(1)} %get-tuple-element.79.refs_0_), channel_id=1, source_target_pairs={{0,2},{1,3},{2,4},{3,5},{4,6},{5,7},{6,0},{7,1},{8,10},{9,11},{10,... | collective-permute-start | bytes 393224 | tf_op jit(solution)/shard_map/ppermute | solution.py:417
  6.4 0.1 lt.21
  6.4 3.1 %fusion.matrix_ref = bf16[4,2048,256]{2,1,0:T(8,128)(2,1)S(1)} fusion(bf16[2048,4,256]{2,1,0:T(4,128)(2,1)} %param.29, f32[4,64,256]{2,1,0:T(8,128)S(1)} %get-tuple-element.57, f32[2048]{0:T(1024)S(1)} %lt.21), kind=kLoop, calls=%fused_computation.1 | loop fusion | flops 4194304 | bytes 8658944 | tf_op jit(solution)/shard_map/jit(_where)/select_n | solution.py:379
  9.6 2.4 %shard_map.186 = (bf16[256,256]{1,0:T(8,128)(2,1)S(1)}, bf16[2048,256]{1,0:T(8,128)(2,1)S(1)}, bf16[256,256]{1,0:T(8,128)(2,1)S(1)}, bf16[256,256]{1,0:T(8,128)(2,1)S(1)}, f32[2048,256]{1,0:T(8,128)S(1)}) custom-call(f32[2048,256]{1,0:T(8,128)} %slip_hbm, bf16[32,2048]{1,0:T(8,128)(2,1)} %basis_in_ref.1), custom_call_target="tpu_custom_call" | custom-call | tf_op jit(solution)/shard_map/pallas_call | solution.py:32
  11.9 2.2 %collective-permute-start.5 = (bf16[256,256]{1,0:T(8,128)(2,1)S(1)}, bf16[256,256]{1,0:T(8,128)(2,1)S(1)}, u32[]{:S(2)}, u32[]{:S(2)}) collective-permute-start(bf16[256,256]{1,0:T(8,128)(2,1)S(1)} %get-tuple-element.65.refs_9_.refs_0_), channel_id=1, source_target_pairs={{0,24},{8,0},{16,8},{24,16},{1,25},{9,1},{17,9},{25,17},{2,26},{10... | collective-permute-start | bytes 393224 | tf_op jit(solution)/shard_map/ppermute | solution.py:413
  14.2 0.2 collective-permute-start.4
  14.4 0.0 collective-permute-done.2.refs_3_
  14.4 0.3 collective-permute-start.3
  14.7 3.7 %shard_map.187 = (f32[1024,8]{1,0:T(8,128)S(1)}, bf16[1024,1024]{1,0:T(8,128)(2,1)S(1)}) custom-call(f32[1,2048]{1,0:T(1,128)} %bitcast.14, f32[1,2048]{1,0:T(1,128)} %bitcast.16, f32[1,2048]{1,0:T(1,128)} %bitcast.18, f32[1,2048]{1,0:T(1,128)} %bitcast.20, f32[1,2048]{1,0:T(1,128)} %bitcast.22, f32[1,2048]{1,0:T(1,128)} %bitcast.24, s32[1,2048]{1,0:T(1,128)} %bitcast.26, ...), custom_call_target="tpu_custom_call" | custom-call | tf_op jit(solution)/shard_map/pallas_call | solution.py:32
  18.4 1.7 %collective-permute-done.3.refs_1_ = bf16[256,256]{1,0:T(8,128)(2,1)S(1)} collective-permute-done((bf16[256,256]{1,0:T(8,128)(2,1)S(1)}, bf16[256,256]{1,0:T(8,128)(2,1)S(1)}, u32[]{:S(2)}, u32[]{:S(2)}) %collective-permute-start.3) | collective-permute-done | bytes 131104 | tf_op jit(solution)/shard_map/ppermute | solution.py:413
  20.2 1.2 %shard_map.189 = bf16[1280,256]{1,0:T(8,128)(2,1)S(1)} custom-call(bf16[4,2048,256]{2,1,0:T(8,128)(2,1)S(1)} %fusion.matrix_ref, bf16[256,256]{1,0:T(8,128)(2,1)S(1)} %get-tuple-element.65.refs_9_.refs_0_, bf16[256,256]{1,0:T(8,128)(2,1)S(1)} %collective-permute-done.3.refs_1_, bf16[256,256]{1,0:T(8,128)(2,1)S(1)} %collective-permute-done.4.refs_2_, ...), custom_call_target="tpu_custom_call" | custom-call | tf_op jit(solution)/shard_map/pallas_call | solution.py:32
  21.4 3.0 %collective-permute-start.6 = (bf16[1280,256]{1,0:T(8,128)(2,1)S(1)}, bf16[1280,256]{1,0:T(8,128)(2,1)S(1)}, u32[]{:S(2)}, u32[]{:S(2)}) collective-permute-start(bf16[1280,256]{1,0:T(8,128)(2,1)S(1)} %shard_map.189), channel_id=1, source_target_pairs={{0,1},{1,0},{2,3},{3,2},{4,5},{5,4},{6,7},{7,6},{8,9},{9,8},{10,11... | collective-permute-start | bytes 1966088 | tf_op jit(solution)/shard_map/ppermute | solution.py:420
  24.5 0.1 collective-permute-start.7
  24.5 1.2 %shard_map.188.kept_ref = f32[1024,256]{1,0:T(8,128)S(1)} custom-call(bf16[4,2048,256]{2,1,0:T(8,128)(2,1)S(1)} %fusion.matrix_ref, bf16[256,256]{1,0:T(8,128)(2,1)S(1)} %get-tuple-element.65.refs_9_.refs_0_, bf16[256,256]{1,0:T(8,128)(2,1)S(1)} %collective-permute-done.3.refs_1_, bf16[256,256]{1,0:T(8,128)(2,1)S(1)} %collective-permute-done.4.refs_2_, ...), custom_call_target="tpu_custom_call" | custom-call | tf_op jit(solution)/shard_map/pallas_call | solution.py:32
  25.8 0.4 collective-permute-done.6.sent_ref.refs_4_
  26.1 0.3 shard_map.190
  26.4 0.1 collective-permute-start.8
  26.5 1.3 %collective-permute-start.9 = (bf16[256,256]{1,0:T(8,128)(2,1)S(1)}, bf16[256,256]{1,0:T(8,128)(2,1)S(1)}, u32[]{:S(2)}, u32[]{:S(2)}) collective-permute-start(bf16[256,256]{1,0:T(8,128)(2,1)S(1)} %get-tuple-element.90), channel_id=1, source_target_pairs={{0,4},{1,5},{2,6},{3,7},{4,0},{5,1},{6,2},{7,3},{8,12},{9,13},{10,... | collective-permute-start | bytes 393224 | tf_op jit(solution)/shard_map/ppermute | solution.py:417
  27.8 0.9 %collective-permute-start.10 = (bf16[256,256]{1,0:T(8,128)(2,1)S(1)}, bf16[256,256]{1,0:T(8,128)(2,1)S(1)}, u32[]{:S(2)}, u32[]{:S(2)}) collective-permute-start(bf16[256,256]{1,0:T(8,128)(2,1)S(1)} %get-tuple-element.91), channel_id=1, source_target_pairs={{0,6},{1,7},{2,0},{3,1},{4,2},{5,3},{6,4},{7,5},{8,14},{9,15},{10,... | collective-permute-start | bytes 393224 | tf_op jit(solution)/shard_map/ppermute | solution.py:417
  28.7 3.6 %collective-permute-start.11 = (bf16[256,256]{1,0:T(8,128)(2,1)S(1)}, bf16[256,256]{1,0:T(8,128)(2,1)S(1)}, u32[]{:S(2)}, u32[]{:S(2)}) collective-permute-start(bf16[256,256]{1,0:T(8,128)(2,1)S(1)} %get-tuple-element.92), channel_id=1, source_target_pairs={{1,2},{3,4},{5,6},{7,8},{9,10},{11,12},{13,14},{15,16},{17,18},{19... | collective-permute-start | bytes 393224 | tf_op jit(solution)/shard_map/ppermute | solution.py:424
  32.3 3.7 %shard_map.191 = (f32[2048,8]{1,0:T(8,128)S(1)}, bf16[1024,1024]{1,0:T(8,128)(2,1)S(1)}, bf16[3,2048,256]{2,1,0:T(8,128)(2,1)S(1)}, f32[2048,256]{1,0:T(8,128)S(1)}) custom-call(f32[1,2048]{1,0:T(1,128)} %bitcast.15, f32[1,2048]{1,0:T(1,128)} %bitcast.17, f32[1,2048]{1,0:T(1,128)} %bitcast.19, f32[1,2048]{1,0:T(1,128)} %bitcast.21, f32[1,2048]{1,0:T(1,128)} %bitcast.23, ...), custom_call_target="tpu_custom_call" | custom-call | tf_op jit(solution)/shard_map/pallas_call | solution.py:32
  36.0 0.0 copy-start
  36.0 0.0 copy-start.1
  36.0 4.9 %shard_map.193 = (f32[2048,256]{1,0:T(8,128)S(1)}, f32[2048,256]{1,0:T(8,128)S(1)}, f32[2048,256]{1,0:T(8,128)S(1)}, f32[2048,256]{1,0:T(8,128)S(1)}) custom-call(bf16[1024,1024]{1,0:T(8,128)(2,1)S(1)} %get-tuple-element.77.low_ref, bf16[1024,1024]{1,0:T(8,128)(2,1)S(1)} %get-tuple-element.78.high_ref, bf16[512,512]{1,0:T(8,128)(2,1)S(1)} %shard_map.192.own_ref, ...), custom_call_target="tpu_custom_call" | custom-call | tf_op jit(solution)/shard_map/pallas_call | solution.py:32
  41.0 0.6 collective-permute-done.10.refs_3_
  41.6 1.2 %collective-permute-done.11.refs_5_ = bf16[256,256]{1,0:T(8,128)(2,1)S(1)} collective-permute-done((bf16[256,256]{1,0:T(8,128)(2,1)S(1)}, bf16[256,256]{1,0:T(8,128)(2,1)S(1)}, u32[]{:S(2)}, u32[]{:S(2)}) %collective-permute-start.11) | collective-permute-done | bytes 131104 | tf_op jit(solution)/shard_map/ppermute | solution.py:424
  42.9 2.6 %shard_map.194 = (f32[2048,256]{1,0:T(8,128)S(1)}, f32[2048,256]{1,0:T(8,128)S(1)}, bf16[2048,256]{1,0:T(8,128)(2,1)S(1)}, bf16[256,256]{1,0:T(8,128)(2,1)S(1)},...) custom-call(f32[2048,256]{1,0:T(8,128)S(1)} %get-tuple-element.86.shift_ref, ...), custom_call_target="tpu_custom_call" | custom-call | tf_op jit(solution)/shard_map/pallas_call | solution.py:32
  45.4 1.0 %collective-permute-start.13 = (bf16[256,256]{1,0:T(8,128)(2,1)S(1)}, bf16[256,256]{1,0:T(8,128)(2,1)S(1)}, u32[]{:S(2)}, u32[]{:S(2)}) collective-permute-start(bf16[256,256]{1,0:T(8,128)(2,1)S(1)} %get-tuple-element.100.refs_0_), channel_id=1, source_target_pairs={{0,16},{8,24},{16,0},{24,8},{1,17},{9,25},{17,1},{25,9},{2,18},{10... | collective-permute-start | bytes 393224 | tf_op jit(solution)/shard_map/ppermute | solution.py:413
  46.4 1.2 %collective-permute-start.12 = (bf16[256,256]{1,0:T(8,128)(2,1)S(1)}, bf16[256,256]{1,0:T(8,128)(2,1)S(1)}, u32[]{:S(2)}, u32[]{:S(2)}) collective-permute-start(bf16[256,256]{1,0:T(8,128)(2,1)S(1)} %get-tuple-element.100.refs_0_), channel_id=1, source_target_pairs={{0,8},{8,16},{16,24},{24,0},{1,9},{9,17},{17,25},{25,1},{2,10},{10... | collective-permute-start | bytes 393224 | tf_op jit(solution)/shard_map/ppermute | solution.py:413
  47.6 3.3 %collective-permute-done.14.refs_3_ = bf16[256,256]{1,0:T(8,128)(2,1)S(1)} collective-permute-done((bf16[256,256]{1,0:T(8,128)(2,1)S(1)}, bf16[256,256]{1,0:T(8,128)(2,1)S(1)}, u32[]{:S(2)}, u32[]{:S(2)}) %collective-permute-start.14) | collective-permute-done | bytes 131104 | tf_op jit(solution)/shard_map/ppermute | solution.py:413
  50.9 2.8 %collective-permute-done.12.refs_1_ = bf16[256,256]{1,0:T(8,128)(2,1)S(1)} collective-permute-done((bf16[256,256]{1,0:T(8,128)(2,1)S(1)}, bf16[256,256]{1,0:T(8,128)(2,1)S(1)}, u32[]{:S(2)}, u32[]{:S(2)}) %collective-permute-start.12) | collective-permute-done | bytes 131104 | tf_op jit(solution)/shard_map/ppermute | solution.py:413
  53.7 1.2 %shard_map.197 = bf16[1280,256]{1,0:T(8,128)(2,1)S(1)} custom-call(bf16[4,2048,256]{2,1,0:T(8,128)(2,1)S(1)} %fusion.matrix_ref, bf16[256,256]{1,0:T(8,128)(2,1)S(1)} %get-tuple-element.100.refs_0_, bf16[256,256]{1,0:T(8,128)(2,1)S(1)} %collective-permute-done.12.refs_1_, bf16[256,256]{1,0:T(8,128)(2,1)S(1)} %collective-permute-done.13.refs_2_, ...), custom_call_target="tpu_custom_call" | custom-call | tf_op jit(solution)/shard_map/pallas_call | solution.py:32
  55.0 0.5 collective-permute-start.15
  55.4 1.2 %shard_map.196.kept_ref = f32[1024,256]{1,0:T(8,128)S(1)} custom-call(bf16[4,2048,256]{2,1,0:T(8,128)(2,1)S(1)} %fusion.matrix_ref, bf16[256,256]{1,0:T(8,128)(2,1)S(1)} %get-tuple-element.100.refs_0_, bf16[256,256]{1,0:T(8,128)(2,1)S(1)} %collective-permute-done.12.refs_1_, bf16[256,256]{1,0:T(8,128)(2,1)S(1)} %collective-permute-done.13.refs_2_, ...), custom_call_target="tpu_custom_call" | custom-call | tf_op jit(solution)/shard_map/pallas_call | solution.py:32
  56.6 0.5 collective-permute-done.15.sent_ref.refs_4_
  57.2 0.3 shard_map.198
  57.4 0.1 collective-permute-start.16
  57.5 2.3 %collective-permute-start.17 = (bf16[256,256]{1,0:T(8,128)(2,1)S(1)}, bf16[256,256]{1,0:T(8,128)(2,1)S(1)}, u32[]{:S(2)}, u32[]{:S(2)}) collective-permute-start(bf16[256,256]{1,0:T(8,128)(2,1)S(1)} %get-tuple-element.109), channel_id=1, source_target_pairs={{0,4},{1,5},{2,6},{3,7},{4,0},{5,1},{6,2},{7,3},{8,12},{9,13},{10,... | collective-permute-start | bytes 393224 | tf_op jit(solution)/shard_map/ppermute | solution.py:417
  59.8 0.8 %collective-permute-start.18 = (bf16[256,256]{1,0:T(8,128)(2,1)S(1)}, bf16[256,256]{1,0:T(8,128)(2,1)S(1)}, u32[]{:S(2)}, u32[]{:S(2)}) collective-permute-start(bf16[256,256]{1,0:T(8,128)(2,1)S(1)} %get-tuple-element.110), channel_id=1, source_target_pairs={{0,6},{1,7},{2,0},{3,1},{4,2},{5,3},{6,4},{7,5},{8,14},{9,15},{10,... | collective-permute-start | bytes 393224 | tf_op jit(solution)/shard_map/ppermute | solution.py:417
  60.6 3.7 %collective-permute-start.19 = (bf16[256,256]{1,0:T(8,128)(2,1)S(1)}, bf16[256,256]{1,0:T(8,128)(2,1)S(1)}, u32[]{:S(2)}, u32[]{:S(2)}) collective-permute-start(bf16[256,256]{1,0:T(8,128)(2,1)S(1)} %get-tuple-element.111), channel_id=1, source_target_pairs={{1,2},{3,4},{5,6},{7,8},{9,10},{11,12},{13,14},{15,16},{17,18},{19... | collective-permute-start | bytes 393224 | tf_op jit(solution)/shard_map/ppermute | solution.py:424
  64.3 2.6 %shard_map.195 = (f32[2048,256]{1,0:T(8,128)S(1)}, f32[2048,256]{1,0:T(8,128)S(1)}, f32[2048,256]{1,0:T(8,128)S(1)}) custom-call(f32[2048,256]{1,0:T(8,128)S(1)} %get-tuple-element.59.slip_ref, f32[2048,256]{1,0:T(8,128)S(1)} %get-tuple-element.76.state_ref, f32[2048,256]{1,0:T(8,128)S(1)} %get-tuple-element.93.slip_mid_ref, ...), custom_call_target="tpu_custom_call" | custom-call | tf_op jit(solution)/shard_map/pallas_call | solution.py:32
  66.9 1.7 %collective-permute-done.17.refs_2_ = bf16[256,256]{1,0:T(8,128)(2,1)S(1)} collective-permute-done((bf16[256,256]{1,0:T(8,128)(2,1)S(1)}, bf16[256,256]{1,0:T(8,128)(2,1)S(1)}, u32[]{:S(2)}, u32[]{:S(2)}) %collective-permute-start.17) | collective-permute-done | bytes 131104 | tf_op jit(solution)/shard_map/ppermute | solution.py:417
  68.6 5.0 %collective-permute-done.18.refs_3_ = bf16[256,256]{1,0:T(8,128)(2,1)S(1)} collective-permute-done((bf16[256,256]{1,0:T(8,128)(2,1)S(1)}, bf16[256,256]{1,0:T(8,128)(2,1)S(1)}, u32[]{:S(2)}, u32[]{:S(2)}) %collective-permute-start.18) | collective-permute-done | bytes 131104 | tf_op jit(solution)/shard_map/ppermute | solution.py:417
  73.6 1.2 %collective-permute-done.19.refs_5_ = bf16[256,256]{1,0:T(8,128)(2,1)S(1)} collective-permute-done((bf16[256,256]{1,0:T(8,128)(2,1)S(1)}, bf16[256,256]{1,0:T(8,128)(2,1)S(1)}, u32[]{:S(2)}, u32[]{:S(2)}) %collective-permute-start.19) | collective-permute-done | bytes 131104 | tf_op jit(solution)/shard_map/ppermute | solution.py:424
  74.8 2.7 %shard_map.199 = (f32[2048,256]{1,0:T(8,128)}, f32[2048,256]{1,0:T(8,128)}) custom-call(f32[2048,256]{1,0:T(8,128)S(1)} %get-tuple-element.97.shift_ref, f32[2048,256]{1,0:T(8,128)S(1)} %get-tuple-element.95.scale_ref, f32[2048,256]{1,0:T(8,128)S(1)} %get-tuple-element.98.rest_ref, f32[2048,256]{1,0:T(8,128)S(1)} %get-tuple-element.99.slip_rest_ref, ...), custom_call_target="tpu_custom_call" | custom-call | tf_op jit(solution)/shard_map/pallas_call | solution.py:32
  (15 shorter events, 0.1 us)
Async XLA Ops:
  1.6 12.8 %collective-permute-start.2 = (bf16[128,512]{1,0:T(8,128)(2,1)S(1)}, bf16[128,512]{1,0:T(8,128)(2,1)S(1)}, u32[]{:S(2)}, u32[]{:S(2)}) collective-permute-start(bf16[128,512]{1,0:T(8,128)(2,1)S(1)} %get-tuple-element.79.refs_0_), channel_id=1, source_target_pairs={{0,6},{1,7},{2,0},{3,1},{4,2},{5,3},{6,4},{7,5},{8,14},{9,15},{10,... | collective-permute-start | bytes 393224 | tf_op jit(solution)/shard_map/ppermute | solution.py:417
  1.7 16.7 %collective-permute-start.1 = (bf16[128,512]{1,0:T(8,128)(2,1)S(1)}, bf16[128,512]{1,0:T(8,128)(2,1)S(1)}, u32[]{:S(2)}, u32[]{:S(2)}) collective-permute-start(bf16[128,512]{1,0:T(8,128)(2,1)S(1)} %get-tuple-element.79.refs_0_), channel_id=1, source_target_pairs={{0,4},{1,5},{2,6},{3,7},{4,0},{5,1},{6,2},{7,3},{8,12},{9,13},{10,... | collective-permute-start | bytes 393224 | tf_op jit(solution)/shard_map/ppermute | solution.py:417
  4.1 14.2 %collective-permute-start = (bf16[128,512]{1,0:T(8,128)(2,1)S(1)}, bf16[128,512]{1,0:T(8,128)(2,1)S(1)}, u32[]{:S(2)}, u32[]{:S(2)}) collective-permute-start(bf16[128,512]{1,0:T(8,128)(2,1)S(1)} %get-tuple-element.79.refs_0_), channel_id=1, source_target_pairs={{0,2},{1,3},{2,4},{3,5},{4,6},{5,7},{6,0},{7,1},{8,10},{9,11},{10,... | collective-permute-start | bytes 393224 | tf_op jit(solution)/shard_map/ppermute | solution.py:417
  11.9 6.5 %collective-permute-start.5 = (bf16[256,256]{1,0:T(8,128)(2,1)S(1)}, bf16[256,256]{1,0:T(8,128)(2,1)S(1)}, u32[]{:S(2)}, u32[]{:S(2)}) collective-permute-start(bf16[256,256]{1,0:T(8,128)(2,1)S(1)} %get-tuple-element.65.refs_9_.refs_0_), channel_id=1, source_target_pairs={{0,24},{8,0},{16,8},{24,16},{1,25},{9,1},{17,9},{25,17},{2,26},{10... | collective-permute-start | bytes 393224 | tf_op jit(solution)/shard_map/ppermute | solution.py:413
  14.2 4.3 %collective-permute-start.4 = (bf16[256,256]{1,0:T(8,128)(2,1)S(1)}, bf16[256,256]{1,0:T(8,128)(2,1)S(1)}, u32[]{:S(2)}, u32[]{:S(2)}) collective-permute-start(bf16[256,256]{1,0:T(8,128)(2,1)S(1)} %get-tuple-element.65.refs_9_.refs_0_), channel_id=1, source_target_pairs={{0,16},{8,24},{16,0},{24,8},{1,17},{9,25},{17,1},{25,9},{2,18},{10... | collective-permute-start | bytes 393224 | tf_op jit(solution)/shard_map/ppermute | solution.py:413
  14.4 5.8 %collective-permute-start.3 = (bf16[256,256]{1,0:T(8,128)(2,1)S(1)}, bf16[256,256]{1,0:T(8,128)(2,1)S(1)}, u32[]{:S(2)}, u32[]{:S(2)}) collective-permute-start(bf16[256,256]{1,0:T(8,128)(2,1)S(1)} %get-tuple-element.65.refs_9_.refs_0_), channel_id=1, source_target_pairs={{0,8},{8,16},{16,24},{24,0},{1,9},{9,17},{17,25},{25,1},{2,10},{10... | collective-permute-start | bytes 393224 | tf_op jit(solution)/shard_map/ppermute | solution.py:413
  21.4 4.7 %collective-permute-start.6 = (bf16[1280,256]{1,0:T(8,128)(2,1)S(1)}, bf16[1280,256]{1,0:T(8,128)(2,1)S(1)}, u32[]{:S(2)}, u32[]{:S(2)}) collective-permute-start(bf16[1280,256]{1,0:T(8,128)(2,1)S(1)} %shard_map.189), channel_id=1, source_target_pairs={{0,1},{1,0},{2,3},{3,2},{4,5},{5,4},{6,7},{7,6},{8,9},{9,8},{10,11... | collective-permute-start | bytes 1966088 | tf_op jit(solution)/shard_map/ppermute | solution.py:420
  24.5 11.5 %collective-permute-start.7 = (bf16[512,512]{1,0:T(8,128)(2,1)S(1)}, bf16[512,512]{1,0:T(8,128)(2,1)S(1)}, u32[]{:S(2)}, u32[]{:S(2)}) collective-permute-start(bf16[512,512]{1,0:T(8,128)(2,1)S(1)} %shard_map.192.own_ref), channel_id=1, source_target_pairs={{0,1},{1,0},{2,3},{3,2},{4,5},{5,4},{6,7},{7,6},{8,9},{9,8},{10,11... | collective-permute-start | bytes 1572872 | tf_op jit(solution)/shard_map/ppermute | solution.py:420
  26.4 14.6 %collective-permute-start.8 = (bf16[256,256]{1,0:T(8,128)(2,1)S(1)}, bf16[256,256]{1,0:T(8,128)(2,1)S(1)}, u32[]{:S(2)}, u32[]{:S(2)}) collective-permute-start(bf16[256,256]{1,0:T(8,128)(2,1)S(1)} %get-tuple-element.89), channel_id=1, source_target_pairs={{0,2},{1,3},{2,4},{3,5},{4,6},{5,7},{6,0},{7,1},{8,10},{9,11},{10,... | collective-permute-start | bytes 393224 | tf_op jit(solution)/shard_map/ppermute | solution.py:417
  26.5 14.5 %collective-permute-start.9 = (bf16[256,256]{1,0:T(8,128)(2,1)S(1)}, bf16[256,256]{1,0:T(8,128)(2,1)S(1)}, u32[]{:S(2)}, u32[]{:S(2)}) collective-permute-start(bf16[256,256]{1,0:T(8,128)(2,1)S(1)} %get-tuple-element.90), channel_id=1, source_target_pairs={{0,4},{1,5},{2,6},{3,7},{4,0},{5,1},{6,2},{7,3},{8,12},{9,13},{10,... | collective-permute-start | bytes 393224 | tf_op jit(solution)/shard_map/ppermute | solution.py:417
  27.8 13.8 %collective-permute-start.10 = (bf16[256,256]{1,0:T(8,128)(2,1)S(1)}, bf16[256,256]{1,0:T(8,128)(2,1)S(1)}, u32[]{:S(2)}, u32[]{:S(2)}) collective-permute-start(bf16[256,256]{1,0:T(8,128)(2,1)S(1)} %get-tuple-element.91), channel_id=1, source_target_pairs={{0,6},{1,7},{2,0},{3,1},{4,2},{5,3},{6,4},{7,5},{8,14},{9,15},{10,... | collective-permute-start | bytes 393224 | tf_op jit(solution)/shard_map/ppermute | solution.py:417
  28.7 14.1 %collective-permute-start.11 = (bf16[256,256]{1,0:T(8,128)(2,1)S(1)}, bf16[256,256]{1,0:T(8,128)(2,1)S(1)}, u32[]{:S(2)}, u32[]{:S(2)}) collective-permute-start(bf16[256,256]{1,0:T(8,128)(2,1)S(1)} %get-tuple-element.92), channel_id=1, source_target_pairs={{1,2},{3,4},{5,6},{7,8},{9,10},{11,12},{13,14},{15,16},{17,18},{19... | collective-permute-start | bytes 393224 | tf_op jit(solution)/shard_map/ppermute | solution.py:424
  36.0 6.8 %copy-start = (bf16[32,2048]{1,0:T(8,128)(2,1)S(1)}, bf16[32,2048]{1,0:T(8,128)(2,1)}, u32[]{:S(2)}) copy-start(bf16[32,2048]{1,0:T(8,128)(2,1)} %basis_out_ref.3) | copy-start | bytes 393220
  36.0 6.8 %copy-start.1 = (bf16[32,2048]{1,0:T(8,128)(2,1)S(1)}, bf16[32,2048]{1,0:T(8,128)(2,1)}, u32[]{:S(2)}) copy-start(bf16[32,2048]{1,0:T(8,128)(2,1)} %basis_in_ref.1) | copy-start | bytes 393220
  45.4 5.5 %collective-permute-start.14 = (bf16[256,256]{1,0:T(8,128)(2,1)S(1)}, bf16[256,256]{1,0:T(8,128)(2,1)S(1)}, u32[]{:S(2)}, u32[]{:S(2)}) collective-permute-start(bf16[256,256]{1,0:T(8,128)(2,1)S(1)} %get-tuple-element.100.refs_0_), channel_id=1, source_target_pairs={{0,24},{8,0},{16,8},{24,16},{1,25},{9,1},{17,9},{25,17},{2,26},{10... | collective-permute-start | bytes 393224 | tf_op jit(solution)/shard_map/ppermute | solution.py:413
  45.4 5.5 %collective-permute-start.13 = (bf16[256,256]{1,0:T(8,128)(2,1)S(1)}, bf16[256,256]{1,0:T(8,128)(2,1)S(1)}, u32[]{:S(2)}, u32[]{:S(2)}) collective-permute-start(bf16[256,256]{1,0:T(8,128)(2,1)S(1)} %get-tuple-element.100.refs_0_), channel_id=1, source_target_pairs={{0,16},{8,24},{16,0},{24,8},{1,17},{9,25},{17,1},{25,9},{2,18},{10... | collective-permute-start | bytes 393224 | tf_op jit(solution)/shard_map/ppermute | solution.py:413
  46.4 7.3 %collective-permute-start.12 = (bf16[256,256]{1,0:T(8,128)(2,1)S(1)}, bf16[256,256]{1,0:T(8,128)(2,1)S(1)}, u32[]{:S(2)}, u32[]{:S(2)}) collective-permute-start(bf16[256,256]{1,0:T(8,128)(2,1)S(1)} %get-tuple-element.100.refs_0_), channel_id=1, source_target_pairs={{0,8},{8,16},{16,24},{24,0},{1,9},{9,17},{17,25},{25,1},{2,10},{10... | collective-permute-start | bytes 393224 | tf_op jit(solution)/shard_map/ppermute | solution.py:413
  55.0 2.2 %collective-permute-start.15 = (bf16[1280,256]{1,0:T(8,128)(2,1)S(1)}, bf16[1280,256]{1,0:T(8,128)(2,1)S(1)}, u32[]{:S(2)}, u32[]{:S(2)}) collective-permute-start(bf16[1280,256]{1,0:T(8,128)(2,1)S(1)} %shard_map.197), channel_id=1, source_target_pairs={{0,1},{1,0},{2,3},{3,2},{4,5},{5,4},{6,7},{7,6},{8,9},{9,8},{10,11... | collective-permute-start | bytes 1966088 | tf_op jit(solution)/shard_map/ppermute | solution.py:420
  57.4 9.4 %collective-permute-start.16 = (bf16[256,256]{1,0:T(8,128)(2,1)S(1)}, bf16[256,256]{1,0:T(8,128)(2,1)S(1)}, u32[]{:S(2)}, u32[]{:S(2)}) collective-permute-start(bf16[256,256]{1,0:T(8,128)(2,1)S(1)} %get-tuple-element.108), channel_id=1, source_target_pairs={{0,2},{1,3},{2,4},{3,5},{4,6},{5,7},{6,0},{7,1},{8,10},{9,11},{10,... | collective-permute-start | bytes 393224 | tf_op jit(solution)/shard_map/ppermute | solution.py:417
  57.5 11.1 %collective-permute-start.17 = (bf16[256,256]{1,0:T(8,128)(2,1)S(1)}, bf16[256,256]{1,0:T(8,128)(2,1)S(1)}, u32[]{:S(2)}, u32[]{:S(2)}) collective-permute-start(bf16[256,256]{1,0:T(8,128)(2,1)S(1)} %get-tuple-element.109), channel_id=1, source_target_pairs={{0,4},{1,5},{2,6},{3,7},{4,0},{5,1},{6,2},{7,3},{8,12},{9,13},{10,... | collective-permute-start | bytes 393224 | tf_op jit(solution)/shard_map/ppermute | solution.py:417
  59.8 13.8 %collective-permute-start.18 = (bf16[256,256]{1,0:T(8,128)(2,1)S(1)}, bf16[256,256]{1,0:T(8,128)(2,1)S(1)}, u32[]{:S(2)}, u32[]{:S(2)}) collective-permute-start(bf16[256,256]{1,0:T(8,128)(2,1)S(1)} %get-tuple-element.110), channel_id=1, source_target_pairs={{0,6},{1,7},{2,0},{3,1},{4,2},{5,3},{6,4},{7,5},{8,14},{9,15},{10,... | collective-permute-start | bytes 393224 | tf_op jit(solution)/shard_map/ppermute | solution.py:417
  60.6 14.2 %collective-permute-start.19 = (bf16[256,256]{1,0:T(8,128)(2,1)S(1)}, bf16[256,256]{1,0:T(8,128)(2,1)S(1)}, u32[]{:S(2)}, u32[]{:S(2)}) collective-permute-start(bf16[256,256]{1,0:T(8,128)(2,1)S(1)} %get-tuple-element.111), channel_id=1, source_target_pairs={{1,2},{3,4},{5,6},{7,8},{9,10},{11,12},{13,14},{15,16},{17,18},{19... | collective-permute-start | bytes 393224 | tf_op jit(solution)/shard_map/ppermute | solution.py:424
where the time goes:
time: 77.8 us; the launch traced here: 77.5 us
  Pallas kernels  28.9 us (37%)
  starting transfers between devices  25.9 us (33%)
  waiting for transfers between devices  18.6 us (24%)
  other arithmetic  3.13 us (4%)
  between operations  0.87 us (1%)
    pallas_call x15, Pallas kernels, call(): pl.pallas_call(kernel, in_specs=specs or [VMEM] * len(operands), out_shap...  28.9 us
    ppermute x9, starting transfers between devices, to_height(): return lax.ppermute(array, 'col', pairs)  10.2 us
    ppermute x6, waiting for transfers between devices, to_row(): lax.ppermute(array, 'row', [(i, (i + d) % row_count) for i in range(row_c...  7.84 us
    ppermute x9, waiting for transfers between devices, to_height(): return lax.ppermute(array, 'col', pairs)  7.43 us
    ppermute x2, starting transfers between devices, to_chip(): return lax.ppermute(array, both, ends + [(j, i) for i, j in ends])  7.22 us
    ppermute x6, starting transfers between devices, to_row(): lax.ppermute(array, 'row', [(i, (i + d) % row_count) for i in range(row_c...  4.98 us
    ppermute x3, starting transfers between devices, to_core(): lax.ppermute(array, 'col', [(2 * z + k, 2 * z + 1 - k) for z in range(hei...  3.56 us
    select_n x1, other arithmetic, masked_coupling(): jnp.where(keep, matrix, jnp.zeros((), BF16)).reshape(sources, rows, width)  3.13 us
  transfers between devices with their start and end apart: 20, of which 10 were waited for; matrix products, arithmetic and copies ran while one was open for 4% of the time, Pallas kernels for 26%

commit v1 on v0

--- a/solution.py
+++ b/solution.py
@@ -56,14 +56,13 @@
     return copies
 
 
-def fill_edges(rounded_ref, pair_ref, cross_ref):
+def fill_edges(first, last, pair_ref, cross_ref):
     even = lax.rem(lax.axis_index("col"), 2) == 0
-    first, last = rounded_ref[:BS], rounded_ref[-BS:]
     pair_ref[...] = jnp.where(even, last, first)
     cross_ref[...] = jnp.where(even, first, last)
 
 
-def project_kernel(slip_hbm, basis_hbm, coeff_ref, rounded_ref, pair_ref, cross_ref, slip_ref, basis_ref, sems):
+def project_kernel(slip_hbm, basis_hbm, coeff_ref, rounded_ref, slip_ref, basis_ref, sems):
     count = slip_ref.shape[0] // BS
     blocks = [pl.ds(n * BS, BS) for n in range(count)]
     copies = start_copies(
@@ -75,20 +74,16 @@
         rounded = slip_ref[at, :].astype(BF16)
         rounded_ref[at, :] = rounded
         coeff_ref[n * R : (n + 1) * R, :] = dot(basis_ref[:, at], rounded).astype(BF16)
-    fill_edges(rounded_ref, pair_ref, cross_ref)
 
 
 def project(slip, basis_in):
     patches, ens = slip.shape
     count = patches // BS
-    edge = jax.ShapeDtypeStruct((BS, ens), BF16)
     return call(
         project_kernel,
         [
             jax.ShapeDtypeStruct((count * R, ens), BF16),
             jax.ShapeDtypeStruct((patches, ens), BF16),
-            edge,
-            edge,
             jax.ShapeDtypeStruct((patches, ens), F32),
         ],
         *in_hbm(slip, basis_in),
@@ -98,7 +93,7 @@
 
 
 def ranks_kernel(
-    col_count, rank_hbm, now_hbm, rate_hbm, wide_ref, joined_ref, rank_ref, sems
+    col_count, rank_hbm, now_hbm, rate_hbm, slip_hbm, wide_ref, joined_ref, pair_ref, cross_ref, rank_ref, ends, sems
 ):
     sources, share, blocks = rank_ref.shape
     ens = now_hbm.shape[1]
@@ -107,6 +102,8 @@
             (rank_hbm, rank_ref),
             (now_hbm, joined_ref.at[:, pl.ds(0, ens)]),
             (rate_hbm, joined_ref.at[:, pl.ds(ens, ens)]),
+            (slip_hbm.at[pl.ds(0, BS), :], ends.at[0]),
+            (slip_hbm.at[pl.ds(slip_hbm.shape[0] - BS, BS), :], ends.at[1]),
         ],
         sems,
     )
@@ -121,8 +118,9 @@
         rank = jnp.where(jnp.abs(receiver - own) > 1, rank_ref[source], 0).astype(F32)
         wide = dot_t(rank.astype(BF16), spread)
         wide_ref[source] = jnp.where(level < wide, wide, 0.0)
-    copies[1].wait()
-    copies[2].wait()
+    for copy in copies[1:]:
+        copy.wait()
+    fill_edges(ends[0].astype(BF16), ends[1].astype(BF16), pair_ref, cross_ref)
 
 
 def side_by_side_kernel(*refs):
@@ -297,7 +295,7 @@
     pair, cross = pair_ref[-BS:], cross_ref[...]
     block(0, far(0) + dot(near_ref[0, :BS, :], jnp.where(even, cross, pair)))
 
-    @pl.loop(1, count - 1, unroll=2)
+    @pl.loop(1, count - 1, unroll=3)
     def _(n):
         block(n, far(n))
 
@@ -305,27 +303,25 @@
 
 
 def finish_first_kernel(
-    heights, shift_ref, scale_ref, rest_ref, slip_ref, numbers_ref, basis_out_ref, basis_in_ref, near_ref, *refs
+    heights, shift_ref, scale_ref, slip_ref, basis_out_ref, basis_in_ref, near_ref, *refs
 ):
     parts, pair_ref, cross_ref = refs[:heights], refs[heights], refs[heights + 1]
-    slip_mid_ref, state_mid_ref, rounded_ref, coeff_ref, pair_out, cross_out = refs[heights + 2 :]
+    speed_ref, rounded_ref, coeff_ref, pair_out, cross_out = refs[heights + 2 :]
 
     def block(n, outer):
         at = rows_at(n, BS)
         speed = jnp.exp(shift_ref[at, :] - scale_ref[at, :] * outer)
-        slip_mid = slip_ref[at, :] + STEP_SIZE * speed
-        slip_mid_ref[at, :] = slip_mid
-        state_mid_ref[at, :] = rest_ref[at, :] - (STEP_SIZE * numbers_ref[at, 4:5]) * speed
-        rounded = slip_mid.astype(BF16)
+        speed_ref[at, :] = speed
+        rounded = (slip_ref[at, :] + STEP_SIZE * speed).astype(BF16)
         rounded_ref[at, :] = rounded
         coeff_ref[rows_at(n, R), :] = dot(basis_in_ref[:, at], rounded).astype(BF16)
 
     over_blocks(block, basis_out_ref, near_ref, parts, pair_ref, cross_ref)
-    fill_edges(rounded_ref, pair_out, cross_out)
+    fill_edges(rounded_ref[:BS], rounded_ref[-BS:], pair_out, cross_out)
 
 
 def prepare_second_kernel(
-    slip_ref, state_ref, slip_mid_ref, state_mid_ref, scale_ref, numbers_ref, near_ref, rounded_ref,
+    slip_ref, state_ref, speed_ref, part_ref, scale_ref, numbers_ref, near_ref, rounded_ref,
     shift_ref, slip_rest_ref, rest_ref,
 ):
     @pl.loop(0, slip_ref.shape[0] // BS)
@@ -333,8 +329,9 @@
         at = rows_at(n, BS)
         numbers = numbers_ref[at, :]
         inv_direct, inv_evolution, ratio = (numbers[:, k : k + 1] for k in range(2, 5))
-        slip = slip_mid_ref[at, :]
-        state = state_mid_ref[at, :]
+        speed = speed_ref[at, :]
+        slip = slip_ref[at, :] + STEP_SIZE * speed
+        state = part_ref[at, :] - (STEP_SIZE * ratio) * speed
         tau = near_tau(n, slip, numbers, near_ref, rounded_ref)
         shift_ref[at, :] = tau * scale_ref[at, :] - state * inv_direct
         slip_rest_ref[at, :] = 0.5 * (slip_ref[at, :] + slip)
@@ -431,9 +428,8 @@
         sent = to_core(couple(1, masked, coeffs, heights, BF16, pair))
         kept = couple(0, masked, coeffs, heights, F32)
         pieces = chip_sum(kept, sent, heights)
-        pieces, cross = lax.optimization_barrier((pieces, cross))
         parts = pieces[:1] + [to_height(pieces[d], d) for d in range(1, heights)]
-        return parts + [sent, to_chip(cross)]
+        return parts + [sent, cross]
 
     def row_coeffs(coeff):
         return [coeff] + [to_row(coeff, d) for d in range(1, row_count)]
@@ -444,20 +440,26 @@
     per_patch = [tau_load, normal_stress, direct_effect, evolution_effect, slip_distance, self_stiffness]
 
     ranks = jnp.transpose(block_rank, (1, 2, 0))
-    wide, joined = call(
+    wide, joined, pair, cross = call(
         functools.partial(ranks_kernel, col_count),
         [
             jax.ShapeDtypeStruct((ranks.shape[0], ranks.shape[2], share), F32),
             jax.ShapeDtypeStruct((size, 2 * ens), BF16),
+            edge,
+            edge,
         ],
-        *in_hbm(ranks, pressure_now, pressure_rate),
-        specs=[HBM] * 3,
-        scratch_shapes=[pltpu.VMEM(ranks.shape, jnp.int32), pltpu.SemaphoreType.DMA((3,))],
+        *in_hbm(ranks, pressure_now, pressure_rate, slip),
+        specs=[HBM] * 4,
+        scratch_shapes=[
+            pltpu.VMEM(ranks.shape, jnp.int32),
+            pltpu.VMEM((2, BS, ens), F32),
+            pltpu.SemaphoreType.DMA((5,)),
+        ],
     )
     fields = [joined] + [to_height(joined, d) for d in range(1, heights)]
     masked = masked_coupling(coupling, wide)
     masked, slip = lax.optimization_barrier((masked, slip))
-    coeff, rounded, pair, cross, slip = project(slip, basis_in)
+    coeff, rounded, slip = project(slip, basis_in)
     coeffs = row_coeffs(coeff)
     brick_lists = [adj_count[None], adj_bricks, adj_weight]
     columns = [array[None] for array in per_patch] + brick_lists
@@ -478,7 +480,7 @@
         specs=[HBM] * 9 + [VMEM],
         scratch_shapes=scratch,
     )
-    fields, coeffs, low = lax.optimization_barrier((fields, coeffs, low))
+    fields, cross, coeffs, low = lax.optimization_barrier((fields, to_chip(cross), coeffs, low))
     own = call(
         side_by_side_kernel, jax.ShapeDtypeStruct((heights * size, 2 * ens), BF16), *fields
     )
@@ -496,16 +498,16 @@
     shift, scale, rest, scale_mid = call(
         prepare_first_kernel, [full] * 4, low, high, own, other, slip, state, numbers, near, rounded
     )
-    slip_mid, state_mid, rounded, coeff, pair, cross = call(
+    speed, rounded, coeff, pair, cross = call(
         functools.partial(finish_first_kernel, heights),
-        [full, full, half, jax.ShapeDtypeStruct((patches // BS * R, ens), BF16), edge, edge],
-        shift, scale, rest, slip, numbers, basis_out, basis_in, near, *outer,
-    )
-    coeffs = row_coeffs(coeff)
+        [full, half, jax.ShapeDtypeStruct((patches // BS * R, ens), BF16), edge, edge],
+        shift, scale, slip, basis_out, basis_in, near, *outer,
+    )
+    coeffs, cross = lax.optimization_barrier((row_coeffs(coeff), to_chip(cross)))
     outer = far_parts(coeffs, pair, cross)
     shift, slip_rest, rest = call(
         prepare_second_kernel, [full] * 3,
-        slip, state, slip_mid, state_mid, scale_mid, numbers, near, rounded,
+        slip, state, speed, rest, scale_mid, numbers, near, rounded,
     )
     slip_out, state_out = call(
         functools.partial(finish_second_kernel, heights),

time: 77.8 us -> 79.9 us (1.027)
  the two profiles are of different devices: /device:TPU:9 before, /device:TPU:0 now
where the time goes in v1:
time: 79.9 us; the launch traced here: 79.1 us
  starting transfers between devices  29.4 us (37%)
  Pallas kernels  29.1 us (36%)
  waiting for transfers between devices  16.4 us (21%)
  other arithmetic  3.13 us (4%)
  between operations  0.88 us (1%)
    pallas_call x15, Pallas kernels, call(): pl.pallas_call(kernel, in_specs=specs or [VMEM] * len(operands), out_shap...  29.1 us
    ppermute x9, starting transfers between devices, to_height(): return lax.ppermute(array, 'col', pairs)  16 us
    ppermute x6, starting transfers between devices, to_row(): lax.ppermute(array, 'row', [(i, (i + d) % row_count) for i in range(row_c...  11.4 us
    ppermute x6, waiting for transfers between devices, to_row(): lax.ppermute(array, 'row', [(i, (i + d) % row_count) for i in range(row_c...  9.17 us
    ppermute x9, waiting for transfers between devices, to_height(): return lax.ppermute(array, 'col', pairs)  6.12 us
    select_n x1, other arithmetic, masked_coupling(): jnp.where(keep, matrix, jnp.zeros((), BF16)).reshape(sources, rows, width)  3.13 us
  transfers between devices with their start and end apart: 20, of which 7 were waited for; matrix products, arithmetic and copies ran while one was open for 4% of the time, Pallas kernels for 26%

profile of v1, /device:TPU:0, one launch (start us, length us, event | category | flops | bytes accessed | tf_op | source)
XLA Modules:
  0.0 79.1 jit_solution(9761294265978957777)
XLA Ops:
  0.6 1.2 %shard_map.185 = (f32[4,64,256]{2,1,0:T(8,128)S(1)}, bf16[128,512]{1,0:T(8,128)(2,1)S(1)}, bf16[256,256]{1,0:T(8,128)(2,1)S(1)}, bf16[256,256]{1,0:T(8,128)(2,1)S(1)}) custom-call(s32[4,8,64]{2,1,0:T(8,128)} %bitcast.28, bf16[128,256]{1,0:T(8,128)(2,1)} %now_hbm.1, bf16[128,256]{1,0:T(8,128)(2,1)} %rate_hbm.1, f32[2048,256]{1,0:T(8,128)} %slip_hbm.2), custom_call_target="tpu_custom_call" | custom-call | tf_op jit(solution)/shard_map/pallas_call | solution.py:32
  1.8 0.7 collective-permute-start.3
  2.5 6.4 %collective-permute-start.2 = (bf16[128,512]{1,0:T(8,128)(2,1)S(1)}, bf16[128,512]{1,0:T(8,128)(2,1)S(1)}, u32[]{:S(2)}, u32[]{:S(2)}) collective-permute-start(bf16[128,512]{1,0:T(8,128)(2,1)S(1)} %get-tuple-element.70.refs_0_), channel_id=1, source_target_pairs={{0,6},{1,7},{2,0},{3,1},{4,2},{5,3},{6,4},{7,5},{8,14},{9,15},{10,... | collective-permute-start | bytes 393224 | tf_op jit(solution)/shard_map/ppermute | solution.py:414
  8.9 1.0 %collective-permute-start = (bf16[128,512]{1,0:T(8,128)(2,1)S(1)}, bf16[128,512]{1,0:T(8,128)(2,1)S(1)}, u32[]{:S(2)}, u32[]{:S(2)}) collective-permute-start(bf16[128,512]{1,0:T(8,128)(2,1)S(1)} %get-tuple-element.70.refs_0_), channel_id=1, source_target_pairs={{0,2},{1,3},{2,4},{3,5},{4,6},{5,7},{6,0},{7,1},{8,10},{9,11},{10,... | collective-permute-start | bytes 393224 | tf_op jit(solution)/shard_map/ppermute | solution.py:414
  9.9 0.1 lt.21
  10.0 3.1 %fusion.matrix_ref = bf16[4,2048,256]{2,1,0:T(8,128)(2,1)S(1)} fusion(bf16[2048,4,256]{2,1,0:T(4,128)(2,1)} %param.29, f32[4,64,256]{2,1,0:T(8,128)S(1)} %get-tuple-element.52, f32[2048]{0:T(1024)S(1)} %lt.21), kind=kLoop, calls=%fused_computation.1 | loop fusion | flops 4194304 | bytes 8658944 | tf_op jit(solution)/shard_map/jit(_where)/select_n | solution.py:376
  13.1 2.4 %shard_map.186 = (bf16[256,256]{1,0:T(8,128)(2,1)S(1)}, bf16[2048,256]{1,0:T(8,128)(2,1)S(1)}, f32[2048,256]{1,0:T(8,128)S(1)}) custom-call(f32[2048,256]{1,0:T(8,128)} %slip_hbm.2, bf16[32,2048]{1,0:T(8,128)(2,1)} %basis_in_ref.1), custom_call_target="tpu_custom_call" | custom-call | tf_op jit(solution)/shard_map/pallas_call | solution.py:32
  15.5 2.9 %collective-permute-start.6 = (bf16[256,256]{1,0:T(8,128)(2,1)S(1)}, bf16[256,256]{1,0:T(8,128)(2,1)S(1)}, u32[]{:S(2)}, u32[]{:S(2)}) collective-permute-start(bf16[256,256]{1,0:T(8,128)(2,1)S(1)} %get-tuple-element.61.refs_9_.refs_0_), channel_id=1, source_target_pairs={{0,24},{8,0},{16,8},{24,16},{1,25},{9,1},{17,9},{25,17},{2,26},{10... | collective-permute-start | bytes 393224 | tf_op jit(solution)/shard_map/ppermute | solution.py:410
  18.4 0.0 collective-permute-done.3.refs_5_
  18.4 0.5 collective-permute-start.5
  18.9 1.5 %collective-permute-start.4 = (bf16[256,256]{1,0:T(8,128)(2,1)S(1)}, bf16[256,256]{1,0:T(8,128)(2,1)S(1)}, u32[]{:S(2)}, u32[]{:S(2)}) collective-permute-start(bf16[256,256]{1,0:T(8,128)(2,1)S(1)} %get-tuple-element.61.refs_9_.refs_0_), channel_id=1, source_target_pairs={{0,8},{8,16},{16,24},{24,0},{1,9},{9,17},{17,25},{25,1},{2,10},{10... | collective-permute-start | bytes 393224 | tf_op jit(solution)/shard_map/ppermute | solution.py:410
  20.4 3.7 %shard_map.187 = (f32[1024,8]{1,0:T(8,128)S(1)}, bf16[1024,1024]{1,0:T(8,128)(2,1)S(1)}) custom-call(f32[1,2048]{1,0:T(1,128)} %bitcast.14, f32[1,2048]{1,0:T(1,128)} %bitcast.16, f32[1,2048]{1,0:T(1,128)} %bitcast.18, f32[1,2048]{1,0:T(1,128)} %bitcast.20, f32[1,2048]{1,0:T(1,128)} %bitcast.22, f32[1,2048]{1,0:T(1,128)} %bitcast.24, s32[1,2048]{1,0:T(1,128)} %bitcast.26, ...), custom_call_target="tpu_custom_call" | custom-call | tf_op jit(solution)/shard_map/pallas_call | solution.py:32
  24.1 0.0 collective-permute-done.1.refs_2_
  24.1 0.0 collective-permute-done.6.refs_3_
  24.1 2.7 %collective-permute-done.5.refs_2_ = bf16[256,256]{1,0:T(8,128)(2,1)S(1)} collective-permute-done((bf16[256,256]{1,0:T(8,128)(2,1)S(1)}, bf16[256,256]{1,0:T(8,128)(2,1)S(1)}, u32[]{:S(2)}, u32[]{:S(2)}) %collective-permute-start.5) | collective-permute-done | bytes 131104 | tf_op jit(solution)/shard_map/ppermute | solution.py:410
  26.8 0.0 collective-permute-done.4.refs_1_
  26.8 1.2 %shard_map.189 = bf16[1280,256]{1,0:T(8,128)(2,1)S(1)} custom-call(bf16[4,2048,256]{2,1,0:T(8,128)(2,1)S(1)} %fusion.matrix_ref, bf16[256,256]{1,0:T(8,128)(2,1)S(1)} %get-tuple-element.61.refs_9_.refs_0_, bf16[256,256]{1,0:T(8,128)(2,1)S(1)} %collective-permute-done.4.refs_1_, bf16[256,256]{1,0:T(8,128)(2,1)S(1)} %collective-permute-done.5.refs_2_, ...), custom_call_target="tpu_custom_call" | custom-call | tf_op jit(solution)/shard_map/pallas_call | solution.py:32
  28.0 0.1 collective-permute-start.7
  28.1 0.6 collective-permute-start.8
  28.7 1.2 %shard_map.188.kept_ref = f32[1024,256]{1,0:T(8,128)S(1)} custom-call(bf16[4,2048,256]{2,1,0:T(8,128)(2,1)S(1)} %fusion.matrix_ref, bf16[256,256]{1,0:T(8,128)(2,1)S(1)} %get-tuple-element.61.refs_9_.refs_0_, bf16[256,256]{1,0:T(8,128)(2,1)S(1)} %collective-permute-done.4.refs_1_, bf16[256,256]{1,0:T(8,128)(2,1)S(1)} %collective-permute-done.5.refs_2_, ...), custom_call_target="tpu_custom_call" | custom-call | tf_op jit(solution)/shard_map/pallas_call | solution.py:32
  29.9 0.3 collective-permute-done.7.sent_ref.refs_4_
  30.2 0.3 shard_map.190
  30.4 1.5 %collective-permute-start.9 = (bf16[256,256]{1,0:T(8,128)(2,1)S(1)}, bf16[256,256]{1,0:T(8,128)(2,1)S(1)}, u32[]{:S(2)}, u32[]{:S(2)}) collective-permute-start(bf16[256,256]{1,0:T(8,128)(2,1)S(1)} %get-tuple-element.79), channel_id=1, source_target_pairs={{0,2},{1,3},{2,4},{3,5},{4,6},{5,7},{6,0},{7,1},{8,10},{9,11},{10,... | collective-permute-start | bytes 393224 | tf_op jit(solution)/shard_map/ppermute | solution.py:414
  32.0 1.3 %collective-permute-start.10 = (bf16[256,256]{1,0:T(8,128)(2,1)S(1)}, bf16[256,256]{1,0:T(8,128)(2,1)S(1)}, u32[]{:S(2)}, u32[]{:S(2)}) collective-permute-start(bf16[256,256]{1,0:T(8,128)(2,1)S(1)} %get-tuple-element.80), channel_id=1, source_target_pairs={{0,4},{1,5},{2,6},{3,7},{4,0},{5,1},{6,2},{7,3},{8,12},{9,13},{10,... | collective-permute-start | bytes 393224 | tf_op jit(solution)/shard_map/ppermute | solution.py:414
  33.3 1.9 %collective-permute-start.11 = (bf16[256,256]{1,0:T(8,128)(2,1)S(1)}, bf16[256,256]{1,0:T(8,128)(2,1)S(1)}, u32[]{:S(2)}, u32[]{:S(2)}) collective-permute-start(bf16[256,256]{1,0:T(8,128)(2,1)S(1)} %get-tuple-element.81), channel_id=1, source_target_pairs={{0,6},{1,7},{2,0},{3,1},{4,2},{5,3},{6,4},{7,5},{8,14},{9,15},{10,... | collective-permute-start | bytes 393224 | tf_op jit(solution)/shard_map/ppermute | solution.py:414
  35.2 3.7 %shard_map.191 = (f32[2048,8]{1,0:T(8,128)S(1)}, bf16[1024,1024]{1,0:T(8,128)(2,1)S(1)}, bf16[3,2048,256]{2,1,0:T(8,128)(2,1)S(1)}, f32[2048,256]{1,0:T(8,128)S(1)}) custom-call(f32[1,2048]{1,0:T(1,128)} %bitcast.15, f32[1,2048]{1,0:T(1,128)} %bitcast.17, f32[1,2048]{1,0:T(1,128)} %bitcast.19, f32[1,2048]{1,0:T(1,128)} %bitcast.21, f32[1,2048]{1,0:T(1,128)} %bitcast.23, ...), custom_call_target="tpu_custom_call" | custom-call | tf_op jit(solution)/shard_map/pallas_call | solution.py:32
  38.9 0.0 copy-start
  38.9 0.0 copy-start.1
  38.9 4.9 %shard_map.193 = (f32[2048,256]{1,0:T(8,128)S(1)}, f32[2048,256]{1,0:T(8,128)S(1)}, f32[2048,256]{1,0:T(8,128)S(1)}, f32[2048,256]{1,0:T(8,128)S(1)}) custom-call(bf16[1024,1024]{1,0:T(8,128)(2,1)S(1)} %get-tuple-element.68.low_ref, bf16[1024,1024]{1,0:T(8,128)(2,1)S(1)} %get-tuple-element.69.high_ref, bf16[512,512]{1,0:T(8,128)(2,1)S(1)} %shard_map.192.own_ref, ...), custom_call_target="tpu_custom_call" | custom-call | tf_op jit(solution)/shard_map/pallas_call | solution.py:32
  43.9 2.3 %shard_map.194 = (f32[2048,256]{1,0:T(8,128)S(1)}, bf16[2048,256]{1,0:T(8,128)(2,1)S(1)}, bf16[256,256]{1,0:T(8,128)(2,1)S(1)}, bf16[256,256]{1,0:T(8,128)(2,1)S(1)}, bf16[256,256]{1,0:T(8,128)(2,1)S(1)}) custom-call(f32[2048,256]{1,0:T(8,128)S(1)} %get-tuple-element.77.shift_ref, f32[2048,256]{1,0:T(8,128)S(1)} %get-tuple-element.78.scale_ref, ...), custom_call_target="tpu_custom_call" | custom-call | tf_op jit(solution)/shard_map/pallas_call | solution.py:32
  46.2 0.7 collective-permute-start.15
  46.8 5.0 %collective-permute-start.14 = (bf16[256,256]{1,0:T(8,128)(2,1)S(1)}, bf16[256,256]{1,0:T(8,128)(2,1)S(1)}, u32[]{:S(2)}, u32[]{:S(2)}) collective-permute-start(bf16[256,256]{1,0:T(8,128)(2,1)S(1)} %get-tuple-element.92.refs_0_), channel_id=1, source_target_pairs={{0,24},{8,0},{16,8},{24,16},{1,25},{9,1},{17,9},{25,17},{2,26},{10... | collective-permute-start | bytes 393224 | tf_op jit(solution)/shard_map/ppermute | solution.py:410
  51.9 1.4 %collective-permute-start.13 = (bf16[256,256]{1,0:T(8,128)(2,1)S(1)}, bf16[256,256]{1,0:T(8,128)(2,1)S(1)}, u32[]{:S(2)}, u32[]{:S(2)}) collective-permute-start(bf16[256,256]{1,0:T(8,128)(2,1)S(1)} %get-tuple-element.92.refs_0_), channel_id=1, source_target_pairs={{0,16},{8,24},{16,0},{24,8},{1,17},{9,25},{17,1},{25,9},{2,18},{10... | collective-permute-start | bytes 393224 | tf_op jit(solution)/shard_map/ppermute | solution.py:410
  53.2 0.1 collective-permute-start.12
  53.4 3.7 %collective-permute-done.14.refs_3_ = bf16[256,256]{1,0:T(8,128)(2,1)S(1)} collective-permute-done((bf16[256,256]{1,0:T(8,128)(2,1)S(1)}, bf16[256,256]{1,0:T(8,128)(2,1)S(1)}, u32[]{:S(2)}, u32[]{:S(2)}) %collective-permute-start.14) | collective-permute-done | bytes 131104 | tf_op jit(solution)/shard_map/ppermute | solution.py:410
  57.1 2.8 %collective-permute-done.13.refs_2_ = bf16[256,256]{1,0:T(8,128)(2,1)S(1)} collective-permute-done((bf16[256,256]{1,0:T(8,128)(2,1)S(1)}, bf16[256,256]{1,0:T(8,128)(2,1)S(1)}, u32[]{:S(2)}, u32[]{:S(2)}) %collective-permute-start.13) | collective-permute-done | bytes 131104 | tf_op jit(solution)/shard_map/ppermute | solution.py:410
  59.9 1.2 %shard_map.197 = bf16[1280,256]{1,0:T(8,128)(2,1)S(1)} custom-call(bf16[4,2048,256]{2,1,0:T(8,128)(2,1)S(1)} %fusion.matrix_ref, bf16[256,256]{1,0:T(8,128)(2,1)S(1)} %get-tuple-element.92.refs_0_, bf16[256,256]{1,0:T(8,128)(2,1)S(1)} %collective-permute-done.12.refs_1_, bf16[256,256]{1,0:T(8,128)(2,1)S(1)} %collective-permute-done.13.refs_2_, ...), custom_call_target="tpu_custom_call" | custom-call | tf_op jit(solution)/shard_map/pallas_call | solution.py:32
  61.1 0.1 collective-permute-start.16
  61.2 1.2 %shard_map.196.kept_ref = f32[1024,256]{1,0:T(8,128)S(1)} custom-call(bf16[4,2048,256]{2,1,0:T(8,128)(2,1)S(1)} %fusion.matrix_ref, bf16[256,256]{1,0:T(8,128)(2,1)S(1)} %get-tuple-element.92.refs_0_, bf16[256,256]{1,0:T(8,128)(2,1)S(1)} %collective-permute-done.12.refs_1_, bf16[256,256]{1,0:T(8,128)(2,1)S(1)} %collective-permute-done.13.refs_2_, ...), custom_call_target="tpu_custom_call" | custom-call | tf_op jit(solution)/shard_map/pallas_call | solution.py:32
  62.4 0.9 %collective-permute-done.16.sent_ref.refs_4_ = bf16[1280,256]{1,0:T(8,128)(2,1)S(1)} collective-permute-done((bf16[1280,256]{1,0:T(8,128)(2,1)S(1)}, bf16[1280,256]{1,0:T(8,128)(2,1)S(1)}, u32[]{:S(2)}, u32[]{:S(2)}) %collective-permute-start.16) | collective-permute-done | bytes 655392 | tf_op jit(solution)/shard_map/ppermute | solution.py:417
  63.3 0.3 shard_map.198
  63.5 0.1 collective-permute-start.17
  63.6 2.1 %collective-permute-start.18 = (bf16[256,256]{1,0:T(8,128)(2,1)S(1)}, bf16[256,256]{1,0:T(8,128)(2,1)S(1)}, u32[]{:S(2)}, u32[]{:S(2)}) collective-permute-start(bf16[256,256]{1,0:T(8,128)(2,1)S(1)} %get-tuple-element.99), channel_id=1, source_target_pairs={{0,4},{1,5},{2,6},{3,7},{4,0},{5,1},{6,2},{7,3},{8,12},{9,13},{10,... | collective-permute-start | bytes 393224 | tf_op jit(solution)/shard_map/ppermute | solution.py:414
  65.7 1.7 %collective-permute-start.19 = (bf16[256,256]{1,0:T(8,128)(2,1)S(1)}, bf16[256,256]{1,0:T(8,128)(2,1)S(1)}, u32[]{:S(2)}, u32[]{:S(2)}) collective-permute-start(bf16[256,256]{1,0:T(8,128)(2,1)S(1)} %get-tuple-element.100), channel_id=1, source_target_pairs={{0,6},{1,7},{2,0},{3,1},{4,2},{5,3},{6,4},{7,5},{8,14},{9,15},{10,... | collective-permute-start | bytes 393224 | tf_op jit(solution)/shard_map/ppermute | solution.py:414
  67.4 3.0 %shard_map.195 = (f32[2048,256]{1,0:T(8,128)S(1)}, f32[2048,256]{1,0:T(8,128)S(1)}, f32[2048,256]{1,0:T(8,128)S(1)}) custom-call(f32[2048,256]{1,0:T(8,128)S(1)} %get-tuple-element.54.slip_ref, f32[2048,256]{1,0:T(8,128)S(1)} %get-tuple-element.67.state_ref, f32[2048,256]{1,0:T(8,128)S(1)} %get-tuple-element.83.speed_ref, ...), custom_call_target="tpu_custom_call" | custom-call | tf_op jit(solution)/shard_map/pallas_call | solution.py:32
  70.4 1.4 %collective-permute-done.17.refs_1_ = bf16[256,256]{1,0:T(8,128)(2,1)S(1)} collective-permute-done((bf16[256,256]{1,0:T(8,128)(2,1)S(1)}, bf16[256,256]{1,0:T(8,128)(2,1)S(1)}, u32[]{:S(2)}, u32[]{:S(2)}) %collective-permute-start.17) | collective-permute-done | bytes 131104 | tf_op jit(solution)/shard_map/ppermute | solution.py:414
  71.9 4.7 %collective-permute-done.18.refs_2_ = bf16[256,256]{1,0:T(8,128)(2,1)S(1)} collective-permute-done((bf16[256,256]{1,0:T(8,128)(2,1)S(1)}, bf16[256,256]{1,0:T(8,128)(2,1)S(1)}, u32[]{:S(2)}, u32[]{:S(2)}) %collective-permute-start.18) | collective-permute-done | bytes 131104 | tf_op jit(solution)/shard_map/ppermute | solution.py:414
  76.6 2.5 %shard_map.199 = (f32[2048,256]{1,0:T(8,128)}, f32[2048,256]{1,0:T(8,128)}) custom-call(f32[2048,256]{1,0:T(8,128)S(1)} %get-tuple-element.87.shift_ref, f32[2048,256]{1,0:T(8,128)S(1)} %get-tuple-element.85.scale_ref, f32[2048,256]{1,0:T(8,128)S(1)} %get-tuple-element.88.rest_ref, f32[2048,256]{1,0:T(8,128)S(1)} %get-tuple-element.89.slip_rest_ref, ...), custom_call_target="tpu_custom_call" | custom-call | tf_op jit(solution)/shard_map/pallas_call | solution.py:32
  (15 shorter events, 0.1 us)
Async XLA Ops:
  1.8 16.5 %collective-permute-start.3 = (bf16[256,256]{1,0:T(8,128)(2,1)S(1)}, bf16[256,256]{1,0:T(8,128)(2,1)S(1)}, u32[]{:S(2)}, u32[]{:S(2)}) collective-permute-start(bf16[256,256]{1,0:T(8,128)(2,1)S(1)} %get-tuple-element.59), channel_id=1, source_target_pairs={{1,2},{3,4},{5,6},{7,8},{9,10},{11,12},{13,14},{15,16},{17,18},{19... | collective-permute-start | bytes 393224 | tf_op jit(solution)/shard_map/ppermute | solution.py:421
  2.5 16.4 %collective-permute-start.2 = (bf16[128,512]{1,0:T(8,128)(2,1)S(1)}, bf16[128,512]{1,0:T(8,128)(2,1)S(1)}, u32[]{:S(2)}, u32[]{:S(2)}) collective-permute-start(bf16[128,512]{1,0:T(8,128)(2,1)S(1)} %get-tuple-element.70.refs_0_), channel_id=1, source_target_pairs={{0,6},{1,7},{2,0},{3,1},{4,2},{5,3},{6,4},{7,5},{8,14},{9,15},{10,... | collective-permute-start | bytes 393224 | tf_op jit(solution)/shard_map/ppermute | solution.py:414
  8.9 15.2 %collective-permute-start.1 = (bf16[128,512]{1,0:T(8,128)(2,1)S(1)}, bf16[128,512]{1,0:T(8,128)(2,1)S(1)}, u32[]{:S(2)}, u32[]{:S(2)}) collective-permute-start(bf16[128,512]{1,0:T(8,128)(2,1)S(1)} %get-tuple-element.70.refs_0_), channel_id=1, source_target_pairs={{0,4},{1,5},{2,6},{3,7},{4,0},{5,1},{6,2},{7,3},{8,12},{9,13},{10,... | collective-permute-start | bytes 393224 | tf_op jit(solution)/shard_map/ppermute | solution.py:414
  8.9 15.2 %collective-permute-start = (bf16[128,512]{1,0:T(8,128)(2,1)S(1)}, bf16[128,512]{1,0:T(8,128)(2,1)S(1)}, u32[]{:S(2)}, u32[]{:S(2)}) collective-permute-start(bf16[128,512]{1,0:T(8,128)(2,1)S(1)} %get-tuple-element.70.refs_0_), channel_id=1, source_target_pairs={{0,2},{1,3},{2,4},{3,5},{4,6},{5,7},{6,0},{7,1},{8,10},{9,11},{10,... | collective-permute-start | bytes 393224 | tf_op jit(solution)/shard_map/ppermute | solution.py:414
  15.5 8.6 %collective-permute-start.6 = (bf16[256,256]{1,0:T(8,128)(2,1)S(1)}, bf16[256,256]{1,0:T(8,128)(2,1)S(1)}, u32[]{:S(2)}, u32[]{:S(2)}) collective-permute-start(bf16[256,256]{1,0:T(8,128)(2,1)S(1)} %get-tuple-element.61.refs_9_.refs_0_), channel_id=1, source_target_pairs={{0,24},{8,0},{16,8},{24,16},{1,25},{9,1},{17,9},{25,17},{2,26},{10... | collective-permute-start | bytes 393224 | tf_op jit(solution)/shard_map/ppermute | solution.py:410
  18.4 8.4 %collective-permute-start.5 = (bf16[256,256]{1,0:T(8,128)(2,1)S(1)}, bf16[256,256]{1,0:T(8,128)(2,1)S(1)}, u32[]{:S(2)}, u32[]{:S(2)}) collective-permute-start(bf16[256,256]{1,0:T(8,128)(2,1)S(1)} %get-tuple-element.61.refs_9_.refs_0_), channel_id=1, source_target_pairs={{0,16},{8,24},{16,0},{24,8},{1,17},{9,25},{17,1},{25,9},{2,18},{10... | collective-permute-start | bytes 393224 | tf_op jit(solution)/shard_map/ppermute | solution.py:410
  18.9 7.9 %collective-permute-start.4 = (bf16[256,256]{1,0:T(8,128)(2,1)S(1)}, bf16[256,256]{1,0:T(8,128)(2,1)S(1)}, u32[]{:S(2)}, u32[]{:S(2)}) collective-permute-start(bf16[256,256]{1,0:T(8,128)(2,1)S(1)} %get-tuple-element.61.refs_9_.refs_0_), channel_id=1, source_target_pairs={{0,8},{8,16},{16,24},{24,0},{1,9},{9,17},{17,25},{25,1},{2,10},{10... | collective-permute-start | bytes 393224 | tf_op jit(solution)/shard_map/ppermute | solution.py:410
  28.0 2.2 %collective-permute-start.7 = (bf16[1280,256]{1,0:T(8,128)(2,1)S(1)}, bf16[1280,256]{1,0:T(8,128)(2,1)S(1)}, u32[]{:S(2)}, u32[]{:S(2)}) collective-permute-start(bf16[1280,256]{1,0:T(8,128)(2,1)S(1)} %shard_map.189), channel_id=1, source_target_pairs={{0,1},{1,0},{2,3},{3,2},{4,5},{5,4},{6,7},{7,6},{8,9},{9,8},{10,11... | collective-permute-start | bytes 1966088 | tf_op jit(solution)/shard_map/ppermute | solution.py:417
  28.1 10.8 %collective-permute-start.8 = (bf16[512,512]{1,0:T(8,128)(2,1)S(1)}, bf16[512,512]{1,0:T(8,128)(2,1)S(1)}, u32[]{:S(2)}, u32[]{:S(2)}) collective-permute-start(bf16[512,512]{1,0:T(8,128)(2,1)S(1)} %shard_map.192.own_ref), channel_id=1, source_target_pairs={{0,1},{1,0},{2,3},{3,2},{4,5},{5,4},{6,7},{7,6},{8,9},{9,8},{10,11... | collective-permute-start | bytes 1572872 | tf_op jit(solution)/shard_map/ppermute | solution.py:417
  30.4 13.4 %collective-permute-start.9 = (bf16[256,256]{1,0:T(8,128)(2,1)S(1)}, bf16[256,256]{1,0:T(8,128)(2,1)S(1)}, u32[]{:S(2)}, u32[]{:S(2)}) collective-permute-start(bf16[256,256]{1,0:T(8,128)(2,1)S(1)} %get-tuple-element.79), channel_id=1, source_target_pairs={{0,2},{1,3},{2,4},{3,5},{4,6},{5,7},{6,0},{7,1},{8,10},{9,11},{10,... | collective-permute-start | bytes 393224 | tf_op jit(solution)/shard_map/ppermute | solution.py:414
  32.0 11.9 %collective-permute-start.10 = (bf16[256,256]{1,0:T(8,128)(2,1)S(1)}, bf16[256,256]{1,0:T(8,128)(2,1)S(1)}, u32[]{:S(2)}, u32[]{:S(2)}) collective-permute-start(bf16[256,256]{1,0:T(8,128)(2,1)S(1)} %get-tuple-element.80), channel_id=1, source_target_pairs={{0,4},{1,5},{2,6},{3,7},{4,0},{5,1},{6,2},{7,3},{8,12},{9,13},{10,... | collective-permute-start | bytes 393224 | tf_op jit(solution)/shard_map/ppermute | solution.py:414
  33.3 10.6 %collective-permute-start.11 = (bf16[256,256]{1,0:T(8,128)(2,1)S(1)}, bf16[256,256]{1,0:T(8,128)(2,1)S(1)}, u32[]{:S(2)}, u32[]{:S(2)}) collective-permute-start(bf16[256,256]{1,0:T(8,128)(2,1)S(1)} %get-tuple-element.81), channel_id=1, source_target_pairs={{0,6},{1,7},{2,0},{3,1},{4,2},{5,3},{6,4},{7,5},{8,14},{9,15},{10,... | collective-permute-start | bytes 393224 | tf_op jit(solution)/shard_map/ppermute | solution.py:414
  38.9 5.0 %copy-start = (bf16[32,2048]{1,0:T(8,128)(2,1)S(1)}, bf16[32,2048]{1,0:T(8,128)(2,1)}, u32[]{:S(2)}) copy-start(bf16[32,2048]{1,0:T(8,128)(2,1)} %basis_out_ref.3) | copy-start | bytes 393220
  38.9 5.0 %copy-start.1 = (bf16[32,2048]{1,0:T(8,128)(2,1)S(1)}, bf16[32,2048]{1,0:T(8,128)(2,1)}, u32[]{:S(2)}) copy-start(bf16[32,2048]{1,0:T(8,128)(2,1)} %basis_in_ref.1) | copy-start | bytes 393220
  46.2 7.2 %collective-permute-start.15 = (bf16[256,256]{1,0:T(8,128)(2,1)S(1)}, bf16[256,256]{1,0:T(8,128)(2,1)S(1)}, u32[]{:S(2)}, u32[]{:S(2)}) collective-permute-start(bf16[256,256]{1,0:T(8,128)(2,1)S(1)} %get-tuple-element.91), channel_id=1, source_target_pairs={{1,2},{3,4},{5,6},{7,8},{9,10},{11,12},{13,14},{15,16},{17,18},{19... | collective-permute-start | bytes 393224 | tf_op jit(solution)/shard_map/ppermute | solution.py:421
  46.8 10.3 %collective-permute-start.14 = (bf16[256,256]{1,0:T(8,128)(2,1)S(1)}, bf16[256,256]{1,0:T(8,128)(2,1)S(1)}, u32[]{:S(2)}, u32[]{:S(2)}) collective-permute-start(bf16[256,256]{1,0:T(8,128)(2,1)S(1)} %get-tuple-element.92.refs_0_), channel_id=1, source_target_pairs={{0,24},{8,0},{16,8},{24,16},{1,25},{9,1},{17,9},{25,17},{2,26},{10... | collective-permute-start | bytes 393224 | tf_op jit(solution)/shard_map/ppermute | solution.py:410
  51.9 8.0 %collective-permute-start.13 = (bf16[256,256]{1,0:T(8,128)(2,1)S(1)}, bf16[256,256]{1,0:T(8,128)(2,1)S(1)}, u32[]{:S(2)}, u32[]{:S(2)}) collective-permute-start(bf16[256,256]{1,0:T(8,128)(2,1)S(1)} %get-tuple-element.92.refs_0_), channel_id=1, source_target_pairs={{0,16},{8,24},{16,0},{24,8},{1,17},{9,25},{17,1},{25,9},{2,18},{10... | collective-permute-start | bytes 393224 | tf_op jit(solution)/shard_map/ppermute | solution.py:410
  53.2 6.7 %collective-permute-start.12 = (bf16[256,256]{1,0:T(8,128)(2,1)S(1)}, bf16[256,256]{1,0:T(8,128)(2,1)S(1)}, u32[]{:S(2)}, u32[]{:S(2)}) collective-permute-start(bf16[256,256]{1,0:T(8,128)(2,1)S(1)} %get-tuple-element.92.refs_0_), channel_id=1, source_target_pairs={{0,8},{8,16},{16,24},{24,0},{1,9},{9,17},{17,25},{25,1},{2,10},{10... | collective-permute-start | bytes 393224 | tf_op jit(solution)/shard_map/ppermute | solution.py:410
  61.1 2.2 %collective-permute-start.16 = (bf16[1280,256]{1,0:T(8,128)(2,1)S(1)}, bf16[1280,256]{1,0:T(8,128)(2,1)S(1)}, u32[]{:S(2)}, u32[]{:S(2)}) collective-permute-start(bf16[1280,256]{1,0:T(8,128)(2,1)S(1)} %shard_map.197), channel_id=1, source_target_pairs={{0,1},{1,0},{2,3},{3,2},{4,5},{5,4},{6,7},{7,6},{8,9},{9,8},{10,11... | collective-permute-start | bytes 1966088 | tf_op jit(solution)/shard_map/ppermute | solution.py:417
  63.5 8.3 %collective-permute-start.17 = (bf16[256,256]{1,0:T(8,128)(2,1)S(1)}, bf16[256,256]{1,0:T(8,128)(2,1)S(1)}, u32[]{:S(2)}, u32[]{:S(2)}) collective-permute-start(bf16[256,256]{1,0:T(8,128)(2,1)S(1)} %get-tuple-element.98), channel_id=1, source_target_pairs={{0,2},{1,3},{2,4},{3,5},{4,6},{5,7},{6,0},{7,1},{8,10},{9,11},{10,... | collective-permute-start | bytes 393224 | tf_op jit(solution)/shard_map/ppermute | solution.py:414
  63.6 12.9 %collective-permute-start.18 = (bf16[256,256]{1,0:T(8,128)(2,1)S(1)}, bf16[256,256]{1,0:T(8,128)(2,1)S(1)}, u32[]{:S(2)}, u32[]{:S(2)}) collective-permute-start(bf16[256,256]{1,0:T(8,128)(2,1)S(1)} %get-tuple-element.99), channel_id=1, source_target_pairs={{0,4},{1,5},{2,6},{3,7},{4,0},{5,1},{6,2},{7,3},{8,12},{9,13},{10,... | collective-permute-start | bytes 393224 | tf_op jit(solution)/shard_map/ppermute | solution.py:414
  65.7 10.9 %collective-permute-start.19 = (bf16[256,256]{1,0:T(8,128)(2,1)S(1)}, bf16[256,256]{1,0:T(8,128)(2,1)S(1)}, u32[]{:S(2)}, u32[]{:S(2)}) collective-permute-start(bf16[256,256]{1,0:T(8,128)(2,1)S(1)} %get-tuple-element.100), channel_id=1, source_target_pairs={{0,6},{1,7},{2,0},{3,1},{4,2},{5,3},{6,4},{7,5},{8,14},{9,15},{10,... | collective-permute-start | bytes 393224 | tf_op jit(solution)/shard_map/ppermute | solution.py:414

commit v2 on v0

--- a/solution.py
+++ b/solution.py
@@ -56,9 +56,8 @@
     return copies
 
 
-def fill_edges(rounded_ref, pair_ref, cross_ref):
+def fill_edges(first, last, pair_ref, cross_ref):
     even = lax.rem(lax.axis_index("col"), 2) == 0
-    first, last = rounded_ref[:BS], rounded_ref[-BS:]
     pair_ref[...] = jnp.where(even, last, first)
     cross_ref[...] = jnp.where(even, first, last)
 
@@ -75,7 +74,7 @@
         rounded = slip_ref[at, :].astype(BF16)
         rounded_ref[at, :] = rounded
         coeff_ref[n * R : (n + 1) * R, :] = dot(basis_ref[:, at], rounded).astype(BF16)
-    fill_edges(rounded_ref, pair_ref, cross_ref)
+    fill_edges(rounded_ref[:BS], rounded_ref[-BS:], pair_ref, cross_ref)
 
 
 def project(slip, basis_in):
@@ -203,9 +202,10 @@
     row, col = lax.axis_index("row"), lax.axis_index("col")
     height, core = lax.div(col, 2), lax.rem(col + flip, 2)
 
-    @pl.loop(0, heights)
+    @pl.loop(0, heights, unroll=True)
     def _(d):
-        at = rows_at(2 * lax.rem(height + d, heights) + core, share)
+        partner = lax.rem(d, 2) * (1 - 2 * lax.rem(height, 2))
+        at = rows_at(2 * lax.rem(height + partner + d - lax.rem(d, 2) + heights, heights) + core, share)
         total = None
         for step in range(sources):
             term = dot(matrix_ref[lax.rem(row + (sources - step), sources), at, :], coeffs[step][...])
@@ -227,19 +227,37 @@
     )
 
 
-def chip_sum_kernel(kept_ref, sent_ref, *outs):
-    share = outs[0].shape[0]
-    for d, out_ref in enumerate(outs):
-
-        @pl.loop(0, share // 32)
+def chip_sum_kernel(kept_ref, sent_ref, own_ref, direct_ref, pass_ref, keep_ref):
+    share = own_ref.shape[0]
+    group = 32
+    for place in range(2 + 2 * (keep_ref.shape[0] // share)):
+        far = place // 2 - 1
+        out_ref = (own_ref, direct_ref)[place % 2] if far < 0 else (keep_ref, pass_ref)[place % 2]
+
+        @pl.loop(0, share // group)
         def _(n):
-            at = pl.ds(pl.multiple_of(d * share + n * 32, 32), 32)
-            out_ref[rows_at(n, 32), :] = (kept_ref[at, :] + sent_ref[at, :].astype(F32)).astype(BF16)
+            at = pl.ds(pl.multiple_of(place * share + n * group, group), group)
+            to = pl.ds(pl.multiple_of(max(far, 0) * share + n * group, group), group)
+            out_ref[to, :] = (kept_ref[at, :] + sent_ref[at, :].astype(F32)).astype(out_ref.dtype)
 
 
 def chip_sum(kept, sent, heights):
     rows, ens = kept.shape
-    return list(call(chip_sum_kernel, [jax.ShapeDtypeStruct((rows // heights, ens), BF16)] * heights, kept, sent))
+    share = rows // heights
+    far = (heights // 2 - 1) * share
+    shapes = [(share, BF16), (share, BF16), (far, BF16), (far, F32)]
+    return call(chip_sum_kernel, [jax.ShapeDtypeStruct((n, ens), kind) for n, kind in shapes], kept, sent)
+
+
+def pair_sum_kernel(keep_ref, came_ref, *outs):
+    share = outs[0].shape[0]
+    group = 32
+    for far, out_ref in enumerate(outs):
+
+        @pl.loop(0, share // group)
+        def _(n):
+            at = pl.ds(pl.multiple_of(far * share + n * group, group), group)
+            out_ref[rows_at(n, group), :] = (keep_ref[at, :] + came_ref[at, :].astype(F32)).astype(BF16)
 
 
 def near_tau(n, slip, numbers, near_ref, rounded_ref):
@@ -297,7 +315,7 @@
     pair, cross = pair_ref[-BS:], cross_ref[...]
     block(0, far(0) + dot(near_ref[0, :BS, :], jnp.where(even, cross, pair)))
 
-    @pl.loop(1, count - 1, unroll=2)
+    @pl.loop(1, count - 1, unroll=True)
     def _(n):
         block(n, far(n))
 
@@ -305,27 +323,25 @@
 
 
 def finish_first_kernel(
-    heights, shift_ref, scale_ref, rest_ref, slip_ref, numbers_ref, basis_out_ref, basis_in_ref, near_ref, *refs
+    count, shift_ref, scale_ref, slip_ref, basis_out_ref, basis_in_ref, near_ref, *refs
 ):
-    parts, pair_ref, cross_ref = refs[:heights], refs[heights], refs[heights + 1]
-    slip_mid_ref, state_mid_ref, rounded_ref, coeff_ref, pair_out, cross_out = refs[heights + 2 :]
+    parts, pair_ref, cross_ref = refs[:count], refs[count], refs[count + 1]
+    speed_ref, rounded_ref, coeff_ref, pair_out, cross_out = refs[count + 2 :]
 
     def block(n, outer):
         at = rows_at(n, BS)
         speed = jnp.exp(shift_ref[at, :] - scale_ref[at, :] * outer)
-        slip_mid = slip_ref[at, :] + STEP_SIZE * speed
-        slip_mid_ref[at, :] = slip_mid
-        state_mid_ref[at, :] = rest_ref[at, :] - (STEP_SIZE * numbers_ref[at, 4:5]) * speed
-        rounded = slip_mid.astype(BF16)
+        speed_ref[at, :] = speed
+        rounded = (slip_ref[at, :] + STEP_SIZE * speed).astype(BF16)
         rounded_ref[at, :] = rounded
         coeff_ref[rows_at(n, R), :] = dot(basis_in_ref[:, at], rounded).astype(BF16)
 
     over_blocks(block, basis_out_ref, near_ref, parts, pair_ref, cross_ref)
-    fill_edges(rounded_ref, pair_out, cross_out)
+    fill_edges(rounded_ref[:BS], rounded_ref[-BS:], pair_out, cross_out)
 
 
 def prepare_second_kernel(
-    slip_ref, state_ref, slip_mid_ref, state_mid_ref, scale_ref, numbers_ref, near_ref, rounded_ref,
+    slip_ref, state_ref, speed_ref, part_ref, scale_ref, numbers_ref, near_ref, rounded_ref,
     shift_ref, slip_rest_ref, rest_ref,
 ):
     @pl.loop(0, slip_ref.shape[0] // BS)
@@ -333,8 +349,9 @@
         at = rows_at(n, BS)
         numbers = numbers_ref[at, :]
         inv_direct, inv_evolution, ratio = (numbers[:, k : k + 1] for k in range(2, 5))
-        slip = slip_mid_ref[at, :]
-        state = state_mid_ref[at, :]
+        speed = speed_ref[at, :]
+        slip = slip_ref[at, :] + STEP_SIZE * speed
+        state = part_ref[at, :] - (STEP_SIZE * ratio) * speed
         tau = near_tau(n, slip, numbers, near_ref, rounded_ref)
         shift_ref[at, :] = tau * scale_ref[at, :] - state * inv_direct
         slip_rest_ref[at, :] = 0.5 * (slip_ref[at, :] + slip)
@@ -343,10 +360,10 @@
 
 
 def finish_second_kernel(
-    heights, shift_ref, scale_ref, rest_ref, slip_rest_ref, numbers_ref, basis_out_ref, near_ref, *refs
+    count, shift_ref, scale_ref, rest_ref, slip_rest_ref, numbers_ref, basis_out_ref, near_ref, *refs
 ):
-    parts, pair_ref, cross_ref = refs[:heights], refs[heights], refs[heights + 1]
-    slip_hbm, state_hbm, slip_ref, state_ref, sems = refs[heights + 2 :]
+    parts, pair_ref, cross_ref = refs[:count], refs[count], refs[count + 1]
+    slip_hbm, state_hbm, slip_ref, state_ref, sems = refs[count + 2 :]
 
     def copies(n):
         at = rows_at(n, BS)
@@ -427,13 +444,20 @@
     slots = adj_bricks.shape[0]
     size = pressure_now.shape[0]
     share = coupling.shape[2]
-    def far_parts(coeffs, pair, cross):
+    def to_partner(array):
+        pairs = [(2 * z + k, 2 * (z + 1 - 2 * (z % 2)) + k) for z in range(heights) for k in range(2)]
+        return lax.ppermute(array, "col", pairs)
+
+    def first_step(coeffs, pair, cross):
         sent = to_core(couple(1, masked, coeffs, heights, BF16, pair))
         kept = couple(0, masked, coeffs, heights, F32)
-        pieces = chip_sum(kept, sent, heights)
-        pieces, cross = lax.optimization_barrier((pieces, cross))
-        parts = pieces[:1] + [to_height(pieces[d], d) for d in range(1, heights)]
-        return parts + [sent, to_chip(cross)]
+        own, direct, passed, keep = chip_sum(kept, sent, heights)
+        own, cross = lax.optimization_barrier((own, cross))
+        return own, to_partner(passed), to_partner(direct), keep, [sent, to_chip(cross)]
+
+    def second_step(own, came, direct, keep, edges):
+        sums = call(pair_sum_kernel, [jax.ShapeDtypeStruct((share, ens), BF16)] * (heights // 2 - 1), keep, came)
+        return [to_height(part, 2 * (d + 1)) for d, part in enumerate(sums)] + [own, direct] + edges
 
     def row_coeffs(coeff):
         return [coeff] + [to_row(coeff, d) for d in range(1, row_count)]
@@ -483,32 +507,34 @@
         side_by_side_kernel, jax.ShapeDtypeStruct((heights * size, 2 * ens), BF16), *fields
     )
     other = to_core(own)
-    outer = far_parts(coeffs, pair, cross)
+    own_part, came, direct, keep, edges = first_step(coeffs, pair, cross)
     numbers, high, near, state = call(
         functools.partial(weights_kernel, heights, size, start),
         [jax.ShapeDtypeStruct((patches, 8), F32), part, jax.ShapeDtypeStruct(near_blocks.shape, BF16), full],
         *in_hbm(*columns, near_blocks, state),
         numbers,
-        outer[0],
+        own_part,
         specs=[HBM] * 11 + [VMEM] * 2,
         scratch_shapes=scratch,
     )
+    came, high = lax.optimization_barrier((came, high))
+    outer = second_step(own_part, came, direct, keep, edges)
     shift, scale, rest, scale_mid = call(
         prepare_first_kernel, [full] * 4, low, high, own, other, slip, state, numbers, near, rounded
     )
-    slip_mid, state_mid, rounded, coeff, pair, cross = call(
-        functools.partial(finish_first_kernel, heights),
-        [full, full, half, jax.ShapeDtypeStruct((patches // BS * R, ens), BF16), edge, edge],
-        shift, scale, rest, slip, numbers, basis_out, basis_in, near, *outer,
+    speed, rounded, coeff, pair, cross = call(
+        functools.partial(finish_first_kernel, len(outer) - 2),
+        [full, half, jax.ShapeDtypeStruct((patches // BS * R, ens), BF16), edge, edge],
+        shift, scale, slip, basis_out, basis_in, near, *outer,
     )
     coeffs = row_coeffs(coeff)
-    outer = far_parts(coeffs, pair, cross)
+    outer = second_step(*first_step(coeffs, pair, cross))
     shift, slip_rest, rest = call(
         prepare_second_kernel, [full] * 3,
-        slip, state, slip_mid, state_mid, scale_mid, numbers, near, rounded,
+        slip, state, speed, rest, scale_mid, numbers, near, rounded,
     )
     slip_out, state_out = call(
-        functools.partial(finish_second_kernel, heights),
+        functools.partial(finish_second_kernel, len(outer) - 2),
         [full] * 2,
         shift, scale_mid, rest, slip_rest, numbers, basis_out, near, *outer,
         out_specs=[HBM] * 2,

time: 77.8 us -> 76.1 us (0.978)
  the two profiles are of different devices: /device:TPU:9 before, /device:TPU:0 now
where the time goes in v2:
time: 76.1 us; the launch traced here: 75.7 us
  Pallas kernels  26.6 us (35%)
  starting transfers between devices  24.9 us (33%)
  waiting for transfers between devices  20.1 us (26%)
  other arithmetic  3.13 us (4%)
  between operations  0.87 us (1%)
    pallas_call x17, Pallas kernels, call(): pl.pallas_call(kernel, in_specs=specs or [VMEM] * len(operands), out_shap...  26.6 us
    ppermute x4, starting transfers between devices, to_partner(): return lax.ppermute(array, 'col', pairs)  8.72 us
    ppermute x6, waiting for transfers between devices, to_row(): lax.ppermute(array, 'row', [(i, (i + d) % row_count) for i in range(row_c...  8.36 us
    ppermute x5, starting transfers between devices, to_height(): return lax.ppermute(array, 'col', pairs)  7.58 us
    ppermute x6, starting transfers between devices, to_row(): lax.ppermute(array, 'row', [(i, (i + d) % row_count) for i in range(row_c...  6.59 us
    ppermute x4, waiting for transfers between devices, to_partner(): return lax.ppermute(array, 'col', pairs)  6.53 us
    select_n x1, other arithmetic, masked_coupling(): jnp.where(keep, matrix, jnp.zeros((), BF16)).reshape(sources, rows, width)  3.13 us
    ppermute x5, waiting for transfers between devices, to_height(): return lax.ppermute(array, 'col', pairs)  3.09 us
  transfers between devices with their start and end apart: 20, of which 8 were waited for; matrix products, arithmetic and copies ran while one was open for 4% of the time, Pallas kernels for 26%

profile of v2, /device:TPU:0, one launch (start us, length us, event | category | flops | bytes accessed | tf_op | source)
XLA Modules:
  0.0 75.7 jit_solution(654243482016952053)
XLA Ops:
  0.6 1.0 %shard_map.185 = (f32[4,64,256]{2,1,0:T(8,128)S(1)}, bf16[128,512]{1,0:T(8,128)(2,1)S(1)}) custom-call(s32[4,8,64]{2,1,0:T(8,128)} %bitcast.28, bf16[128,256]{1,0:T(8,128)(2,1)} %now_hbm.1, bf16[128,256]{1,0:T(8,128)(2,1)} %rate_hbm.1), custom_call_target="tpu_custom_call" | custom-call | tf_op jit(solution)/shard_map/pallas_call | solution.py:32
  1.6 5.1 %collective-permute-start.2 = (bf16[128,512]{1,0:T(8,128)(2,1)S(1)}, bf16[128,512]{1,0:T(8,128)(2,1)S(1)}, u32[]{:S(2)}, u32[]{:S(2)}) collective-permute-start(bf16[128,512]{1,0:T(8,128)(2,1)S(1)} %get-tuple-element.73.refs_0_), channel_id=1, source_target_pairs={{0,6},{1,7},{2,0},{3,1},{4,2},{5,3},{6,4},{7,5},{8,14},{9,15},{10,... | collective-permute-start | bytes 393224 | tf_op jit(solution)/shard_map/ppermute | solution.py:434
  6.7 1.0 %collective-permute-start = (bf16[128,512]{1,0:T(8,128)(2,1)S(1)}, bf16[128,512]{1,0:T(8,128)(2,1)S(1)}, u32[]{:S(2)}, u32[]{:S(2)}) collective-permute-start(bf16[128,512]{1,0:T(8,128)(2,1)S(1)} %get-tuple-element.73.refs_0_), channel_id=1, source_target_pairs={{0,2},{1,3},{2,4},{3,5},{4,6},{5,7},{6,0},{7,1},{8,10},{9,11},{10,... | collective-permute-start | bytes 393224 | tf_op jit(solution)/shard_map/ppermute | solution.py:434
  7.7 0.1 lt.21
  7.8 3.1 %fusion.matrix_ref = bf16[4,2048,256]{2,1,0:T(8,128)(2,1)S(1)} fusion(bf16[2048,4,256]{2,1,0:T(4,128)(2,1)} %param.29, f32[4,64,256]{2,1,0:T(8,128)S(1)} %get-tuple-element.52, f32[2048]{0:T(1024)S(1)} %lt.21), kind=kLoop, calls=%fused_computation.1 | loop fusion | flops 4194304 | bytes 8658944 | tf_op jit(solution)/shard_map/jit(_where)/select_n | solution.py:396
  10.9 2.4 %shard_map.186 = (bf16[256,256]{1,0:T(8,128)(2,1)S(1)}, bf16[2048,256]{1,0:T(8,128)(2,1)S(1)}, bf16[256,256]{1,0:T(8,128)(2,1)S(1)}, bf16[256,256]{1,0:T(8,128)(2,1)S(1)}, f32[2048,256]{1,0:T(8,128)S(1)}) custom-call(f32[2048,256]{1,0:T(8,128)} %slip_hbm, bf16[32,2048]{1,0:T(8,128)(2,1)} %basis_in_ref.1), custom_call_target="tpu_custom_call" | custom-call | tf_op jit(solution)/shard_map/pallas_call | solution.py:32
  13.3 2.5 %collective-permute-start.5 = (bf16[256,256]{1,0:T(8,128)(2,1)S(1)}, bf16[256,256]{1,0:T(8,128)(2,1)S(1)}, u32[]{:S(2)}, u32[]{:S(2)}) collective-permute-start(bf16[256,256]{1,0:T(8,128)(2,1)S(1)} %get-tuple-element.60.refs_9_.refs_0_), channel_id=1, source_target_pairs={{0,24},{8,0},{16,8},{24,16},{1,25},{9,1},{17,9},{25,17},{2,26},{10... | collective-permute-start | bytes 393224 | tf_op jit(solution)/shard_map/ppermute | solution.py:430
  15.8 0.5 collective-permute-start.4
  16.3 0.0 collective-permute-done.2.refs_3_
  16.3 0.6 collective-permute-start.3
  16.9 3.7 %shard_map.187 = (f32[1024,8]{1,0:T(8,128)S(1)}, bf16[1024,1024]{1,0:T(8,128)(2,1)S(1)}) custom-call(f32[1,2048]{1,0:T(1,128)} %bitcast.14, f32[1,2048]{1,0:T(1,128)} %bitcast.16, f32[1,2048]{1,0:T(1,128)} %bitcast.18, f32[1,2048]{1,0:T(1,128)} %bitcast.20, f32[1,2048]{1,0:T(1,128)} %bitcast.22, f32[1,2048]{1,0:T(1,128)} %bitcast.24, s32[1,2048]{1,0:T(1,128)} %bitcast.26, ...), custom_call_target="tpu_custom_call" | custom-call | tf_op jit(solution)/shard_map/pallas_call | solution.py:32
  20.6 0.0 collective-permute-done.5.refs_3_
  20.6 2.3 %collective-permute-done.4.refs_2_ = bf16[256,256]{1,0:T(8,128)(2,1)S(1)} collective-permute-done((bf16[256,256]{1,0:T(8,128)(2,1)S(1)}, bf16[256,256]{1,0:T(8,128)(2,1)S(1)}, u32[]{:S(2)}, u32[]{:S(2)}) %collective-permute-start.4) | collective-permute-done | bytes 131104 | tf_op jit(solution)/shard_map/ppermute | solution.py:430
  23.0 0.0 collective-permute-done.3.refs_1_
  23.0 0.7 shard_map.189
  23.7 0.1 collective-permute-start.6
  23.8 0.6 collective-permute-start.8
  24.4 0.7 shard_map.188.kept_ref
  25.1 0.8 %collective-permute-done.6.sent_ref.refs_3_ = bf16[1280,256]{1,0:T(8,128)(2,1)S(1)} collective-permute-done((bf16[1280,256]{1,0:T(8,128)(2,1)S(1)}, bf16[1280,256]{1,0:T(8,128)(2,1)S(1)}, u32[]{:S(2)}, u32[]{:S(2)}) %collective-permute-start.6) | collective-permute-done | bytes 655392 | tf_op jit(solution)/shard_map/ppermute | solution.py:437
  25.9 0.3 shard_map.190
  26.1 2.5 %collective-permute-start.7 = (bf16[256,256]{1,0:T(8,128)(2,1)S(1)}, bf16[256,256]{1,0:T(8,128)(2,1)S(1)}, u32[]{:S(2)}, u32[]{:S(2)}) collective-permute-start(bf16[256,256]{1,0:T(8,128)(2,1)S(1)} %get-tuple-element.70), channel_id=1, source_target_pairs={{0,2},{1,3},{2,0},{3,1},{4,6},{5,7},{6,4},{7,5},{8,10},{9,11},{10,... | collective-permute-start | bytes 393224 | tf_op jit(solution)/shard_map/ppermute | solution.py:449
  28.7 0.7 collective-permute-start.11
  29.3 2.8 %collective-permute-start.10 = (bf16[256,256]{1,0:T(8,128)(2,1)S(1)}, bf16[256,256]{1,0:T(8,128)(2,1)S(1)}, u32[]{:S(2)}, u32[]{:S(2)}) collective-permute-start(bf16[256,256]{1,0:T(8,128)(2,1)S(1)} %get-tuple-element.84), channel_id=1, source_target_pairs={{0,2},{1,3},{2,0},{3,1},{4,6},{5,7},{6,4},{7,5},{8,10},{9,11},{10,... | collective-permute-start | bytes 393224 | tf_op jit(solution)/shard_map/ppermute | solution.py:449
  32.1 3.7 %shard_map.191 = (f32[2048,8]{1,0:T(8,128)S(1)}, bf16[1024,1024]{1,0:T(8,128)(2,1)S(1)}, bf16[3,2048,256]{2,1,0:T(8,128)(2,1)S(1)}, f32[2048,256]{1,0:T(8,128)S(1)}) custom-call(f32[1,2048]{1,0:T(1,128)} %bitcast.15, f32[1,2048]{1,0:T(1,128)} %bitcast.17, f32[1,2048]{1,0:T(1,128)} %bitcast.19, f32[1,2048]{1,0:T(1,128)} %bitcast.21, f32[1,2048]{1,0:T(1,128)} %bitcast.23, ...), custom_call_target="tpu_custom_call" | custom-call | tf_op jit(solution)/shard_map/pallas_call | solution.py:32
  35.8 0.0 collective-permute-done.7.came_ref
  35.8 0.1 shard_map.194
  35.9 1.1 %collective-permute-start.9 = (bf16[256,256]{1,0:T(8,128)(2,1)S(1)}, bf16[256,256]{1,0:T(8,128)(2,1)S(1)}, u32[]{:S(2)}, u32[]{:S(2)}) collective-permute-start(bf16[256,256]{1,0:T(8,128)(2,1)S(1)} %shard_map.194), channel_id=1, source_target_pairs={{0,4},{1,5},{2,6},{3,7},{4,0},{5,1},{6,2},{7,3},{8,12},{9,13},{10,... | collective-permute-start | bytes 393224 | tf_op jit(solution)/shard_map/ppermute | solution.py:434
  37.0 4.9 %shard_map.193 = (f32[2048,256]{1,0:T(8,128)S(1)}, f32[2048,256]{1,0:T(8,128)S(1)}, f32[2048,256]{1,0:T(8,128)S(1)}, f32[2048,256]{1,0:T(8,128)S(1)}) custom-call(bf16[1024,1024]{1,0:T(8,128)(2,1)S(1)} %get-tuple-element.69.low_ref, bf16[1024,1024]{1,0:T(8,128)(2,1)S(1)} %get-tuple-element.72.high_ref, bf16[512,512]{1,0:T(8,128)(2,1)S(1)} %shard_map.192.own_ref, ...), custom_call_target="tpu_custom_call" | custom-call | tf_op jit(solution)/shard_map/pallas_call | solution.py:32
  42.0 3.1 %collective-permute-done.9.refs_0_ = bf16[256,256]{1,0:T(8,128)(2,1)S(1)} collective-permute-done((bf16[256,256]{1,0:T(8,128)(2,1)S(1)}, bf16[256,256]{1,0:T(8,128)(2,1)S(1)}, u32[]{:S(2)}, u32[]{:S(2)}) %collective-permute-start.9) | collective-permute-done | bytes 131104 | tf_op jit(solution)/shard_map/ppermute | solution.py:434
  45.1 1.8 %shard_map.195 = (f32[2048,256]{1,0:T(8,128)S(1)}, bf16[2048,256]{1,0:T(8,128)(2,1)S(1)}, bf16[256,256]{1,0:T(8,128)(2,1)S(1)}, bf16[256,256]{1,0:T(8,128)(2,1)S(1)}, bf16[256,256]{1,0:T(8,128)(2,1)S(1)}) custom-call(f32[2048,256]{1,0:T(8,128)S(1)} %get-tuple-element.80.shift_ref, f32[2048,256]{1,0:T(8,128)S(1)} %get-tuple-element.81.scale_ref, ...), custom_call_target="tpu_custom_call" | custom-call | tf_op jit(solution)/shard_map/pallas_call | solution.py:32
  46.9 0.2 collective-permute-start.14
  47.1 2.5 %collective-permute-start.13 = (bf16[256,256]{1,0:T(8,128)(2,1)S(1)}, bf16[256,256]{1,0:T(8,128)(2,1)S(1)}, u32[]{:S(2)}, u32[]{:S(2)}) collective-permute-start(bf16[256,256]{1,0:T(8,128)(2,1)S(1)} %get-tuple-element.93.refs_0_), channel_id=1, source_target_pairs={{0,16},{8,24},{16,0},{24,8},{1,17},{9,25},{17,1},{25,9},{2,18},{10... | collective-permute-start | bytes 393224 | tf_op jit(solution)/shard_map/ppermute | solution.py:430
  49.6 0.3 collective-permute-start.12
  49.9 2.8 %collective-permute-done.14.refs_3_ = bf16[256,256]{1,0:T(8,128)(2,1)S(1)} collective-permute-done((bf16[256,256]{1,0:T(8,128)(2,1)S(1)}, bf16[256,256]{1,0:T(8,128)(2,1)S(1)}, u32[]{:S(2)}, u32[]{:S(2)}) %collective-permute-start.14) | collective-permute-done | bytes 131104 | tf_op jit(solution)/shard_map/ppermute | solution.py:430
  52.7 3.2 %collective-permute-done.13.refs_2_ = bf16[256,256]{1,0:T(8,128)(2,1)S(1)} collective-permute-done((bf16[256,256]{1,0:T(8,128)(2,1)S(1)}, bf16[256,256]{1,0:T(8,128)(2,1)S(1)}, u32[]{:S(2)}, u32[]{:S(2)}) %collective-permute-start.13) | collective-permute-done | bytes 131104 | tf_op jit(solution)/shard_map/ppermute | solution.py:430
  55.9 0.7 shard_map.198
  56.6 0.1 collective-permute-start.15
  56.7 0.7 shard_map.197.kept_ref
  57.4 1.4 %collective-permute-done.15.sent_ref.refs_3_ = bf16[1280,256]{1,0:T(8,128)(2,1)S(1)} collective-permute-done((bf16[1280,256]{1,0:T(8,128)(2,1)S(1)}, bf16[1280,256]{1,0:T(8,128)(2,1)S(1)}, u32[]{:S(2)}, u32[]{:S(2)}) %collective-permute-start.15) | collective-permute-done | bytes 655392 | tf_op jit(solution)/shard_map/ppermute | solution.py:437
  58.8 0.3 shard_map.199
  59.1 0.1 collective-permute-start.16
  59.1 0.7 collective-permute-start.19
  59.8 3.3 %collective-permute-start.18 = (bf16[256,256]{1,0:T(8,128)(2,1)S(1)}, bf16[256,256]{1,0:T(8,128)(2,1)S(1)}, u32[]{:S(2)}, u32[]{:S(2)}) collective-permute-start(bf16[256,256]{1,0:T(8,128)(2,1)S(1)} %get-tuple-element.100), channel_id=1, source_target_pairs={{0,2},{1,3},{2,0},{3,1},{4,6},{5,7},{6,4},{7,5},{8,10},{9,11},{10,... | collective-permute-start | bytes 393224 | tf_op jit(solution)/shard_map/ppermute | solution.py:449
  63.1 1.5 %collective-permute-done.16.came_ref = bf16[256,256]{1,0:T(8,128)(2,1)S(1)} collective-permute-done((bf16[256,256]{1,0:T(8,128)(2,1)S(1)}, bf16[256,256]{1,0:T(8,128)(2,1)S(1)}, u32[]{:S(2)}, u32[]{:S(2)}) %collective-permute-start.16) | collective-permute-done | bytes 131104 | tf_op jit(solution)/shard_map/ppermute | solution.py:449
  64.7 0.3 collective-permute-start.17
  65.1 3.0 %shard_map.196 = (f32[2048,256]{1,0:T(8,128)S(1)}, f32[2048,256]{1,0:T(8,128)S(1)}, f32[2048,256]{1,0:T(8,128)S(1)}) custom-call(f32[2048,256]{1,0:T(8,128)S(1)} %get-tuple-element.54.slip_ref, f32[2048,256]{1,0:T(8,128)S(1)} %get-tuple-element.68.state_ref, f32[2048,256]{1,0:T(8,128)S(1)} %get-tuple-element.86.speed_ref, ...), custom_call_target="tpu_custom_call" | custom-call | tf_op jit(solution)/shard_map/pallas_call | solution.py:32
  68.1 5.0 %collective-permute-done.18.refs_2_ = bf16[256,256]{1,0:T(8,128)(2,1)S(1)} collective-permute-done((bf16[256,256]{1,0:T(8,128)(2,1)S(1)}, bf16[256,256]{1,0:T(8,128)(2,1)S(1)}, u32[]{:S(2)}, u32[]{:S(2)}) %collective-permute-start.18) | collective-permute-done | bytes 131104 | tf_op jit(solution)/shard_map/ppermute | solution.py:449
  73.1 2.6 %shard_map.201 = (f32[2048,256]{1,0:T(8,128)}, f32[2048,256]{1,0:T(8,128)}) custom-call(f32[2048,256]{1,0:T(8,128)S(1)} %get-tuple-element.90.shift_ref, f32[2048,256]{1,0:T(8,128)S(1)} %get-tuple-element.88.scale_ref, f32[2048,256]{1,0:T(8,128)S(1)} %get-tuple-element.91.rest_ref, f32[2048,256]{1,0:T(8,128)S(1)} %get-tuple-element.92.slip_rest_ref, ...), custom_call_target="tpu_custom_call" | custom-call | tf_op jit(solution)/shard_map/pallas_call | solution.py:32
  (17 shorter events, 0.1 us)
Async XLA Ops:
  1.6 14.7 %collective-permute-start.2 = (bf16[128,512]{1,0:T(8,128)(2,1)S(1)}, bf16[128,512]{1,0:T(8,128)(2,1)S(1)}, u32[]{:S(2)}, u32[]{:S(2)}) collective-permute-start(bf16[128,512]{1,0:T(8,128)(2,1)S(1)} %get-tuple-element.73.refs_0_), channel_id=1, source_target_pairs={{0,6},{1,7},{2,0},{3,1},{4,2},{5,3},{6,4},{7,5},{8,14},{9,15},{10,... | collective-permute-start | bytes 393224 | tf_op jit(solution)/shard_map/ppermute | solution.py:434
  6.7 13.9 %collective-permute-start.1 = (bf16[128,512]{1,0:T(8,128)(2,1)S(1)}, bf16[128,512]{1,0:T(8,128)(2,1)S(1)}, u32[]{:S(2)}, u32[]{:S(2)}) collective-permute-start(bf16[128,512]{1,0:T(8,128)(2,1)S(1)} %get-tuple-element.73.refs_0_), channel_id=1, source_target_pairs={{0,4},{1,5},{2,6},{3,7},{4,0},{5,1},{6,2},{7,3},{8,12},{9,13},{10,... | collective-permute-start | bytes 393224 | tf_op jit(solution)/shard_map/ppermute | solution.py:434
  6.7 13.9 %collective-permute-start = (bf16[128,512]{1,0:T(8,128)(2,1)S(1)}, bf16[128,512]{1,0:T(8,128)(2,1)S(1)}, u32[]{:S(2)}, u32[]{:S(2)}) collective-permute-start(bf16[128,512]{1,0:T(8,128)(2,1)S(1)} %get-tuple-element.73.refs_0_), channel_id=1, source_target_pairs={{0,2},{1,3},{2,4},{3,5},{4,6},{5,7},{6,0},{7,1},{8,10},{9,11},{10,... | collective-permute-start | bytes 393224 | tf_op jit(solution)/shard_map/ppermute | solution.py:434
  13.3 7.3 %collective-permute-start.5 = (bf16[256,256]{1,0:T(8,128)(2,1)S(1)}, bf16[256,256]{1,0:T(8,128)(2,1)S(1)}, u32[]{:S(2)}, u32[]{:S(2)}) collective-permute-start(bf16[256,256]{1,0:T(8,128)(2,1)S(1)} %get-tuple-element.60.refs_9_.refs_0_), channel_id=1, source_target_pairs={{0,24},{8,0},{16,8},{24,16},{1,25},{9,1},{17,9},{25,17},{2,26},{10... | collective-permute-start | bytes 393224 | tf_op jit(solution)/shard_map/ppermute | solution.py:430
  15.8 7.2 %collective-permute-start.4 = (bf16[256,256]{1,0:T(8,128)(2,1)S(1)}, bf16[256,256]{1,0:T(8,128)(2,1)S(1)}, u32[]{:S(2)}, u32[]{:S(2)}) collective-permute-start(bf16[256,256]{1,0:T(8,128)(2,1)S(1)} %get-tuple-element.60.refs_9_.refs_0_), channel_id=1, source_target_pairs={{0,16},{8,24},{16,0},{24,8},{1,17},{9,25},{17,1},{25,9},{2,18},{10... | collective-permute-start | bytes 393224 | tf_op jit(solution)/shard_map/ppermute | solution.py:430
  16.3 6.7 %collective-permute-start.3 = (bf16[256,256]{1,0:T(8,128)(2,1)S(1)}, bf16[256,256]{1,0:T(8,128)(2,1)S(1)}, u32[]{:S(2)}, u32[]{:S(2)}) collective-permute-start(bf16[256,256]{1,0:T(8,128)(2,1)S(1)} %get-tuple-element.60.refs_9_.refs_0_), channel_id=1, source_target_pairs={{0,8},{8,16},{16,24},{24,0},{1,9},{9,17},{17,25},{25,1},{2,10},{10... | collective-permute-start | bytes 393224 | tf_op jit(solution)/shard_map/ppermute | solution.py:430
  23.7 2.2 %collective-permute-start.6 = (bf16[1280,256]{1,0:T(8,128)(2,1)S(1)}, bf16[1280,256]{1,0:T(8,128)(2,1)S(1)}, u32[]{:S(2)}, u32[]{:S(2)}) collective-permute-start(bf16[1280,256]{1,0:T(8,128)(2,1)S(1)} %shard_map.189), channel_id=1, source_target_pairs={{0,1},{1,0},{2,3},{3,2},{4,5},{5,4},{6,7},{7,6},{8,9},{9,8},{10,11... | collective-permute-start | bytes 1966088 | tf_op jit(solution)/shard_map/ppermute | solution.py:437
  23.8 13.2 %collective-permute-start.8 = (bf16[512,512]{1,0:T(8,128)(2,1)S(1)}, bf16[512,512]{1,0:T(8,128)(2,1)S(1)}, u32[]{:S(2)}, u32[]{:S(2)}) collective-permute-start(bf16[512,512]{1,0:T(8,128)(2,1)S(1)} %shard_map.192.own_ref), channel_id=1, source_target_pairs={{0,1},{1,0},{2,3},{3,2},{4,5},{5,4},{6,7},{7,6},{8,9},{9,8},{10,11... | collective-permute-start | bytes 1572872 | tf_op jit(solution)/shard_map/ppermute | solution.py:437
  26.1 9.7 %collective-permute-start.7 = (bf16[256,256]{1,0:T(8,128)(2,1)S(1)}, bf16[256,256]{1,0:T(8,128)(2,1)S(1)}, u32[]{:S(2)}, u32[]{:S(2)}) collective-permute-start(bf16[256,256]{1,0:T(8,128)(2,1)S(1)} %get-tuple-element.70), channel_id=1, source_target_pairs={{0,2},{1,3},{2,0},{3,1},{4,6},{5,7},{6,4},{7,5},{8,10},{9,11},{10,... | collective-permute-start | bytes 393224 | tf_op jit(solution)/shard_map/ppermute | solution.py:449
  28.7 13.3 %collective-permute-start.11 = (bf16[256,256]{1,0:T(8,128)(2,1)S(1)}, bf16[256,256]{1,0:T(8,128)(2,1)S(1)}, u32[]{:S(2)}, u32[]{:S(2)}) collective-permute-start(bf16[256,256]{1,0:T(8,128)(2,1)S(1)} %get-tuple-element.85), channel_id=1, source_target_pairs={{1,2},{3,4},{5,6},{7,8},{9,10},{11,12},{13,14},{15,16},{17,18},{19... | collective-permute-start | bytes 393224 | tf_op jit(solution)/shard_map/ppermute | solution.py:441
  29.3 12.6 %collective-permute-start.10 = (bf16[256,256]{1,0:T(8,128)(2,1)S(1)}, bf16[256,256]{1,0:T(8,128)(2,1)S(1)}, u32[]{:S(2)}, u32[]{:S(2)}) collective-permute-start(bf16[256,256]{1,0:T(8,128)(2,1)S(1)} %get-tuple-element.84), channel_id=1, source_target_pairs={{0,2},{1,3},{2,0},{3,1},{4,6},{5,7},{6,4},{7,5},{8,10},{9,11},{10,... | collective-permute-start | bytes 393224 | tf_op jit(solution)/shard_map/ppermute | solution.py:449
  35.9 9.1 %collective-permute-start.9 = (bf16[256,256]{1,0:T(8,128)(2,1)S(1)}, bf16[256,256]{1,0:T(8,128)(2,1)S(1)}, u32[]{:S(2)}, u32[]{:S(2)}) collective-permute-start(bf16[256,256]{1,0:T(8,128)(2,1)S(1)} %shard_map.194), channel_id=1, source_target_pairs={{0,4},{1,5},{2,6},{3,7},{4,0},{5,1},{6,2},{7,3},{8,12},{9,13},{10,... | collective-permute-start | bytes 393224 | tf_op jit(solution)/shard_map/ppermute | solution.py:434
  37.0 8.0 %copy-start = (bf16[32,2048]{1,0:T(8,128)(2,1)S(1)}, bf16[32,2048]{1,0:T(8,128)(2,1)}, u32[]{:S(2)}) copy-start(bf16[32,2048]{1,0:T(8,128)(2,1)} %basis_out_ref.3) | copy-start | bytes 393220
  37.0 8.0 %copy-start.1 = (bf16[32,2048]{1,0:T(8,128)(2,1)S(1)}, bf16[32,2048]{1,0:T(8,128)(2,1)}, u32[]{:S(2)}) copy-start(bf16[32,2048]{1,0:T(8,128)(2,1)} %basis_in_ref.1) | copy-start | bytes 393220
  46.9 5.8 %collective-permute-start.14 = (bf16[256,256]{1,0:T(8,128)(2,1)S(1)}, bf16[256,256]{1,0:T(8,128)(2,1)S(1)}, u32[]{:S(2)}, u32[]{:S(2)}) collective-permute-start(bf16[256,256]{1,0:T(8,128)(2,1)S(1)} %get-tuple-element.93.refs_0_), channel_id=1, source_target_pairs={{0,24},{8,0},{16,8},{24,16},{1,25},{9,1},{17,9},{25,17},{2,26},{10... | collective-permute-start | bytes 393224 | tf_op jit(solution)/shard_map/ppermute | solution.py:430
  47.1 8.8 %collective-permute-start.13 = (bf16[256,256]{1,0:T(8,128)(2,1)S(1)}, bf16[256,256]{1,0:T(8,128)(2,1)S(1)}, u32[]{:S(2)}, u32[]{:S(2)}) collective-permute-start(bf16[256,256]{1,0:T(8,128)(2,1)S(1)} %get-tuple-element.93.refs_0_), channel_id=1, source_target_pairs={{0,16},{8,24},{16,0},{24,8},{1,17},{9,25},{17,1},{25,9},{2,18},{10... | collective-permute-start | bytes 393224 | tf_op jit(solution)/shard_map/ppermute | solution.py:430
  49.6 6.3 %collective-permute-start.12 = (bf16[256,256]{1,0:T(8,128)(2,1)S(1)}, bf16[256,256]{1,0:T(8,128)(2,1)S(1)}, u32[]{:S(2)}, u32[]{:S(2)}) collective-permute-start(bf16[256,256]{1,0:T(8,128)(2,1)S(1)} %get-tuple-element.93.refs_0_), channel_id=1, source_target_pairs={{0,8},{8,16},{16,24},{24,0},{1,9},{9,17},{17,25},{25,1},{2,10},{10... | collective-permute-start | bytes 393224 | tf_op jit(solution)/shard_map/ppermute | solution.py:430
  56.6 2.2 %collective-permute-start.15 = (bf16[1280,256]{1,0:T(8,128)(2,1)S(1)}, bf16[1280,256]{1,0:T(8,128)(2,1)S(1)}, u32[]{:S(2)}, u32[]{:S(2)}) collective-permute-start(bf16[1280,256]{1,0:T(8,128)(2,1)S(1)} %shard_map.198), channel_id=1, source_target_pairs={{0,1},{1,0},{2,3},{3,2},{4,5},{5,4},{6,7},{7,6},{8,9},{9,8},{10,11... | collective-permute-start | bytes 1966088 | tf_op jit(solution)/shard_map/ppermute | solution.py:437
  59.1 5.6 %collective-permute-start.16 = (bf16[256,256]{1,0:T(8,128)(2,1)S(1)}, bf16[256,256]{1,0:T(8,128)(2,1)S(1)}, u32[]{:S(2)}, u32[]{:S(2)}) collective-permute-start(bf16[256,256]{1,0:T(8,128)(2,1)S(1)} %get-tuple-element.96), channel_id=1, source_target_pairs={{0,2},{1,3},{2,0},{3,1},{4,6},{5,7},{6,4},{7,5},{8,10},{9,11},{10,... | collective-permute-start | bytes 393224 | tf_op jit(solution)/shard_map/ppermute | solution.py:449
  59.1 9.0 %collective-permute-start.19 = (bf16[256,256]{1,0:T(8,128)(2,1)S(1)}, bf16[256,256]{1,0:T(8,128)(2,1)S(1)}, u32[]{:S(2)}, u32[]{:S(2)}) collective-permute-start(bf16[256,256]{1,0:T(8,128)(2,1)S(1)} %get-tuple-element.101), channel_id=1, source_target_pairs={{1,2},{3,4},{5,6},{7,8},{9,10},{11,12},{13,14},{15,16},{17,18},{19... | collective-permute-start | bytes 393224 | tf_op jit(solution)/shard_map/ppermute | solution.py:441
  59.8 13.3 %collective-permute-start.18 = (bf16[256,256]{1,0:T(8,128)(2,1)S(1)}, bf16[256,256]{1,0:T(8,128)(2,1)S(1)}, u32[]{:S(2)}, u32[]{:S(2)}) collective-permute-start(bf16[256,256]{1,0:T(8,128)(2,1)S(1)} %get-tuple-element.100), channel_id=1, source_target_pairs={{0,2},{1,3},{2,0},{3,1},{4,6},{5,7},{6,4},{7,5},{8,10},{9,11},{10,... | collective-permute-start | bytes 393224 | tf_op jit(solution)/shard_map/ppermute | solution.py:449
  64.7 8.4 %collective-permute-start.17 = (bf16[256,256]{1,0:T(8,128)(2,1)S(1)}, bf16[256,256]{1,0:T(8,128)(2,1)S(1)}, u32[]{:S(2)}, u32[]{:S(2)}) collective-permute-start(bf16[256,256]{1,0:T(8,128)(2,1)S(1)} %shard_map.200), channel_id=1, source_target_pairs={{0,4},{1,5},{2,6},{3,7},{4,0},{5,1},{6,2},{7,3},{8,12},{9,13},{10,... | collective-permute-start | bytes 393224 | tf_op jit(solution)/shard_map/ppermute | solution.py:434

commit v3 on v2

--- a/solution.py
+++ b/solution.py
@@ -452,12 +452,12 @@
         sent = to_core(couple(1, masked, coeffs, heights, BF16, pair))
         kept = couple(0, masked, coeffs, heights, F32)
         own, direct, passed, keep = chip_sum(kept, sent, heights)
-        own, cross = lax.optimization_barrier((own, cross))
-        return own, to_partner(passed), to_partner(direct), keep, [sent, to_chip(cross)]
-
-    def second_step(own, came, direct, keep, edges):
+        return own, to_partner(passed), to_partner(direct), keep, sent, cross
+
+    def second_step(own, came, direct, keep, sent, cross):
         sums = call(pair_sum_kernel, [jax.ShapeDtypeStruct((share, ens), BF16)] * (heights // 2 - 1), keep, came)
-        return [to_height(part, 2 * (d + 1)) for d, part in enumerate(sums)] + [own, direct] + edges
+        sums, cross = lax.optimization_barrier((sums, cross))
+        return [to_height(part, 2 * (d + 1)) for d, part in enumerate(sums)] + [own, direct, sent, to_chip(cross)]
 
     def row_coeffs(coeff):
         return [coeff] + [to_row(coeff, d) for d in range(1, row_count)]
@@ -507,7 +507,7 @@
         side_by_side_kernel, jax.ShapeDtypeStruct((heights * size, 2 * ens), BF16), *fields
     )
     other = to_core(own)
-    own_part, came, direct, keep, edges = first_step(coeffs, pair, cross)
+    own_part, came, direct, keep, sent, cross = first_step(coeffs, pair, cross)
     numbers, high, near, state = call(
         functools.partial(weights_kernel, heights, size, start),
         [jax.ShapeDtypeStruct((patches, 8), F32), part, jax.ShapeDtypeStruct(near_blocks.shape, BF16), full],
@@ -518,7 +518,7 @@
         scratch_shapes=scratch,
     )
     came, high = lax.optimization_barrier((came, high))
-    outer = second_step(own_part, came, direct, keep, edges)
+    outer = second_step(own_part, came, direct, keep, sent, cross)
     shift, scale, rest, scale_mid = call(
         prepare_first_kernel, [full] * 4, low, high, own, other, slip, state, numbers, near, rounded
     )

time: 76.1 us -> 76.9 us (1.011)
  the two profiles are of different devices: /device:TPU:0 before, /device:TPU:1 now
where the time goes in v3:
time: 76.9 us; the launch traced here: 76.5 us
  starting transfers between devices  32.7 us (43%)
  Pallas kernels  26.6 us (35%)
  waiting for transfers between devices  13.1 us (17%)
  other arithmetic  3.13 us (4%)
  between operations  0.9 us (1%)
    pallas_call x17, Pallas kernels, call(): pl.pallas_call(kernel, in_specs=specs or [VMEM] * len(operands), out_shap...  26.6 us
    ppermute x2, starting transfers between devices, to_chip(): return lax.ppermute(array, both, ends + [(j, i) for i, j in ends])  10.1 us
    ppermute x5, starting transfers between devices, to_height(): return lax.ppermute(array, 'col', pairs)  7.07 us
    ppermute x3, starting transfers between devices, to_core(): lax.ppermute(array, 'col', [(2 * z + k, 2 * z + 1 - k) for z in range(hei...  6.5 us
    ppermute x6, waiting for transfers between devices, to_row(): lax.ppermute(array, 'row', [(i, (i + d) % row_count) for i in range(row_c...  5.86 us
    ppermute x6, starting transfers between devices, to_row(): lax.ppermute(array, 'row', [(i, (i + d) % row_count) for i in range(row_c...  5.14 us
    ppermute x4, starting transfers between devices, to_partner(): return lax.ppermute(array, 'col', pairs)  3.87 us
    ppermute x4, waiting for transfers between devices, to_partner(): return lax.ppermute(array, 'col', pairs)  3.25 us
  transfers between devices with their start and end apart: 20, of which 7 were waited for; matrix products, arithmetic and copies ran while one was open for 4% of the time, Pallas kernels for 25%

profile of v3, /device:TPU:1, one launch (start us, length us, event | category | flops | bytes accessed | tf_op | source)
XLA Modules:
  0.0 76.5 jit_solution(79072579014238121)
XLA Ops:
  0.6 1.0 %shard_map.185 = (f32[4,64,256]{2,1,0:T(8,128)S(1)}, bf16[128,512]{1,0:T(8,128)(2,1)S(1)}) custom-call(s32[4,8,64]{2,1,0:T(8,128)} %bitcast.28, bf16[128,256]{1,0:T(8,128)(2,1)} %now_hbm.1, bf16[128,256]{1,0:T(8,128)(2,1)} %rate_hbm.1), custom_call_target="tpu_custom_call" | custom-call | tf_op jit(solution)/shard_map/pallas_call | solution.py:32
  1.6 4.2 %collective-permute-start.2 = (bf16[128,512]{1,0:T(8,128)(2,1)S(1)}, bf16[128,512]{1,0:T(8,128)(2,1)S(1)}, u32[]{:S(2)}, u32[]{:S(2)}) collective-permute-start(bf16[128,512]{1,0:T(8,128)(2,1)S(1)} %get-tuple-element.71.refs_0_), channel_id=1, source_target_pairs={{0,6},{1,7},{2,0},{3,1},{4,2},{5,3},{6,4},{7,5},{8,14},{9,15},{10,... | collective-permute-start | bytes 393224 | tf_op jit(solution)/shard_map/ppermute | solution.py:434
  5.8 0.5 collective-permute-start
  6.3 0.1 lt.21
  6.4 3.1 %fusion.matrix_ref = bf16[4,2048,256]{2,1,0:T(8,128)(2,1)S(1)} fusion(bf16[2048,4,256]{2,1,0:T(4,128)(2,1)} %param.29, f32[4,64,256]{2,1,0:T(8,128)S(1)} %get-tuple-element.52, f32[2048]{0:T(1024)S(1)} %lt.21), kind=kLoop, calls=%fused_computation.1 | loop fusion | flops 4194304 | bytes 8658944 | tf_op jit(solution)/shard_map/jit(_where)/select_n | solution.py:396
  9.5 2.4 %shard_map.186 = (bf16[256,256]{1,0:T(8,128)(2,1)S(1)}, bf16[2048,256]{1,0:T(8,128)(2,1)S(1)}, bf16[256,256]{1,0:T(8,128)(2,1)S(1)}, bf16[256,256]{1,0:T(8,128)(2,1)S(1)}, f32[2048,256]{1,0:T(8,128)S(1)}) custom-call(f32[2048,256]{1,0:T(8,128)} %slip_hbm, bf16[32,2048]{1,0:T(8,128)(2,1)} %basis_in_ref.1), custom_call_target="tpu_custom_call" | custom-call | tf_op jit(solution)/shard_map/pallas_call | solution.py:32
  11.9 2.2 %collective-permute-start.5 = (bf16[256,256]{1,0:T(8,128)(2,1)S(1)}, bf16[256,256]{1,0:T(8,128)(2,1)S(1)}, u32[]{:S(2)}, u32[]{:S(2)}) collective-permute-start(bf16[256,256]{1,0:T(8,128)(2,1)S(1)} %get-tuple-element.60.refs_9_.refs_0_), channel_id=1, source_target_pairs={{0,24},{8,0},{16,8},{24,16},{1,25},{9,1},{17,9},{25,17},{2,26},{10... | collective-permute-start | bytes 393224 | tf_op jit(solution)/shard_map/ppermute | solution.py:430
  14.1 0.2 collective-permute-start.4
  14.3 0.0 collective-permute-done.2.refs_3_
  14.3 0.3 collective-permute-start.3
  14.6 3.7 %shard_map.187 = (f32[1024,8]{1,0:T(8,128)S(1)}, bf16[1024,1024]{1,0:T(8,128)(2,1)S(1)}) custom-call(f32[1,2048]{1,0:T(1,128)} %bitcast.14, f32[1,2048]{1,0:T(1,128)} %bitcast.16, f32[1,2048]{1,0:T(1,128)} %bitcast.18, f32[1,2048]{1,0:T(1,128)} %bitcast.20, f32[1,2048]{1,0:T(1,128)} %bitcast.22, f32[1,2048]{1,0:T(1,128)} %bitcast.24, s32[1,2048]{1,0:T(1,128)} %bitcast.26, ...), custom_call_target="tpu_custom_call" | custom-call | tf_op jit(solution)/shard_map/pallas_call | solution.py:32
  18.3 0.0 collective-permute-done.1.refs_2_
  18.3 0.0 collective-permute-done.5.refs_3_
  18.4 1.7 %collective-permute-done.3.refs_1_ = bf16[256,256]{1,0:T(8,128)(2,1)S(1)} collective-permute-done((bf16[256,256]{1,0:T(8,128)(2,1)S(1)}, bf16[256,256]{1,0:T(8,128)(2,1)S(1)}, u32[]{:S(2)}, u32[]{:S(2)}) %collective-permute-start.3) | collective-permute-done | bytes 131104 | tf_op jit(solution)/shard_map/ppermute | solution.py:430
  20.1 0.7 shard_map.189
  20.8 3.0 %collective-permute-start.6 = (bf16[1280,256]{1,0:T(8,128)(2,1)S(1)}, bf16[1280,256]{1,0:T(8,128)(2,1)S(1)}, u32[]{:S(2)}, u32[]{:S(2)}) collective-permute-start(bf16[1280,256]{1,0:T(8,128)(2,1)S(1)} %shard_map.189), channel_id=1, source_target_pairs={{0,1},{1,0},{2,3},{3,2},{4,5},{5,4},{6,7},{7,6},{8,9},{9,8},{10,11... | collective-permute-start | bytes 1966088 | tf_op jit(solution)/shard_map/ppermute | solution.py:437
  23.9 0.1 collective-permute-start.8
  24.0 0.7 shard_map.188.kept_ref
  24.7 0.9 %collective-permute-done.6.sent_ref.refs_3_ = bf16[1280,256]{1,0:T(8,128)(2,1)S(1)} collective-permute-done((bf16[1280,256]{1,0:T(8,128)(2,1)S(1)}, bf16[1280,256]{1,0:T(8,128)(2,1)S(1)}, u32[]{:S(2)}, u32[]{:S(2)}) %collective-permute-start.6) | collective-permute-done | bytes 655392 | tf_op jit(solution)/shard_map/ppermute | solution.py:437
  25.6 0.3 shard_map.190
  25.8 2.3 %collective-permute-start.7 = (bf16[256,256]{1,0:T(8,128)(2,1)S(1)}, bf16[256,256]{1,0:T(8,128)(2,1)S(1)}, u32[]{:S(2)}, u32[]{:S(2)}) collective-permute-start(bf16[256,256]{1,0:T(8,128)(2,1)S(1)} %get-tuple-element.68), channel_id=1, source_target_pairs={{0,2},{1,3},{2,0},{3,1},{4,6},{5,7},{6,4},{7,5},{8,10},{9,11},{10,... | collective-permute-start | bytes 393224 | tf_op jit(solution)/shard_map/ppermute | solution.py:449
  28.1 0.1 collective-permute-start.10
  28.2 3.7 %shard_map.191 = (f32[2048,8]{1,0:T(8,128)S(1)}, bf16[1024,1024]{1,0:T(8,128)(2,1)S(1)}, bf16[3,2048,256]{2,1,0:T(8,128)(2,1)S(1)}, f32[2048,256]{1,0:T(8,128)S(1)}) custom-call(f32[1,2048]{1,0:T(1,128)} %bitcast.15, f32[1,2048]{1,0:T(1,128)} %bitcast.17, f32[1,2048]{1,0:T(1,128)} %bitcast.19, f32[1,2048]{1,0:T(1,128)} %bitcast.21, f32[1,2048]{1,0:T(1,128)} %bitcast.23, ...), custom_call_target="tpu_custom_call" | custom-call | tf_op jit(solution)/shard_map/pallas_call | solution.py:32
  31.9 0.1 shard_map.194
  31.9 1.1 %collective-permute-start.9 = (bf16[256,256]{1,0:T(8,128)(2,1)S(1)}, bf16[256,256]{1,0:T(8,128)(2,1)S(1)}, u32[]{:S(2)}, u32[]{:S(2)}) collective-permute-start(bf16[256,256]{1,0:T(8,128)(2,1)S(1)} %shard_map.194), channel_id=1, source_target_pairs={{0,4},{1,5},{2,6},{3,7},{4,0},{5,1},{6,2},{7,3},{8,12},{9,13},{10,... | collective-permute-start | bytes 393224 | tf_op jit(solution)/shard_map/ppermute | solution.py:434
  33.0 4.8 %collective-permute-start.11 = (bf16[256,256]{1,0:T(8,128)(2,1)S(1)}, bf16[256,256]{1,0:T(8,128)(2,1)S(1)}, u32[]{:S(2)}, u32[]{:S(2)}) collective-permute-start(bf16[256,256]{1,0:T(8,128)(2,1)S(1)} %get-tuple-element.85), channel_id=1, source_target_pairs={{1,2},{3,4},{5,6},{7,8},{9,10},{11,12},{13,14},{15,16},{17,18},{19... | collective-permute-start | bytes 393224 | tf_op jit(solution)/shard_map/ppermute | solution.py:441
  37.8 0.0 copy-start
  37.8 0.0 copy-start.1
  37.8 4.9 %shard_map.193 = (f32[2048,256]{1,0:T(8,128)S(1)}, f32[2048,256]{1,0:T(8,128)S(1)}, f32[2048,256]{1,0:T(8,128)S(1)}, f32[2048,256]{1,0:T(8,128)S(1)}) custom-call(bf16[1024,1024]{1,0:T(8,128)(2,1)S(1)} %get-tuple-element.67.low_ref, bf16[1024,1024]{1,0:T(8,128)(2,1)S(1)} %get-tuple-element.70.high_ref, bf16[512,512]{1,0:T(8,128)(2,1)S(1)} %shard_map.192.own_ref, ...), custom_call_target="tpu_custom_call" | custom-call | tf_op jit(solution)/shard_map/pallas_call | solution.py:32
  42.8 1.9 %shard_map.195 = (f32[2048,256]{1,0:T(8,128)S(1)}, bf16[2048,256]{1,0:T(8,128)(2,1)S(1)}, bf16[256,256]{1,0:T(8,128)(2,1)S(1)}, bf16[256,256]{1,0:T(8,128)(2,1)S(1)}, bf16[256,256]{1,0:T(8,128)(2,1)S(1)}) custom-call(f32[2048,256]{1,0:T(8,128)S(1)} %get-tuple-element.78.shift_ref, f32[2048,256]{1,0:T(8,128)S(1)} %get-tuple-element.79.scale_ref, ...), custom_call_target="tpu_custom_call" | custom-call | tf_op jit(solution)/shard_map/pallas_call | solution.py:32
  44.7 0.1 collective-permute-start.14
  44.8 1.0 %collective-permute-start.13 = (bf16[256,256]{1,0:T(8,128)(2,1)S(1)}, bf16[256,256]{1,0:T(8,128)(2,1)S(1)}, u32[]{:S(2)}, u32[]{:S(2)}) collective-permute-start(bf16[256,256]{1,0:T(8,128)(2,1)S(1)} %get-tuple-element.93.refs_0_), channel_id=1, source_target_pairs={{0,16},{8,24},{16,0},{24,8},{1,17},{9,25},{17,1},{25,9},{2,18},{10... | collective-permute-start | bytes 393224 | tf_op jit(solution)/shard_map/ppermute | solution.py:430
  45.8 1.3 %collective-permute-start.12 = (bf16[256,256]{1,0:T(8,128)(2,1)S(1)}, bf16[256,256]{1,0:T(8,128)(2,1)S(1)}, u32[]{:S(2)}, u32[]{:S(2)}) collective-permute-start(bf16[256,256]{1,0:T(8,128)(2,1)S(1)} %get-tuple-element.93.refs_0_), channel_id=1, source_target_pairs={{0,8},{8,16},{16,24},{24,0},{1,9},{9,17},{17,25},{25,1},{2,10},{10... | collective-permute-start | bytes 393224 | tf_op jit(solution)/shard_map/ppermute | solution.py:430
  47.0 2.2 %collective-permute-done.14.refs_3_ = bf16[256,256]{1,0:T(8,128)(2,1)S(1)} collective-permute-done((bf16[256,256]{1,0:T(8,128)(2,1)S(1)}, bf16[256,256]{1,0:T(8,128)(2,1)S(1)}, u32[]{:S(2)}, u32[]{:S(2)}) %collective-permute-start.14) | collective-permute-done | bytes 131104 | tf_op jit(solution)/shard_map/ppermute | solution.py:430
  49.3 1.9 %collective-permute-done.12.refs_1_ = bf16[256,256]{1,0:T(8,128)(2,1)S(1)} collective-permute-done((bf16[256,256]{1,0:T(8,128)(2,1)S(1)}, bf16[256,256]{1,0:T(8,128)(2,1)S(1)}, u32[]{:S(2)}, u32[]{:S(2)}) %collective-permute-start.12) | collective-permute-done | bytes 131104 | tf_op jit(solution)/shard_map/ppermute | solution.py:430
  51.1 0.7 shard_map.198
  51.9 3.4 %collective-permute-start.15 = (bf16[1280,256]{1,0:T(8,128)(2,1)S(1)}, bf16[1280,256]{1,0:T(8,128)(2,1)S(1)}, u32[]{:S(2)}, u32[]{:S(2)}) collective-permute-start(bf16[1280,256]{1,0:T(8,128)(2,1)S(1)} %shard_map.198), channel_id=1, source_target_pairs={{0,1},{1,0},{2,3},{3,2},{4,5},{5,4},{6,7},{7,6},{8,9},{9,8},{10,11... | collective-permute-start | bytes 1966088 | tf_op jit(solution)/shard_map/ppermute | solution.py:437
  55.3 0.7 shard_map.197.kept_ref
  56.0 1.0 %collective-permute-done.15.sent_ref.refs_3_ = bf16[1280,256]{1,0:T(8,128)(2,1)S(1)} collective-permute-done((bf16[1280,256]{1,0:T(8,128)(2,1)S(1)}, bf16[1280,256]{1,0:T(8,128)(2,1)S(1)}, u32[]{:S(2)}, u32[]{:S(2)}) %collective-permute-start.15) | collective-permute-done | bytes 655392 | tf_op jit(solution)/shard_map/ppermute | solution.py:437
  57.0 0.3 shard_map.199
  57.2 0.2 collective-permute-start.16
  57.5 1.3 %collective-permute-start.18 = (bf16[256,256]{1,0:T(8,128)(2,1)S(1)}, bf16[256,256]{1,0:T(8,128)(2,1)S(1)}, u32[]{:S(2)}, u32[]{:S(2)}) collective-permute-start(bf16[256,256]{1,0:T(8,128)(2,1)S(1)} %get-tuple-element.100), channel_id=1, source_target_pairs={{0,2},{1,3},{2,0},{3,1},{4,6},{5,7},{6,4},{7,5},{8,10},{9,11},{10,... | collective-permute-start | bytes 393224 | tf_op jit(solution)/shard_map/ppermute | solution.py:449
  58.8 3.2 %collective-permute-done.16.came_ref = bf16[256,256]{1,0:T(8,128)(2,1)S(1)} collective-permute-done((bf16[256,256]{1,0:T(8,128)(2,1)S(1)}, bf16[256,256]{1,0:T(8,128)(2,1)S(1)}, u32[]{:S(2)}, u32[]{:S(2)}) %collective-permute-start.16) | collective-permute-done | bytes 131104 | tf_op jit(solution)/shard_map/ppermute | solution.py:449
  62.1 1.3 %collective-permute-start.17 = (bf16[256,256]{1,0:T(8,128)(2,1)S(1)}, bf16[256,256]{1,0:T(8,128)(2,1)S(1)}, u32[]{:S(2)}, u32[]{:S(2)}) collective-permute-start(bf16[256,256]{1,0:T(8,128)(2,1)S(1)} %shard_map.200), channel_id=1, source_target_pairs={{0,4},{1,5},{2,6},{3,7},{4,0},{5,1},{6,2},{7,3},{8,12},{9,13},{10,... | collective-permute-start | bytes 393224 | tf_op jit(solution)/shard_map/ppermute | solution.py:434
  63.4 5.4 %collective-permute-start.19 = (bf16[256,256]{1,0:T(8,128)(2,1)S(1)}, bf16[256,256]{1,0:T(8,128)(2,1)S(1)}, u32[]{:S(2)}, u32[]{:S(2)}) collective-permute-start(bf16[256,256]{1,0:T(8,128)(2,1)S(1)} %get-tuple-element.101), channel_id=1, source_target_pairs={{1,2},{3,4},{5,6},{7,8},{9,10},{11,12},{13,14},{15,16},{17,18},{19... | collective-permute-start | bytes 393224 | tf_op jit(solution)/shard_map/ppermute | solution.py:441
  68.8 3.0 %shard_map.196 = (f32[2048,256]{1,0:T(8,128)S(1)}, f32[2048,256]{1,0:T(8,128)S(1)}, f32[2048,256]{1,0:T(8,128)S(1)}) custom-call(f32[2048,256]{1,0:T(8,128)S(1)} %get-tuple-element.54.slip_ref, f32[2048,256]{1,0:T(8,128)S(1)} %get-tuple-element.66.state_ref, f32[2048,256]{1,0:T(8,128)S(1)} %get-tuple-element.86.speed_ref, ...), custom_call_target="tpu_custom_call" | custom-call | tf_op jit(solution)/shard_map/pallas_call | solution.py:32
  71.9 2.0 %collective-permute-done.19.refs_4_ = bf16[256,256]{1,0:T(8,128)(2,1)S(1)} collective-permute-done((bf16[256,256]{1,0:T(8,128)(2,1)S(1)}, bf16[256,256]{1,0:T(8,128)(2,1)S(1)}, u32[]{:S(2)}, u32[]{:S(2)}) %collective-permute-start.19) | collective-permute-done | bytes 131104 | tf_op jit(solution)/shard_map/ppermute | solution.py:441
  73.9 2.6 %shard_map.201 = (f32[2048,256]{1,0:T(8,128)}, f32[2048,256]{1,0:T(8,128)}) custom-call(f32[2048,256]{1,0:T(8,128)S(1)} %get-tuple-element.90.shift_ref, f32[2048,256]{1,0:T(8,128)S(1)} %get-tuple-element.88.scale_ref, f32[2048,256]{1,0:T(8,128)S(1)} %get-tuple-element.91.rest_ref, f32[2048,256]{1,0:T(8,128)S(1)} %get-tuple-element.92.slip_rest_ref, ...), custom_call_target="tpu_custom_call" | custom-call | tf_op jit(solution)/shard_map/pallas_call | solution.py:32
  (17 shorter events, 0.1 us)
Async XLA Ops:
  1.6 12.7 %collective-permute-start.2 = (bf16[128,512]{1,0:T(8,128)(2,1)S(1)}, bf16[128,512]{1,0:T(8,128)(2,1)S(1)}, u32[]{:S(2)}, u32[]{:S(2)}) collective-permute-start(bf16[128,512]{1,0:T(8,128)(2,1)S(1)} %get-tuple-element.71.refs_0_), channel_id=1, source_target_pairs={{0,6},{1,7},{2,0},{3,1},{4,2},{5,3},{6,4},{7,5},{8,14},{9,15},{10,... | collective-permute-start | bytes 393224 | tf_op jit(solution)/shard_map/ppermute | solution.py:434
  5.8 12.5 %collective-permute-start.1 = (bf16[128,512]{1,0:T(8,128)(2,1)S(1)}, bf16[128,512]{1,0:T(8,128)(2,1)S(1)}, u32[]{:S(2)}, u32[]{:S(2)}) collective-permute-start(bf16[128,512]{1,0:T(8,128)(2,1)S(1)} %get-tuple-element.71.refs_0_), channel_id=1, source_target_pairs={{0,4},{1,5},{2,6},{3,7},{4,0},{5,1},{6,2},{7,3},{8,12},{9,13},{10,... | collective-permute-start | bytes 393224 | tf_op jit(solution)/shard_map/ppermute | solution.py:434
  5.8 12.5 %collective-permute-start = (bf16[128,512]{1,0:T(8,128)(2,1)S(1)}, bf16[128,512]{1,0:T(8,128)(2,1)S(1)}, u32[]{:S(2)}, u32[]{:S(2)}) collective-permute-start(bf16[128,512]{1,0:T(8,128)(2,1)S(1)} %get-tuple-element.71.refs_0_), channel_id=1, source_target_pairs={{0,2},{1,3},{2,4},{3,5},{4,6},{5,7},{6,0},{7,1},{8,10},{9,11},{10,... | collective-permute-start | bytes 393224 | tf_op jit(solution)/shard_map/ppermute | solution.py:434
  11.9 6.5 %collective-permute-start.5 = (bf16[256,256]{1,0:T(8,128)(2,1)S(1)}, bf16[256,256]{1,0:T(8,128)(2,1)S(1)}, u32[]{:S(2)}, u32[]{:S(2)}) collective-permute-start(bf16[256,256]{1,0:T(8,128)(2,1)S(1)} %get-tuple-element.60.refs_9_.refs_0_), channel_id=1, source_target_pairs={{0,24},{8,0},{16,8},{24,16},{1,25},{9,1},{17,9},{25,17},{2,26},{10... | collective-permute-start | bytes 393224 | tf_op jit(solution)/shard_map/ppermute | solution.py:430
  14.1 4.3 %collective-permute-start.4 = (bf16[256,256]{1,0:T(8,128)(2,1)S(1)}, bf16[256,256]{1,0:T(8,128)(2,1)S(1)}, u32[]{:S(2)}, u32[]{:S(2)}) collective-permute-start(bf16[256,256]{1,0:T(8,128)(2,1)S(1)} %get-tuple-element.60.refs_9_.refs_0_), channel_id=1, source_target_pairs={{0,16},{8,24},{16,0},{24,8},{1,17},{9,25},{17,1},{25,9},{2,18},{10... | collective-permute-start | bytes 393224 | tf_op jit(solution)/shard_map/ppermute | solution.py:430
  14.3 5.8 %collective-permute-start.3 = (bf16[256,256]{1,0:T(8,128)(2,1)S(1)}, bf16[256,256]{1,0:T(8,128)(2,1)S(1)}, u32[]{:S(2)}, u32[]{:S(2)}) collective-permute-start(bf16[256,256]{1,0:T(8,128)(2,1)S(1)} %get-tuple-element.60.refs_9_.refs_0_), channel_id=1, source_target_pairs={{0,8},{8,16},{16,24},{24,0},{1,9},{9,17},{17,25},{25,1},{2,10},{10... | collective-permute-start | bytes 393224 | tf_op jit(solution)/shard_map/ppermute | solution.py:430
  20.8 4.7 %collective-permute-start.6 = (bf16[1280,256]{1,0:T(8,128)(2,1)S(1)}, bf16[1280,256]{1,0:T(8,128)(2,1)S(1)}, u32[]{:S(2)}, u32[]{:S(2)}) collective-permute-start(bf16[1280,256]{1,0:T(8,128)(2,1)S(1)} %shard_map.189), channel_id=1, source_target_pairs={{0,1},{1,0},{2,3},{3,2},{4,5},{5,4},{6,7},{7,6},{8,9},{9,8},{10,11... | collective-permute-start | bytes 1966088 | tf_op jit(solution)/shard_map/ppermute | solution.py:437
  23.9 13.9 %collective-permute-start.8 = (bf16[512,512]{1,0:T(8,128)(2,1)S(1)}, bf16[512,512]{1,0:T(8,128)(2,1)S(1)}, u32[]{:S(2)}, u32[]{:S(2)}) collective-permute-start(bf16[512,512]{1,0:T(8,128)(2,1)S(1)} %shard_map.192.own_ref), channel_id=1, source_target_pairs={{0,1},{1,0},{2,3},{3,2},{4,5},{5,4},{6,7},{7,6},{8,9},{9,8},{10,11... | collective-permute-start | bytes 1572872 | tf_op jit(solution)/shard_map/ppermute | solution.py:437
  25.8 6.0 %collective-permute-start.7 = (bf16[256,256]{1,0:T(8,128)(2,1)S(1)}, bf16[256,256]{1,0:T(8,128)(2,1)S(1)}, u32[]{:S(2)}, u32[]{:S(2)}) collective-permute-start(bf16[256,256]{1,0:T(8,128)(2,1)S(1)} %get-tuple-element.68), channel_id=1, source_target_pairs={{0,2},{1,3},{2,0},{3,1},{4,6},{5,7},{6,4},{7,5},{8,10},{9,11},{10,... | collective-permute-start | bytes 393224 | tf_op jit(solution)/shard_map/ppermute | solution.py:449
  28.1 14.7 %collective-permute-start.10 = (bf16[256,256]{1,0:T(8,128)(2,1)S(1)}, bf16[256,256]{1,0:T(8,128)(2,1)S(1)}, u32[]{:S(2)}, u32[]{:S(2)}) collective-permute-start(bf16[256,256]{1,0:T(8,128)(2,1)S(1)} %get-tuple-element.84), channel_id=1, source_target_pairs={{0,2},{1,3},{2,0},{3,1},{4,6},{5,7},{6,4},{7,5},{8,10},{9,11},{10,... | collective-permute-start | bytes 393224 | tf_op jit(solution)/shard_map/ppermute | solution.py:449
  31.9 10.8 %collective-permute-start.9 = (bf16[256,256]{1,0:T(8,128)(2,1)S(1)}, bf16[256,256]{1,0:T(8,128)(2,1)S(1)}, u32[]{:S(2)}, u32[]{:S(2)}) collective-permute-start(bf16[256,256]{1,0:T(8,128)(2,1)S(1)} %shard_map.194), channel_id=1, source_target_pairs={{0,4},{1,5},{2,6},{3,7},{4,0},{5,1},{6,2},{7,3},{8,12},{9,13},{10,... | collective-permute-start | bytes 393224 | tf_op jit(solution)/shard_map/ppermute | solution.py:434
  33.0 9.8 %collective-permute-start.11 = (bf16[256,256]{1,0:T(8,128)(2,1)S(1)}, bf16[256,256]{1,0:T(8,128)(2,1)S(1)}, u32[]{:S(2)}, u32[]{:S(2)}) collective-permute-start(bf16[256,256]{1,0:T(8,128)(2,1)S(1)} %get-tuple-element.85), channel_id=1, source_target_pairs={{1,2},{3,4},{5,6},{7,8},{9,10},{11,12},{13,14},{15,16},{17,18},{19... | collective-permute-start | bytes 393224 | tf_op jit(solution)/shard_map/ppermute | solution.py:441
  37.8 5.0 %copy-start = (bf16[32,2048]{1,0:T(8,128)(2,1)S(1)}, bf16[32,2048]{1,0:T(8,128)(2,1)}, u32[]{:S(2)}) copy-start(bf16[32,2048]{1,0:T(8,128)(2,1)} %basis_out_ref.3) | copy-start | bytes 393220
  37.8 5.0 %copy-start.1 = (bf16[32,2048]{1,0:T(8,128)(2,1)S(1)}, bf16[32,2048]{1,0:T(8,128)(2,1)}, u32[]{:S(2)}) copy-start(bf16[32,2048]{1,0:T(8,128)(2,1)} %basis_in_ref.1) | copy-start | bytes 393220
  44.7 4.6 %collective-permute-start.14 = (bf16[256,256]{1,0:T(8,128)(2,1)S(1)}, bf16[256,256]{1,0:T(8,128)(2,1)S(1)}, u32[]{:S(2)}, u32[]{:S(2)}) collective-permute-start(bf16[256,256]{1,0:T(8,128)(2,1)S(1)} %get-tuple-element.93.refs_0_), channel_id=1, source_target_pairs={{0,24},{8,0},{16,8},{24,16},{1,25},{9,1},{17,9},{25,17},{2,26},{10... | collective-permute-start | bytes 393224 | tf_op jit(solution)/shard_map/ppermute | solution.py:430
  44.8 4.5 %collective-permute-start.13 = (bf16[256,256]{1,0:T(8,128)(2,1)S(1)}, bf16[256,256]{1,0:T(8,128)(2,1)S(1)}, u32[]{:S(2)}, u32[]{:S(2)}) collective-permute-start(bf16[256,256]{1,0:T(8,128)(2,1)S(1)} %get-tuple-element.93.refs_0_), channel_id=1, source_target_pairs={{0,16},{8,24},{16,0},{24,8},{1,17},{9,25},{17,1},{25,9},{2,18},{10... | collective-permute-start | bytes 393224 | tf_op jit(solution)/shard_map/ppermute | solution.py:430
  45.8 5.4 %collective-permute-start.12 = (bf16[256,256]{1,0:T(8,128)(2,1)S(1)}, bf16[256,256]{1,0:T(8,128)(2,1)S(1)}, u32[]{:S(2)}, u32[]{:S(2)}) collective-permute-start(bf16[256,256]{1,0:T(8,128)(2,1)S(1)} %get-tuple-element.93.refs_0_), channel_id=1, source_target_pairs={{0,8},{8,16},{16,24},{24,0},{1,9},{9,17},{17,25},{25,1},{2,10},{10... | collective-permute-start | bytes 393224 | tf_op jit(solution)/shard_map/ppermute | solution.py:430
  51.9 5.1 %collective-permute-start.15 = (bf16[1280,256]{1,0:T(8,128)(2,1)S(1)}, bf16[1280,256]{1,0:T(8,128)(2,1)S(1)}, u32[]{:S(2)}, u32[]{:S(2)}) collective-permute-start(bf16[1280,256]{1,0:T(8,128)(2,1)S(1)} %shard_map.198), channel_id=1, source_target_pairs={{0,1},{1,0},{2,3},{3,2},{4,5},{5,4},{6,7},{7,6},{8,9},{9,8},{10,11... | collective-permute-start | bytes 1966088 | tf_op jit(solution)/shard_map/ppermute | solution.py:437
  57.2 4.8 %collective-permute-start.16 = (bf16[256,256]{1,0:T(8,128)(2,1)S(1)}, bf16[256,256]{1,0:T(8,128)(2,1)S(1)}, u32[]{:S(2)}, u32[]{:S(2)}) collective-permute-start(bf16[256,256]{1,0:T(8,128)(2,1)S(1)} %get-tuple-element.96), channel_id=1, source_target_pairs={{0,2},{1,3},{2,0},{3,1},{4,6},{5,7},{6,4},{7,5},{8,10},{9,11},{10,... | collective-permute-start | bytes 393224 | tf_op jit(solution)/shard_map/ppermute | solution.py:449
  57.5 14.3 %collective-permute-start.18 = (bf16[256,256]{1,0:T(8,128)(2,1)S(1)}, bf16[256,256]{1,0:T(8,128)(2,1)S(1)}, u32[]{:S(2)}, u32[]{:S(2)}) collective-permute-start(bf16[256,256]{1,0:T(8,128)(2,1)S(1)} %get-tuple-element.100), channel_id=1, source_target_pairs={{0,2},{1,3},{2,0},{3,1},{4,6},{5,7},{6,4},{7,5},{8,10},{9,11},{10,... | collective-permute-start | bytes 393224 | tf_op jit(solution)/shard_map/ppermute | solution.py:449
  62.1 9.8 %collective-permute-start.17 = (bf16[256,256]{1,0:T(8,128)(2,1)S(1)}, bf16[256,256]{1,0:T(8,128)(2,1)S(1)}, u32[]{:S(2)}, u32[]{:S(2)}) collective-permute-start(bf16[256,256]{1,0:T(8,128)(2,1)S(1)} %shard_map.200), channel_id=1, source_target_pairs={{0,4},{1,5},{2,6},{3,7},{4,0},{5,1},{6,2},{7,3},{8,12},{9,13},{10,... | collective-permute-start | bytes 393224 | tf_op jit(solution)/shard_map/ppermute | solution.py:434
  63.4 10.5 %collective-permute-start.19 = (bf16[256,256]{1,0:T(8,128)(2,1)S(1)}, bf16[256,256]{1,0:T(8,128)(2,1)S(1)}, u32[]{:S(2)}, u32[]{:S(2)}) collective-permute-start(bf16[256,256]{1,0:T(8,128)(2,1)S(1)} %get-tuple-element.101), channel_id=1, source_target_pairs={{1,2},{3,4},{5,6},{7,8},{9,10},{11,12},{13,14},{15,16},{17,18},{19... | collective-permute-start | bytes 393224 | tf_op jit(solution)/shard_map/ppermute | solution.py:441

commit v4 on v3

--- a/solution.py
+++ b/solution.py
@@ -448,16 +448,20 @@
         pairs = [(2 * z + k, 2 * (z + 1 - 2 * (z % 2)) + k) for z in range(heights) for k in range(2)]
         return lax.ppermute(array, "col", pairs)
 
-    def first_step(coeffs, pair, cross):
+    def first_step(coeffs, pair, cross, later):
         sent = to_core(couple(1, masked, coeffs, heights, BF16, pair))
         kept = couple(0, masked, coeffs, heights, F32)
         own, direct, passed, keep = chip_sum(kept, sent, heights)
-        return own, to_partner(passed), to_partner(direct), keep, sent, cross
-
-    def second_step(own, came, direct, keep, sent, cross):
+        if not later:
+            own, cross = lax.optimization_barrier((own, cross))
+        return own, to_partner(passed), to_partner(direct), keep, sent, cross if later else to_chip(cross)
+
+    def second_step(own, came, direct, keep, sent, cross, later):
         sums = call(pair_sum_kernel, [jax.ShapeDtypeStruct((share, ens), BF16)] * (heights // 2 - 1), keep, came)
-        sums, cross = lax.optimization_barrier((sums, cross))
-        return [to_height(part, 2 * (d + 1)) for d, part in enumerate(sums)] + [own, direct, sent, to_chip(cross)]
+        if later:
+            sums, cross = lax.optimization_barrier((sums, cross))
+            cross = to_chip(cross)
+        return [to_height(part, 2 * (d + 1)) for d, part in enumerate(sums)] + [own, direct, sent, cross]
 
     def row_coeffs(coeff):
         return [coeff] + [to_row(coeff, d) for d in range(1, row_count)]
@@ -507,7 +511,7 @@
         side_by_side_kernel, jax.ShapeDtypeStruct((heights * size, 2 * ens), BF16), *fields
     )
     other = to_core(own)
-    own_part, came, direct, keep, sent, cross = first_step(coeffs, pair, cross)
+    own_part, came, direct, keep, sent, cross = first_step(coeffs, pair, cross, True)
     numbers, high, near, state = call(
         functools.partial(weights_kernel, heights, size, start),
         [jax.ShapeDtypeStruct((patches, 8), F32), part, jax.ShapeDtypeStruct(near_blocks.shape, BF16), full],
@@ -518,7 +522,7 @@
         scratch_shapes=scratch,
     )
     came, high = lax.optimization_barrier((came, high))
-    outer = second_step(own_part, came, direct, keep, sent, cross)
+    outer = second_step(own_part, came, direct, keep, sent, cross, True)
     shift, scale, rest, scale_mid = call(
         prepare_first_kernel, [full] * 4, low, high, own, other, slip, state, numbers, near, rounded
     )
@@ -528,7 +532,7 @@
         shift, scale, slip, basis_out, basis_in, near, *outer,
     )
     coeffs = row_coeffs(coeff)
-    outer = second_step(*first_step(coeffs, pair, cross))
+    outer = second_step(*first_step(coeffs, pair, cross, False), False)
     shift, slip_rest, rest = call(
         prepare_second_kernel, [full] * 3,
         slip, state, speed, rest, scale_mid, numbers, near, rounded,

time: 76.9 us -> 74.6 us (0.970)
  the two profiles are of different devices: /device:TPU:1 before, /device:TPU:0 now
where the time goes in v4:
time: 74.6 us; the launch traced here: 74.2 us
  Pallas kernels  26.6 us (36%)
  starting transfers between devices  26.3 us (35%)
  waiting for transfers between devices  17.2 us (23%)
  other arithmetic  3.13 us (4%)
  between operations  0.87 us (1%)
    pallas_call x17, Pallas kernels, call(): pl.pallas_call(kernel, in_specs=specs or [VMEM] * len(operands), out_shap...  26.6 us
    ppermute x5, starting transfers between devices, to_height(): return lax.ppermute(array, 'col', pairs)  9.3 us
    ppermute x6, starting transfers between devices, to_row(): lax.ppermute(array, 'row', [(i, (i + d) % row_count) for i in range(row_c...  8.97 us
    ppermute x6, waiting for transfers between devices, to_row(): lax.ppermute(array, 'row', [(i, (i + d) % row_count) for i in range(row_c...  7.3 us
    ppermute x4, starting transfers between devices, to_partner(): return lax.ppermute(array, 'col', pairs)  6.02 us
    ppermute x4, waiting for transfers between devices, to_partner(): return lax.ppermute(array, 'col', pairs)  5.9 us
    select_n x1, other arithmetic, masked_coupling(): jnp.where(keep, matrix, jnp.zeros((), BF16)).reshape(sources, rows, width)  3.13 us
    ppermute x3, waiting for transfers between devices, to_core(): lax.ppermute(array, 'col', [(2 * z + k, 2 * z + 1 - k) for z in range(hei...  2.16 us
  transfers between devices with their start and end apart: 20, of which 10 were waited for; matrix products, arithmetic and copies ran while one was open for 4% of the time, Pallas kernels for 26%

profile of v4, /device:TPU:0, one launch (start us, length us, event | category | flops | bytes accessed | tf_op | source)
XLA Modules:
  0.0 74.2 jit_solution(8154767838953340834)
XLA Ops:
  0.6 1.0 %shard_map.185 = (f32[4,64,256]{2,1,0:T(8,128)S(1)}, bf16[128,512]{1,0:T(8,128)(2,1)S(1)}) custom-call(s32[4,8,64]{2,1,0:T(8,128)} %bitcast.28, bf16[128,256]{1,0:T(8,128)(2,1)} %now_hbm.1, bf16[128,256]{1,0:T(8,128)(2,1)} %rate_hbm.1), custom_call_target="tpu_custom_call" | custom-call | tf_op jit(solution)/shard_map/pallas_call | solution.py:32
  1.6 5.1 %collective-permute-start.2 = (bf16[128,512]{1,0:T(8,128)(2,1)S(1)}, bf16[128,512]{1,0:T(8,128)(2,1)S(1)}, u32[]{:S(2)}, u32[]{:S(2)}) collective-permute-start(bf16[128,512]{1,0:T(8,128)(2,1)S(1)} %get-tuple-element.71.refs_0_), channel_id=1, source_target_pairs={{0,6},{1,7},{2,0},{3,1},{4,2},{5,3},{6,4},{7,5},{8,14},{9,15},{10,... | collective-permute-start | bytes 393224 | tf_op jit(solution)/shard_map/ppermute | solution.py:434
  6.7 1.0 %collective-permute-start = (bf16[128,512]{1,0:T(8,128)(2,1)S(1)}, bf16[128,512]{1,0:T(8,128)(2,1)S(1)}, u32[]{:S(2)}, u32[]{:S(2)}) collective-permute-start(bf16[128,512]{1,0:T(8,128)(2,1)S(1)} %get-tuple-element.71.refs_0_), channel_id=1, source_target_pairs={{0,2},{1,3},{2,4},{3,5},{4,6},{5,7},{6,0},{7,1},{8,10},{9,11},{10,... | collective-permute-start | bytes 393224 | tf_op jit(solution)/shard_map/ppermute | solution.py:434
  7.7 0.1 lt.21
  7.8 3.1 %fusion.matrix_ref = bf16[4,2048,256]{2,1,0:T(8,128)(2,1)S(1)} fusion(bf16[2048,4,256]{2,1,0:T(4,128)(2,1)} %param.29, f32[4,64,256]{2,1,0:T(8,128)S(1)} %get-tuple-element.52, f32[2048]{0:T(1024)S(1)} %lt.21), kind=kLoop, calls=%fused_computation.1 | loop fusion | flops 4194304 | bytes 8658944 | tf_op jit(solution)/shard_map/jit(_where)/select_n | solution.py:396
  10.9 2.4 %shard_map.186 = (bf16[256,256]{1,0:T(8,128)(2,1)S(1)}, bf16[2048,256]{1,0:T(8,128)(2,1)S(1)}, bf16[256,256]{1,0:T(8,128)(2,1)S(1)}, bf16[256,256]{1,0:T(8,128)(2,1)S(1)}, f32[2048,256]{1,0:T(8,128)S(1)}) custom-call(f32[2048,256]{1,0:T(8,128)} %slip_hbm, bf16[32,2048]{1,0:T(8,128)(2,1)} %basis_in_ref.1), custom_call_target="tpu_custom_call" | custom-call | tf_op jit(solution)/shard_map/pallas_call | solution.py:32
  13.3 2.5 %collective-permute-start.5 = (bf16[256,256]{1,0:T(8,128)(2,1)S(1)}, bf16[256,256]{1,0:T(8,128)(2,1)S(1)}, u32[]{:S(2)}, u32[]{:S(2)}) collective-permute-start(bf16[256,256]{1,0:T(8,128)(2,1)S(1)} %get-tuple-element.60.refs_9_.refs_0_), channel_id=1, source_target_pairs={{0,24},{8,0},{16,8},{24,16},{1,25},{9,1},{17,9},{25,17},{2,26},{10... | collective-permute-start | bytes 393224 | tf_op jit(solution)/shard_map/ppermute | solution.py:430
  15.8 0.5 collective-permute-start.4
  16.3 0.0 collective-permute-done.2.refs_3_
  16.3 0.6 collective-permute-start.3
  16.9 3.7 %shard_map.187 = (f32[1024,8]{1,0:T(8,128)S(1)}, bf16[1024,1024]{1,0:T(8,128)(2,1)S(1)}) custom-call(f32[1,2048]{1,0:T(1,128)} %bitcast.14, f32[1,2048]{1,0:T(1,128)} %bitcast.16, f32[1,2048]{1,0:T(1,128)} %bitcast.18, f32[1,2048]{1,0:T(1,128)} %bitcast.20, f32[1,2048]{1,0:T(1,128)} %bitcast.22, f32[1,2048]{1,0:T(1,128)} %bitcast.24, s32[1,2048]{1,0:T(1,128)} %bitcast.26, ...), custom_call_target="tpu_custom_call" | custom-call | tf_op jit(solution)/shard_map/pallas_call | solution.py:32
  20.6 2.3 %collective-permute-done.4.refs_2_ = bf16[256,256]{1,0:T(8,128)(2,1)S(1)} collective-permute-done((bf16[256,256]{1,0:T(8,128)(2,1)S(1)}, bf16[256,256]{1,0:T(8,128)(2,1)S(1)}, u32[]{:S(2)}, u32[]{:S(2)}) %collective-permute-start.4) | collective-permute-done | bytes 131104 | tf_op jit(solution)/shard_map/ppermute | solution.py:430
  23.0 0.7 shard_map.189
  23.7 0.1 collective-permute-start.6
  23.8 0.6 collective-permute-start.8
  24.4 0.7 shard_map.188.kept_ref
  25.1 0.8 %collective-permute-done.6.sent_ref.refs_3_ = bf16[1280,256]{1,0:T(8,128)(2,1)S(1)} collective-permute-done((bf16[1280,256]{1,0:T(8,128)(2,1)S(1)}, bf16[1280,256]{1,0:T(8,128)(2,1)S(1)}, u32[]{:S(2)}, u32[]{:S(2)}) %collective-permute-start.6) | collective-permute-done | bytes 655392 | tf_op jit(solution)/shard_map/ppermute | solution.py:437
  25.9 0.3 shard_map.190
  26.1 2.5 %collective-permute-start.7 = (bf16[256,256]{1,0:T(8,128)(2,1)S(1)}, bf16[256,256]{1,0:T(8,128)(2,1)S(1)}, u32[]{:S(2)}, u32[]{:S(2)}) collective-permute-start(bf16[256,256]{1,0:T(8,128)(2,1)S(1)} %get-tuple-element.68), channel_id=1, source_target_pairs={{0,2},{1,3},{2,0},{3,1},{4,6},{5,7},{6,4},{7,5},{8,10},{9,11},{10,... | collective-permute-start | bytes 393224 | tf_op jit(solution)/shard_map/ppermute | solution.py:449
  28.7 0.1 collective-permute-start.10
  28.8 3.7 %shard_map.191 = (f32[2048,8]{1,0:T(8,128)S(1)}, bf16[1024,1024]{1,0:T(8,128)(2,1)S(1)}, bf16[3,2048,256]{2,1,0:T(8,128)(2,1)S(1)}, f32[2048,256]{1,0:T(8,128)S(1)}) custom-call(f32[1,2048]{1,0:T(1,128)} %bitcast.15, f32[1,2048]{1,0:T(1,128)} %bitcast.17, f32[1,2048]{1,0:T(1,128)} %bitcast.19, f32[1,2048]{1,0:T(1,128)} %bitcast.21, f32[1,2048]{1,0:T(1,128)} %bitcast.23, ...), custom_call_target="tpu_custom_call" | custom-call | tf_op jit(solution)/shard_map/pallas_call | solution.py:32
  32.5 0.5 collective-permute-done.7.came_ref
  33.0 1.7 %collective-permute-start.9 = (bf16[256,256]{1,0:T(8,128)(2,1)S(1)}, bf16[256,256]{1,0:T(8,128)(2,1)S(1)}, u32[]{:S(2)}, u32[]{:S(2)}) collective-permute-start(bf16[256,256]{1,0:T(8,128)(2,1)S(1)} %shard_map.194), channel_id=1, source_target_pairs={{0,4},{1,5},{2,6},{3,7},{4,0},{5,1},{6,2},{7,3},{8,12},{9,13},{10,... | collective-permute-start | bytes 393224 | tf_op jit(solution)/shard_map/ppermute | solution.py:434
  34.7 0.7 collective-permute-start.11
  35.4 0.0 copy-start
  35.4 0.0 copy-start.1
  35.4 4.9 %shard_map.193 = (f32[2048,256]{1,0:T(8,128)S(1)}, f32[2048,256]{1,0:T(8,128)S(1)}, f32[2048,256]{1,0:T(8,128)S(1)}, f32[2048,256]{1,0:T(8,128)S(1)}) custom-call(bf16[1024,1024]{1,0:T(8,128)(2,1)S(1)} %get-tuple-element.67.low_ref, bf16[1024,1024]{1,0:T(8,128)(2,1)S(1)} %get-tuple-element.70.high_ref, bf16[512,512]{1,0:T(8,128)(2,1)S(1)} %shard_map.192.own_ref, ...), custom_call_target="tpu_custom_call" | custom-call | tf_op jit(solution)/shard_map/pallas_call | solution.py:32
  40.4 1.8 %collective-permute-done.9.refs_0_ = bf16[256,256]{1,0:T(8,128)(2,1)S(1)} collective-permute-done((bf16[256,256]{1,0:T(8,128)(2,1)S(1)}, bf16[256,256]{1,0:T(8,128)(2,1)S(1)}, u32[]{:S(2)}, u32[]{:S(2)}) %collective-permute-start.9) | collective-permute-done | bytes 131104 | tf_op jit(solution)/shard_map/ppermute | solution.py:434
  42.2 1.9 %shard_map.195 = (f32[2048,256]{1,0:T(8,128)S(1)}, bf16[2048,256]{1,0:T(8,128)(2,1)S(1)}, bf16[256,256]{1,0:T(8,128)(2,1)S(1)}, bf16[256,256]{1,0:T(8,128)(2,1)S(1)}, bf16[256,256]{1,0:T(8,128)(2,1)S(1)}) custom-call(f32[2048,256]{1,0:T(8,128)S(1)} %get-tuple-element.78.shift_ref, f32[2048,256]{1,0:T(8,128)S(1)} %get-tuple-element.79.scale_ref, ...), custom_call_target="tpu_custom_call" | custom-call | tf_op jit(solution)/shard_map/pallas_call | solution.py:32
  44.1 3.2 %collective-permute-start.14 = (bf16[256,256]{1,0:T(8,128)(2,1)S(1)}, bf16[256,256]{1,0:T(8,128)(2,1)S(1)}, u32[]{:S(2)}, u32[]{:S(2)}) collective-permute-start(bf16[256,256]{1,0:T(8,128)(2,1)S(1)} %get-tuple-element.93.refs_0_), channel_id=1, source_target_pairs={{0,24},{8,0},{16,8},{24,16},{1,25},{9,1},{17,9},{25,17},{2,26},{10... | collective-permute-start | bytes 393224 | tf_op jit(solution)/shard_map/ppermute | solution.py:430
  47.3 1.3 %collective-permute-start.13 = (bf16[256,256]{1,0:T(8,128)(2,1)S(1)}, bf16[256,256]{1,0:T(8,128)(2,1)S(1)}, u32[]{:S(2)}, u32[]{:S(2)}) collective-permute-start(bf16[256,256]{1,0:T(8,128)(2,1)S(1)} %get-tuple-element.93.refs_0_), channel_id=1, source_target_pairs={{0,16},{8,24},{16,0},{24,8},{1,17},{9,25},{17,1},{25,9},{2,18},{10... | collective-permute-start | bytes 393224 | tf_op jit(solution)/shard_map/ppermute | solution.py:430
  48.6 0.9 %collective-permute-start.12 = (bf16[256,256]{1,0:T(8,128)(2,1)S(1)}, bf16[256,256]{1,0:T(8,128)(2,1)S(1)}, u32[]{:S(2)}, u32[]{:S(2)}) collective-permute-start(bf16[256,256]{1,0:T(8,128)(2,1)S(1)} %get-tuple-element.93.refs_0_), channel_id=1, source_target_pairs={{0,8},{8,16},{16,24},{24,0},{1,9},{9,17},{17,25},{25,1},{2,10},{10... | collective-permute-start | bytes 393224 | tf_op jit(solution)/shard_map/ppermute | solution.py:430
  49.5 2.0 %collective-permute-done.14.refs_3_ = bf16[256,256]{1,0:T(8,128)(2,1)S(1)} collective-permute-done((bf16[256,256]{1,0:T(8,128)(2,1)S(1)}, bf16[256,256]{1,0:T(8,128)(2,1)S(1)}, u32[]{:S(2)}, u32[]{:S(2)}) %collective-permute-start.14) | collective-permute-done | bytes 131104 | tf_op jit(solution)/shard_map/ppermute | solution.py:430
  51.4 1.9 %collective-permute-done.13.refs_2_ = bf16[256,256]{1,0:T(8,128)(2,1)S(1)} collective-permute-done((bf16[256,256]{1,0:T(8,128)(2,1)S(1)}, bf16[256,256]{1,0:T(8,128)(2,1)S(1)}, u32[]{:S(2)}, u32[]{:S(2)}) %collective-permute-start.13) | collective-permute-done | bytes 131104 | tf_op jit(solution)/shard_map/ppermute | solution.py:430
  53.4 1.1 %collective-permute-done.12.refs_1_ = bf16[256,256]{1,0:T(8,128)(2,1)S(1)} collective-permute-done((bf16[256,256]{1,0:T(8,128)(2,1)S(1)}, bf16[256,256]{1,0:T(8,128)(2,1)S(1)}, u32[]{:S(2)}, u32[]{:S(2)}) %collective-permute-start.12) | collective-permute-done | bytes 131104 | tf_op jit(solution)/shard_map/ppermute | solution.py:430
  54.4 0.7 shard_map.198
  55.1 0.1 collective-permute-start.15
  55.2 0.7 shard_map.197.kept_ref
  55.9 1.4 %collective-permute-done.15.sent_ref.refs_3_ = bf16[1280,256]{1,0:T(8,128)(2,1)S(1)} collective-permute-done((bf16[1280,256]{1,0:T(8,128)(2,1)S(1)}, bf16[1280,256]{1,0:T(8,128)(2,1)S(1)}, u32[]{:S(2)}, u32[]{:S(2)}) %collective-permute-start.15) | collective-permute-done | bytes 655392 | tf_op jit(solution)/shard_map/ppermute | solution.py:437
  57.3 0.3 shard_map.199
  57.6 0.5 collective-permute-start.16
  58.1 0.7 collective-permute-start.19
  58.8 2.9 %collective-permute-start.18 = (bf16[256,256]{1,0:T(8,128)(2,1)S(1)}, bf16[256,256]{1,0:T(8,128)(2,1)S(1)}, u32[]{:S(2)}, u32[]{:S(2)}) collective-permute-start(bf16[256,256]{1,0:T(8,128)(2,1)S(1)} %get-tuple-element.100), channel_id=1, source_target_pairs={{0,2},{1,3},{2,0},{3,1},{4,6},{5,7},{6,4},{7,5},{8,10},{9,11},{10,... | collective-permute-start | bytes 393224 | tf_op jit(solution)/shard_map/ppermute | solution.py:449
  61.6 1.5 %collective-permute-done.16.came_ref = bf16[256,256]{1,0:T(8,128)(2,1)S(1)} collective-permute-done((bf16[256,256]{1,0:T(8,128)(2,1)S(1)}, bf16[256,256]{1,0:T(8,128)(2,1)S(1)}, u32[]{:S(2)}, u32[]{:S(2)}) %collective-permute-start.16) | collective-permute-done | bytes 131104 | tf_op jit(solution)/shard_map/ppermute | solution.py:449
  63.2 1.5 %collective-permute-start.17 = (bf16[256,256]{1,0:T(8,128)(2,1)S(1)}, bf16[256,256]{1,0:T(8,128)(2,1)S(1)}, u32[]{:S(2)}, u32[]{:S(2)}) collective-permute-start(bf16[256,256]{1,0:T(8,128)(2,1)S(1)} %shard_map.200), channel_id=1, source_target_pairs={{0,4},{1,5},{2,6},{3,7},{4,0},{5,1},{6,2},{7,3},{8,12},{9,13},{10,... | collective-permute-start | bytes 393224 | tf_op jit(solution)/shard_map/ppermute | solution.py:434
  64.7 3.0 %shard_map.196 = (f32[2048,256]{1,0:T(8,128)S(1)}, f32[2048,256]{1,0:T(8,128)S(1)}, f32[2048,256]{1,0:T(8,128)S(1)}) custom-call(f32[2048,256]{1,0:T(8,128)S(1)} %get-tuple-element.54.slip_ref, f32[2048,256]{1,0:T(8,128)S(1)} %get-tuple-element.66.state_ref, f32[2048,256]{1,0:T(8,128)S(1)} %get-tuple-element.86.speed_ref, ...), custom_call_target="tpu_custom_call" | custom-call | tf_op jit(solution)/shard_map/pallas_call | solution.py:32
  67.7 3.9 %collective-permute-done.18.refs_2_ = bf16[256,256]{1,0:T(8,128)(2,1)S(1)} collective-permute-done((bf16[256,256]{1,0:T(8,128)(2,1)S(1)}, bf16[256,256]{1,0:T(8,128)(2,1)S(1)}, u32[]{:S(2)}, u32[]{:S(2)}) %collective-permute-start.18) | collective-permute-done | bytes 131104 | tf_op jit(solution)/shard_map/ppermute | solution.py:449
  71.6 2.6 %shard_map.201 = (f32[2048,256]{1,0:T(8,128)}, f32[2048,256]{1,0:T(8,128)}) custom-call(f32[2048,256]{1,0:T(8,128)S(1)} %get-tuple-element.90.shift_ref, f32[2048,256]{1,0:T(8,128)S(1)} %get-tuple-element.88.scale_ref, f32[2048,256]{1,0:T(8,128)S(1)} %get-tuple-element.91.rest_ref, f32[2048,256]{1,0:T(8,128)S(1)} %get-tuple-element.92.slip_rest_ref, ...), custom_call_target="tpu_custom_call" | custom-call | tf_op jit(solution)/shard_map/pallas_call | solution.py:32
  (17 shorter events, 0.2 us)
Async XLA Ops:
  1.6 14.7 %collective-permute-start.2 = (bf16[128,512]{1,0:T(8,128)(2,1)S(1)}, bf16[128,512]{1,0:T(8,128)(2,1)S(1)}, u32[]{:S(2)}, u32[]{:S(2)}) collective-permute-start(bf16[128,512]{1,0:T(8,128)(2,1)S(1)} %get-tuple-element.71.refs_0_), channel_id=1, source_target_pairs={{0,6},{1,7},{2,0},{3,1},{4,2},{5,3},{6,4},{7,5},{8,14},{9,15},{10,... | collective-permute-start | bytes 393224 | tf_op jit(solution)/shard_map/ppermute | solution.py:434
  6.7 13.9 %collective-permute-start.1 = (bf16[128,512]{1,0:T(8,128)(2,1)S(1)}, bf16[128,512]{1,0:T(8,128)(2,1)S(1)}, u32[]{:S(2)}, u32[]{:S(2)}) collective-permute-start(bf16[128,512]{1,0:T(8,128)(2,1)S(1)} %get-tuple-element.71.refs_0_), channel_id=1, source_target_pairs={{0,4},{1,5},{2,6},{3,7},{4,0},{5,1},{6,2},{7,3},{8,12},{9,13},{10,... | collective-permute-start | bytes 393224 | tf_op jit(solution)/shard_map/ppermute | solution.py:434
  6.7 13.9 %collective-permute-start = (bf16[128,512]{1,0:T(8,128)(2,1)S(1)}, bf16[128,512]{1,0:T(8,128)(2,1)S(1)}, u32[]{:S(2)}, u32[]{:S(2)}) collective-permute-start(bf16[128,512]{1,0:T(8,128)(2,1)S(1)} %get-tuple-element.71.refs_0_), channel_id=1, source_target_pairs={{0,2},{1,3},{2,4},{3,5},{4,6},{5,7},{6,0},{7,1},{8,10},{9,11},{10,... | collective-permute-start | bytes 393224 | tf_op jit(solution)/shard_map/ppermute | solution.py:434
  13.3 7.3 %collective-permute-start.5 = (bf16[256,256]{1,0:T(8,128)(2,1)S(1)}, bf16[256,256]{1,0:T(8,128)(2,1)S(1)}, u32[]{:S(2)}, u32[]{:S(2)}) collective-permute-start(bf16[256,256]{1,0:T(8,128)(2,1)S(1)} %get-tuple-element.60.refs_9_.refs_0_), channel_id=1, source_target_pairs={{0,24},{8,0},{16,8},{24,16},{1,25},{9,1},{17,9},{25,17},{2,26},{10... | collective-permute-start | bytes 393224 | tf_op jit(solution)/shard_map/ppermute | solution.py:430
  15.8 7.2 %collective-permute-start.4 = (bf16[256,256]{1,0:T(8,128)(2,1)S(1)}, bf16[256,256]{1,0:T(8,128)(2,1)S(1)}, u32[]{:S(2)}, u32[]{:S(2)}) collective-permute-start(bf16[256,256]{1,0:T(8,128)(2,1)S(1)} %get-tuple-element.60.refs_9_.refs_0_), channel_id=1, source_target_pairs={{0,16},{8,24},{16,0},{24,8},{1,17},{9,25},{17,1},{25,9},{2,18},{10... | collective-permute-start | bytes 393224 | tf_op jit(solution)/shard_map/ppermute | solution.py:430
  16.3 6.7 %collective-permute-start.3 = (bf16[256,256]{1,0:T(8,128)(2,1)S(1)}, bf16[256,256]{1,0:T(8,128)(2,1)S(1)}, u32[]{:S(2)}, u32[]{:S(2)}) collective-permute-start(bf16[256,256]{1,0:T(8,128)(2,1)S(1)} %get-tuple-element.60.refs_9_.refs_0_), channel_id=1, source_target_pairs={{0,8},{8,16},{16,24},{24,0},{1,9},{9,17},{17,25},{25,1},{2,10},{10... | collective-permute-start | bytes 393224 | tf_op jit(solution)/shard_map/ppermute | solution.py:430
  23.7 2.2 %collective-permute-start.6 = (bf16[1280,256]{1,0:T(8,128)(2,1)S(1)}, bf16[1280,256]{1,0:T(8,128)(2,1)S(1)}, u32[]{:S(2)}, u32[]{:S(2)}) collective-permute-start(bf16[1280,256]{1,0:T(8,128)(2,1)S(1)} %shard_map.189), channel_id=1, source_target_pairs={{0,1},{1,0},{2,3},{3,2},{4,5},{5,4},{6,7},{7,6},{8,9},{9,8},{10,11... | collective-permute-start | bytes 1966088 | tf_op jit(solution)/shard_map/ppermute | solution.py:437
  23.8 11.6 %collective-permute-start.8 = (bf16[512,512]{1,0:T(8,128)(2,1)S(1)}, bf16[512,512]{1,0:T(8,128)(2,1)S(1)}, u32[]{:S(2)}, u32[]{:S(2)}) collective-permute-start(bf16[512,512]{1,0:T(8,128)(2,1)S(1)} %shard_map.192.own_ref), channel_id=1, source_target_pairs={{0,1},{1,0},{2,3},{3,2},{4,5},{5,4},{6,7},{7,6},{8,9},{9,8},{10,11... | collective-permute-start | bytes 1572872 | tf_op jit(solution)/shard_map/ppermute | solution.py:437
  26.1 6.8 %collective-permute-start.7 = (bf16[256,256]{1,0:T(8,128)(2,1)S(1)}, bf16[256,256]{1,0:T(8,128)(2,1)S(1)}, u32[]{:S(2)}, u32[]{:S(2)}) collective-permute-start(bf16[256,256]{1,0:T(8,128)(2,1)S(1)} %get-tuple-element.68), channel_id=1, source_target_pairs={{0,2},{1,3},{2,0},{3,1},{4,6},{5,7},{6,4},{7,5},{8,10},{9,11},{10,... | collective-permute-start | bytes 393224 | tf_op jit(solution)/shard_map/ppermute | solution.py:449
  28.7 11.7 %collective-permute-start.10 = (bf16[256,256]{1,0:T(8,128)(2,1)S(1)}, bf16[256,256]{1,0:T(8,128)(2,1)S(1)}, u32[]{:S(2)}, u32[]{:S(2)}) collective-permute-start(bf16[256,256]{1,0:T(8,128)(2,1)S(1)} %get-tuple-element.84), channel_id=1, source_target_pairs={{0,2},{1,3},{2,0},{3,1},{4,6},{5,7},{6,4},{7,5},{8,10},{9,11},{10,... | collective-permute-start | bytes 393224 | tf_op jit(solution)/shard_map/ppermute | solution.py:449
  33.0 9.2 %collective-permute-start.9 = (bf16[256,256]{1,0:T(8,128)(2,1)S(1)}, bf16[256,256]{1,0:T(8,128)(2,1)S(1)}, u32[]{:S(2)}, u32[]{:S(2)}) collective-permute-start(bf16[256,256]{1,0:T(8,128)(2,1)S(1)} %shard_map.194), channel_id=1, source_target_pairs={{0,4},{1,5},{2,6},{3,7},{4,0},{5,1},{6,2},{7,3},{8,12},{9,13},{10,... | collective-permute-start | bytes 393224 | tf_op jit(solution)/shard_map/ppermute | solution.py:434
  34.7 7.5 %collective-permute-start.11 = (bf16[256,256]{1,0:T(8,128)(2,1)S(1)}, bf16[256,256]{1,0:T(8,128)(2,1)S(1)}, u32[]{:S(2)}, u32[]{:S(2)}) collective-permute-start(bf16[256,256]{1,0:T(8,128)(2,1)S(1)} %get-tuple-element.85), channel_id=1, source_target_pairs={{1,2},{3,4},{5,6},{7,8},{9,10},{11,12},{13,14},{15,16},{17,18},{19... | collective-permute-start | bytes 393224 | tf_op jit(solution)/shard_map/ppermute | solution.py:441
  35.4 6.8 %copy-start = (bf16[32,2048]{1,0:T(8,128)(2,1)S(1)}, bf16[32,2048]{1,0:T(8,128)(2,1)}, u32[]{:S(2)}) copy-start(bf16[32,2048]{1,0:T(8,128)(2,1)} %basis_out_ref.3) | copy-start | bytes 393220
  35.4 6.8 %copy-start.1 = (bf16[32,2048]{1,0:T(8,128)(2,1)S(1)}, bf16[32,2048]{1,0:T(8,128)(2,1)}, u32[]{:S(2)}) copy-start(bf16[32,2048]{1,0:T(8,128)(2,1)} %basis_in_ref.1) | copy-start | bytes 393220
  44.1 7.3 %collective-permute-start.14 = (bf16[256,256]{1,0:T(8,128)(2,1)S(1)}, bf16[256,256]{1,0:T(8,128)(2,1)S(1)}, u32[]{:S(2)}, u32[]{:S(2)}) collective-permute-start(bf16[256,256]{1,0:T(8,128)(2,1)S(1)} %get-tuple-element.93.refs_0_), channel_id=1, source_target_pairs={{0,24},{8,0},{16,8},{24,16},{1,25},{9,1},{17,9},{25,17},{2,26},{10... | collective-permute-start | bytes 393224 | tf_op jit(solution)/shard_map/ppermute | solution.py:430
  47.3 6.1 %collective-permute-start.13 = (bf16[256,256]{1,0:T(8,128)(2,1)S(1)}, bf16[256,256]{1,0:T(8,128)(2,1)S(1)}, u32[]{:S(2)}, u32[]{:S(2)}) collective-permute-start(bf16[256,256]{1,0:T(8,128)(2,1)S(1)} %get-tuple-element.93.refs_0_), channel_id=1, source_target_pairs={{0,16},{8,24},{16,0},{24,8},{1,17},{9,25},{17,1},{25,9},{2,18},{10... | collective-permute-start | bytes 393224 | tf_op jit(solution)/shard_map/ppermute | solution.py:430
  48.6 5.9 %collective-permute-start.12 = (bf16[256,256]{1,0:T(8,128)(2,1)S(1)}, bf16[256,256]{1,0:T(8,128)(2,1)S(1)}, u32[]{:S(2)}, u32[]{:S(2)}) collective-permute-start(bf16[256,256]{1,0:T(8,128)(2,1)S(1)} %get-tuple-element.93.refs_0_), channel_id=1, source_target_pairs={{0,8},{8,16},{16,24},{24,0},{1,9},{9,17},{17,25},{25,1},{2,10},{10... | collective-permute-start | bytes 393224 | tf_op jit(solution)/shard_map/ppermute | solution.py:430
  55.1 2.2 %collective-permute-start.15 = (bf16[1280,256]{1,0:T(8,128)(2,1)S(1)}, bf16[1280,256]{1,0:T(8,128)(2,1)S(1)}, u32[]{:S(2)}, u32[]{:S(2)}) collective-permute-start(bf16[1280,256]{1,0:T(8,128)(2,1)S(1)} %shard_map.198), channel_id=1, source_target_pairs={{0,1},{1,0},{2,3},{3,2},{4,5},{5,4},{6,7},{7,6},{8,9},{9,8},{10,11... | collective-permute-start | bytes 1966088 | tf_op jit(solution)/shard_map/ppermute | solution.py:437
  57.6 5.6 %collective-permute-start.16 = (bf16[256,256]{1,0:T(8,128)(2,1)S(1)}, bf16[256,256]{1,0:T(8,128)(2,1)S(1)}, u32[]{:S(2)}, u32[]{:S(2)}) collective-permute-start(bf16[256,256]{1,0:T(8,128)(2,1)S(1)} %get-tuple-element.96), channel_id=1, source_target_pairs={{0,2},{1,3},{2,0},{3,1},{4,6},{5,7},{6,4},{7,5},{8,10},{9,11},{10,... | collective-permute-start | bytes 393224 | tf_op jit(solution)/shard_map/ppermute | solution.py:449
  58.1 9.6 %collective-permute-start.19 = (bf16[256,256]{1,0:T(8,128)(2,1)S(1)}, bf16[256,256]{1,0:T(8,128)(2,1)S(1)}, u32[]{:S(2)}, u32[]{:S(2)}) collective-permute-start(bf16[256,256]{1,0:T(8,128)(2,1)S(1)} %get-tuple-element.101), channel_id=1, source_target_pairs={{1,2},{3,4},{5,6},{7,8},{9,10},{11,12},{13,14},{15,16},{17,18},{19... | collective-permute-start | bytes 393224 | tf_op jit(solution)/shard_map/ppermute | solution.py:441
  58.8 12.8 %collective-permute-start.18 = (bf16[256,256]{1,0:T(8,128)(2,1)S(1)}, bf16[256,256]{1,0:T(8,128)(2,1)S(1)}, u32[]{:S(2)}, u32[]{:S(2)}) collective-permute-start(bf16[256,256]{1,0:T(8,128)(2,1)S(1)} %get-tuple-element.100), channel_id=1, source_target_pairs={{0,2},{1,3},{2,0},{3,1},{4,6},{5,7},{6,4},{7,5},{8,10},{9,11},{10,... | collective-permute-start | bytes 393224 | tf_op jit(solution)/shard_map/ppermute | solution.py:449
  63.2 8.4 %collective-permute-start.17 = (bf16[256,256]{1,0:T(8,128)(2,1)S(1)}, bf16[256,256]{1,0:T(8,128)(2,1)S(1)}, u32[]{:S(2)}, u32[]{:S(2)}) collective-permute-start(bf16[256,256]{1,0:T(8,128)(2,1)S(1)} %shard_map.200), channel_id=1, source_target_pairs={{0,4},{1,5},{2,6},{3,7},{4,0},{5,1},{6,2},{7,3},{8,12},{9,13},{10,... | collective-permute-start | bytes 393224 | tf_op jit(solution)/shard_map/ppermute | solution.py:434

commit v5 on v4

--- a/solution.py
+++ b/solution.py
@@ -62,15 +62,9 @@
     cross_ref[...] = jnp.where(even, first, last)
 
 
-def project_kernel(slip_hbm, basis_hbm, coeff_ref, rounded_ref, pair_ref, cross_ref, slip_ref, basis_ref, sems):
-    count = slip_ref.shape[0] // BS
-    blocks = [pl.ds(n * BS, BS) for n in range(count)]
-    copies = start_copies(
-        [(basis_hbm, basis_ref)] + [(slip_hbm.at[at, :], slip_ref.at[at, :]) for at in blocks], sems
-    )
-    copies[0].wait()
-    for n, at in enumerate(blocks):
-        copies[1 + n].wait()
+def project_kernel(slip_ref, basis_ref, coeff_ref, rounded_ref, pair_ref, cross_ref):
+    for n in range(slip_ref.shape[0] // BS):
+        at = pl.ds(n * BS, BS)
         rounded = slip_ref[at, :].astype(BF16)
         rounded_ref[at, :] = rounded
         coeff_ref[n * R : (n + 1) * R, :] = dot(basis_ref[:, at], rounded).astype(BF16)
@@ -79,20 +73,17 @@
 
 def project(slip, basis_in):
     patches, ens = slip.shape
-    count = patches // BS
     edge = jax.ShapeDtypeStruct((BS, ens), BF16)
     return call(
         project_kernel,
         [
-            jax.ShapeDtypeStruct((count * R, ens), BF16),
+            jax.ShapeDtypeStruct((patches // BS * R, ens), BF16),
             jax.ShapeDtypeStruct((patches, ens), BF16),
             edge,
             edge,
-            jax.ShapeDtypeStruct((patches, ens), F32),
         ],
-        *in_hbm(slip, basis_in),
-        specs=[HBM] * 2,
-        scratch_shapes=[pltpu.VMEM(basis_in.shape, BF16), pltpu.SemaphoreType.DMA((1 + count,))],
+        slip,
+        basis_in,
     )
 
 
@@ -456,11 +447,8 @@
             own, cross = lax.optimization_barrier((own, cross))
         return own, to_partner(passed), to_partner(direct), keep, sent, cross if later else to_chip(cross)
 
-    def second_step(own, came, direct, keep, sent, cross, later):
+    def second_step(own, came, direct, keep, sent, cross):
         sums = call(pair_sum_kernel, [jax.ShapeDtypeStruct((share, ens), BF16)] * (heights // 2 - 1), keep, came)
-        if later:
-            sums, cross = lax.optimization_barrier((sums, cross))
-            cross = to_chip(cross)
         return [to_height(part, 2 * (d + 1)) for d, part in enumerate(sums)] + [own, direct, sent, cross]
 
     def row_coeffs(coeff):
@@ -485,7 +473,7 @@
     fields = [joined] + [to_height(joined, d) for d in range(1, heights)]
     masked = masked_coupling(coupling, wide)
     masked, slip = lax.optimization_barrier((masked, slip))
-    coeff, rounded, pair, cross, slip = project(slip, basis_in)
+    coeff, rounded, pair, cross = project(slip, basis_in)
     coeffs = row_coeffs(coeff)
     brick_lists = [adj_count[None], adj_bricks, adj_weight]
     columns = [array[None] for array in per_patch] + brick_lists
@@ -522,17 +510,19 @@
         scratch_shapes=scratch,
     )
     came, high = lax.optimization_barrier((came, high))
-    outer = second_step(own_part, came, direct, keep, sent, cross, True)
+    outer = second_step(own_part, came, direct, keep, sent, cross)
     shift, scale, rest, scale_mid = call(
         prepare_first_kernel, [full] * 4, low, high, own, other, slip, state, numbers, near, rounded
     )
+    shift, cross = lax.optimization_barrier((shift, cross))
+    outer[-1] = to_chip(cross)
     speed, rounded, coeff, pair, cross = call(
         functools.partial(finish_first_kernel, len(outer) - 2),
         [full, half, jax.ShapeDtypeStruct((patches // BS * R, ens), BF16), edge, edge],
         shift, scale, slip, basis_out, basis_in, near, *outer,
     )
     coeffs = row_coeffs(coeff)
-    outer = second_step(*first_step(coeffs, pair, cross, False), False)
+    outer = second_step(*first_step(coeffs, pair, cross, False))
     shift, slip_rest, rest = call(
         prepare_second_kernel, [full] * 3,
         slip, state, speed, rest, scale_mid, numbers, near, rounded,

time: 74.6 us -> 78.4 us (1.051)
  starting transfers between devices: 26.3 us -> 30.5 us
  Pallas kernels: 26.6 us -> 24.5 us
  waiting for transfers between devices: 17.2 us -> 18.7 us
    ppermute x6, starting transfers between devices: 8.97 us -> 14.6 us  [to_row(): lax.ppermute(array, 'row', [(i, (i + d) % row_count) for i in range(row_c...]
    pallas_call x17, Pallas kernels: 26.6 us -> 24.5 us  [call(): pl.pallas_call(kernel, in_specs=specs or [VMEM] * len(operands), out_shap...]
    ppermute x5, starting transfers between devices: 9.3 us -> 7.91 us  [to_height(): return lax.ppermute(array, 'col', pairs)]
    ppermute x4, waiting for transfers between devices: 5.9 us -> 7.03 us  [to_partner(): return lax.ppermute(array, 'col', pairs)]
  transfers between devices with their start and end apart: 20 -> 20, of which waited for: 10 -> 11; matrix products, arithmetic and copies ran while one was open for 4% -> 4% of each run, Pallas kernels for 26% -> 22%
where the time goes in v5:
time: 78.4 us; the launch traced here: 78 us
  starting transfers between devices  30.5 us (39%)
  Pallas kernels  24.5 us (31%)
  waiting for transfers between devices  18.7 us (24%)
  other arithmetic  3.28 us (4%)
  between operations  0.87 us (1%)
    pallas_call x17, Pallas kernels, call(): pl.pallas_call(kernel, in_specs=specs or [VMEM] * len(operands), out_shap...  24.5 us
    ppermute x6, starting transfers between devices, to_row(): lax.ppermute(array, 'row', [(i, (i + d) % row_count) for i in range(row_c...  14.6 us
    ppermute x5, starting transfers between devices, to_height(): return lax.ppermute(array, 'col', pairs)  7.91 us
    ppermute x6, waiting for transfers between devices, to_row(): lax.ppermute(array, 'row', [(i, (i + d) % row_count) for i in range(row_c...  7.29 us
    ppermute x4, waiting for transfers between devices, to_partner(): return lax.ppermute(array, 'col', pairs)  7.03 us
    ppermute x4, starting transfers between devices, to_partner(): return lax.ppermute(array, 'col', pairs)  6.01 us
    select_n x1, other arithmetic, masked_coupling(): jnp.where(keep, matrix, jnp.zeros((), BF16)).reshape(sources, rows, width)  3.28 us
    ppermute x5, waiting for transfers between devices, to_height(): return lax.ppermute(array, 'col', pairs)  2.19 us
  transfers between devices with their start and end apart: 20, of which 11 were waited for; matrix products, arithmetic and copies ran while one was open for 4% of the time, Pallas kernels for 22%

profile of v5, /device:TPU:0, one launch (start us, length us, event | category | flops | bytes accessed | tf_op | source)
XLA Modules:
  0.0 78.0 jit_solution(14245253506495785410)
XLA Ops:
  0.6 1.0 %shard_map.185 = (f32[4,64,256]{2,1,0:T(8,128)S(1)}, bf16[128,512]{1,0:T(8,128)(2,1)S(1)}) custom-call(s32[4,8,64]{2,1,0:T(8,128)} %bitcast.28, bf16[128,256]{1,0:T(8,128)(2,1)} %now_hbm.1, bf16[128,256]{1,0:T(8,128)(2,1)} %rate_hbm.1), custom_call_target="tpu_custom_call" | custom-call | tf_op jit(solution)/shard_map/pallas_call | solution.py:32
  1.6 5.1 %collective-permute-start.2 = (bf16[128,512]{1,0:T(8,128)(2,1)S(1)}, bf16[128,512]{1,0:T(8,128)(2,1)S(1)}, u32[]{:S(2)}, u32[]{:S(2)}) collective-permute-start(bf16[128,512]{1,0:T(8,128)(2,1)S(1)} %get-tuple-element.69.refs_0_), channel_id=1, source_target_pairs={{0,6},{1,7},{2,0},{3,1},{4,2},{5,3},{6,4},{7,5},{8,14},{9,15},{10,... | collective-permute-start | bytes 393224 | tf_op jit(solution)/shard_map/ppermute | solution.py:425
  6.7 0.0 collective-permute-start.1
  6.7 1.0 %collective-permute-start = (bf16[128,512]{1,0:T(8,128)(2,1)S(1)}, bf16[128,512]{1,0:T(8,128)(2,1)S(1)}, u32[]{:S(2)}, u32[]{:S(2)}) collective-permute-start(bf16[128,512]{1,0:T(8,128)(2,1)S(1)} %get-tuple-element.69.refs_0_), channel_id=1, source_target_pairs={{0,2},{1,3},{2,4},{3,5},{4,6},{5,7},{6,0},{7,1},{8,10},{9,11},{10,... | collective-permute-start | bytes 393224 | tf_op jit(solution)/shard_map/ppermute | solution.py:425
  7.7 0.1 lt.21
  7.8 3.3 %fusion.matrix_ref = bf16[4,2048,256]{2,1,0:T(8,128)(2,1)S(1)} fusion(bf16[2048,4,256]{2,1,0:T(4,128)(2,1)} %param.29, f32[4,64,256]{2,1,0:T(8,128)S(1)} %get-tuple-element.51, f32[2048]{0:T(1024)S(1)} %lt.21), kind=kLoop, calls=%fused_computation.1 | loop fusion | flops 4194304 | bytes 8658944 | tf_op jit(solution)/shard_map/jit(_where)/select_n | solution.py:387
  11.1 0.3 shard_map.186
  11.5 2.5 %collective-permute-start.5 = (bf16[256,256]{1,0:T(8,128)(2,1)S(1)}, bf16[256,256]{1,0:T(8,128)(2,1)S(1)}, u32[]{:S(2)}, u32[]{:S(2)}) collective-permute-start(bf16[256,256]{1,0:T(8,128)(2,1)S(1)} %get-tuple-element.58.refs_9_.refs_0_), channel_id=1, source_target_pairs={{0,24},{8,0},{16,8},{24,16},{1,25},{9,1},{17,9},{25,17},{2,26},{10... | collective-permute-start | bytes 393224 | tf_op jit(solution)/shard_map/ppermute | solution.py:421
  13.9 0.5 collective-permute-start.4
  14.5 0.6 collective-permute-start.3
  15.1 3.7 %shard_map.187 = (f32[1024,8]{1,0:T(8,128)S(1)}, bf16[1024,1024]{1,0:T(8,128)(2,1)S(1)}) custom-call(f32[1,2048]{1,0:T(1,128)} %bitcast.14, f32[1,2048]{1,0:T(1,128)} %bitcast.16, f32[1,2048]{1,0:T(1,128)} %bitcast.18, f32[1,2048]{1,0:T(1,128)} %bitcast.20, f32[1,2048]{1,0:T(1,128)} %bitcast.22, f32[1,2048]{1,0:T(1,128)} %bitcast.24, s32[1,2048]{1,0:T(1,128)} %bitcast.26, ...), custom_call_target="tpu_custom_call" | custom-call | tf_op jit(solution)/shard_map/pallas_call | solution.py:32
  18.7 0.0 collective-permute-done.1.refs_2_
  18.8 2.3 %collective-permute-done.4.refs_2_ = bf16[256,256]{1,0:T(8,128)(2,1)S(1)} collective-permute-done((bf16[256,256]{1,0:T(8,128)(2,1)S(1)}, bf16[256,256]{1,0:T(8,128)(2,1)S(1)}, u32[]{:S(2)}, u32[]{:S(2)}) %collective-permute-start.4) | collective-permute-done | bytes 131104 | tf_op jit(solution)/shard_map/ppermute | solution.py:421
  21.1 0.7 shard_map.189
  21.8 0.1 collective-permute-start.6
  22.0 0.6 collective-permute-start.8
  22.5 0.7 shard_map.188.kept_ref
  23.2 0.8 collective-permute-done.6.sent_ref.refs_3_
  24.0 0.3 shard_map.190
  24.3 2.5 %collective-permute-start.7 = (bf16[256,256]{1,0:T(8,128)(2,1)S(1)}, bf16[256,256]{1,0:T(8,128)(2,1)S(1)}, u32[]{:S(2)}, u32[]{:S(2)}) collective-permute-start(bf16[256,256]{1,0:T(8,128)(2,1)S(1)} %get-tuple-element.66), channel_id=1, source_target_pairs={{0,2},{1,3},{2,0},{3,1},{4,6},{5,7},{6,4},{7,5},{8,10},{9,11},{10,... | collective-permute-start | bytes 393224 | tf_op jit(solution)/shard_map/ppermute | solution.py:440
  26.8 0.1 collective-permute-start.10
  26.9 3.7 %shard_map.191 = (f32[2048,8]{1,0:T(8,128)S(1)}, bf16[1024,1024]{1,0:T(8,128)(2,1)S(1)}, bf16[3,2048,256]{2,1,0:T(8,128)(2,1)S(1)}, f32[2048,256]{1,0:T(8,128)S(1)}) custom-call(f32[1,2048]{1,0:T(1,128)} %bitcast.15, f32[1,2048]{1,0:T(1,128)} %bitcast.17, f32[1,2048]{1,0:T(1,128)} %bitcast.19, f32[1,2048]{1,0:T(1,128)} %bitcast.21, f32[1,2048]{1,0:T(1,128)} %bitcast.23, ...), custom_call_target="tpu_custom_call" | custom-call | tf_op jit(solution)/shard_map/pallas_call | solution.py:32
  30.6 0.5 collective-permute-done.7.came_ref
  31.1 1.7 %collective-permute-start.9 = (bf16[256,256]{1,0:T(8,128)(2,1)S(1)}, bf16[256,256]{1,0:T(8,128)(2,1)S(1)}, u32[]{:S(2)}, u32[]{:S(2)}) collective-permute-start(bf16[256,256]{1,0:T(8,128)(2,1)S(1)} %shard_map.194), channel_id=1, source_target_pairs={{0,4},{1,5},{2,6},{3,7},{4,0},{5,1},{6,2},{7,3},{8,12},{9,13},{10,... | collective-permute-start | bytes 393224 | tf_op jit(solution)/shard_map/ppermute | solution.py:425
  32.9 4.9 %shard_map.193 = (f32[2048,256]{1,0:T(8,128)S(1)}, f32[2048,256]{1,0:T(8,128)S(1)}, f32[2048,256]{1,0:T(8,128)S(1)}, f32[2048,256]{1,0:T(8,128)S(1)}) custom-call(bf16[1024,1024]{1,0:T(8,128)(2,1)S(1)} %get-tuple-element.65.low_ref, bf16[1024,1024]{1,0:T(8,128)(2,1)S(1)} %get-tuple-element.68.high_ref, bf16[512,512]{1,0:T(8,128)(2,1)S(1)} %shard_map.192.own_ref, ...), custom_call_target="tpu_custom_call" | custom-call | tf_op jit(solution)/shard_map/pallas_call | solution.py:32
  37.8 0.7 collective-permute-start.11
  38.5 1.2 %collective-permute-done.9.refs_0_ = bf16[256,256]{1,0:T(8,128)(2,1)S(1)} collective-permute-done((bf16[256,256]{1,0:T(8,128)(2,1)S(1)}, bf16[256,256]{1,0:T(8,128)(2,1)S(1)}, u32[]{:S(2)}, u32[]{:S(2)}) %collective-permute-start.9) | collective-permute-done | bytes 131104 | tf_op jit(solution)/shard_map/ppermute | solution.py:425
  39.7 1.8 %shard_map.195 = (f32[2048,256]{1,0:T(8,128)S(1)}, bf16[2048,256]{1,0:T(8,128)(2,1)S(1)}, bf16[256,256]{1,0:T(8,128)(2,1)S(1)}, bf16[256,256]{1,0:T(8,128)(2,1)S(1)}, bf16[256,256]{1,0:T(8,128)(2,1)S(1)}) custom-call(f32[2048,256]{1,0:T(8,128)S(1)} %get-tuple-element.78.shift_ref, f32[2048,256]{1,0:T(8,128)S(1)} %get-tuple-element.79.scale_ref, ...), custom_call_target="tpu_custom_call" | custom-call | tf_op jit(solution)/shard_map/pallas_call | solution.py:32
  41.5 8.8 %collective-permute-start.14 = (bf16[256,256]{1,0:T(8,128)(2,1)S(1)}, bf16[256,256]{1,0:T(8,128)(2,1)S(1)}, u32[]{:S(2)}, u32[]{:S(2)}) collective-permute-start(bf16[256,256]{1,0:T(8,128)(2,1)S(1)} %get-tuple-element.91.refs_0_), channel_id=1, source_target_pairs={{0,24},{8,0},{16,8},{24,16},{1,25},{9,1},{17,9},{25,17},{2,26},{10... | collective-permute-start | bytes 393224 | tf_op jit(solution)/shard_map/ppermute | solution.py:421
  50.3 1.3 %collective-permute-start.13 = (bf16[256,256]{1,0:T(8,128)(2,1)S(1)}, bf16[256,256]{1,0:T(8,128)(2,1)S(1)}, u32[]{:S(2)}, u32[]{:S(2)}) collective-permute-start(bf16[256,256]{1,0:T(8,128)(2,1)S(1)} %get-tuple-element.91.refs_0_), channel_id=1, source_target_pairs={{0,16},{8,24},{16,0},{24,8},{1,17},{9,25},{17,1},{25,9},{2,18},{10... | collective-permute-start | bytes 393224 | tf_op jit(solution)/shard_map/ppermute | solution.py:421
  51.6 0.9 %collective-permute-start.12 = (bf16[256,256]{1,0:T(8,128)(2,1)S(1)}, bf16[256,256]{1,0:T(8,128)(2,1)S(1)}, u32[]{:S(2)}, u32[]{:S(2)}) collective-permute-start(bf16[256,256]{1,0:T(8,128)(2,1)S(1)} %get-tuple-element.91.refs_0_), channel_id=1, source_target_pairs={{0,8},{8,16},{16,24},{24,0},{1,9},{9,17},{17,25},{25,1},{2,10},{10... | collective-permute-start | bytes 393224 | tf_op jit(solution)/shard_map/ppermute | solution.py:421
  52.5 0.6 collective-permute-done.14.refs_3_
  53.1 2.2 %collective-permute-done.13.refs_2_ = bf16[256,256]{1,0:T(8,128)(2,1)S(1)} collective-permute-done((bf16[256,256]{1,0:T(8,128)(2,1)S(1)}, bf16[256,256]{1,0:T(8,128)(2,1)S(1)}, u32[]{:S(2)}, u32[]{:S(2)}) %collective-permute-start.13) | collective-permute-done | bytes 131104 | tf_op jit(solution)/shard_map/ppermute | solution.py:421
  55.3 2.2 %collective-permute-done.12.refs_1_ = bf16[256,256]{1,0:T(8,128)(2,1)S(1)} collective-permute-done((bf16[256,256]{1,0:T(8,128)(2,1)S(1)}, bf16[256,256]{1,0:T(8,128)(2,1)S(1)}, u32[]{:S(2)}, u32[]{:S(2)}) %collective-permute-start.12) | collective-permute-done | bytes 131104 | tf_op jit(solution)/shard_map/ppermute | solution.py:421
  57.5 0.7 shard_map.198
  58.2 0.1 collective-permute-start.15
  58.3 0.7 shard_map.197.kept_ref
  59.0 1.4 %collective-permute-done.15.sent_ref.refs_3_ = bf16[1280,256]{1,0:T(8,128)(2,1)S(1)} collective-permute-done((bf16[1280,256]{1,0:T(8,128)(2,1)S(1)}, bf16[1280,256]{1,0:T(8,128)(2,1)S(1)}, u32[]{:S(2)}, u32[]{:S(2)}) %collective-permute-start.15) | collective-permute-done | bytes 655392 | tf_op jit(solution)/shard_map/ppermute | solution.py:428
  60.3 0.3 shard_map.199
  60.6 0.1 collective-permute-start.16
  60.7 0.7 collective-permute-start.19
  61.4 3.3 %collective-permute-start.18 = (bf16[256,256]{1,0:T(8,128)(2,1)S(1)}, bf16[256,256]{1,0:T(8,128)(2,1)S(1)}, u32[]{:S(2)}, u32[]{:S(2)}) collective-permute-start(bf16[256,256]{1,0:T(8,128)(2,1)S(1)} %get-tuple-element.98), channel_id=1, source_target_pairs={{0,2},{1,3},{2,0},{3,1},{4,6},{5,7},{6,4},{7,5},{8,10},{9,11},{10,... | collective-permute-start | bytes 393224 | tf_op jit(solution)/shard_map/ppermute | solution.py:440
  64.7 1.5 %collective-permute-done.16.came_ref = bf16[256,256]{1,0:T(8,128)(2,1)S(1)} collective-permute-done((bf16[256,256]{1,0:T(8,128)(2,1)S(1)}, bf16[256,256]{1,0:T(8,128)(2,1)S(1)}, u32[]{:S(2)}, u32[]{:S(2)}) %collective-permute-start.16) | collective-permute-done | bytes 131104 | tf_op jit(solution)/shard_map/ppermute | solution.py:440
  66.3 0.1 collective-permute-start.17
  66.4 3.0 %shard_map.196 = (f32[2048,256]{1,0:T(8,128)S(1)}, f32[2048,256]{1,0:T(8,128)S(1)}, f32[2048,256]{1,0:T(8,128)S(1)}) custom-call(f32[2048,256]{1,0:T(8,128)S(1)} %copy-done, f32[2048,256]{1,0:T(8,128)S(1)} %get-tuple-element.64.state_ref, f32[2048,256]{1,0:T(8,128)S(1)} %get-tuple-element.84.speed_ref, f32[2048,256]{1,0:T(8,128)S(1)} %get-tuple-element.85.part_ref, ...), custom_call_target="tpu_custom_call" | custom-call | tf_op jit(solution)/shard_map/pallas_call | solution.py:32
  69.4 5.0 %collective-permute-done.18.refs_2_ = bf16[256,256]{1,0:T(8,128)(2,1)S(1)} collective-permute-done((bf16[256,256]{1,0:T(8,128)(2,1)S(1)}, bf16[256,256]{1,0:T(8,128)(2,1)S(1)}, u32[]{:S(2)}, u32[]{:S(2)}) %collective-permute-start.18) | collective-permute-done | bytes 131104 | tf_op jit(solution)/shard_map/ppermute | solution.py:440
  74.4 1.0 %collective-permute-done.17.refs_0_ = bf16[256,256]{1,0:T(8,128)(2,1)S(1)} collective-permute-done((bf16[256,256]{1,0:T(8,128)(2,1)S(1)}, bf16[256,256]{1,0:T(8,128)(2,1)S(1)}, u32[]{:S(2)}, u32[]{:S(2)}) %collective-permute-start.17) | collective-permute-done | bytes 131104 | tf_op jit(solution)/shard_map/ppermute | solution.py:425
  75.4 2.6 %shard_map.201 = (f32[2048,256]{1,0:T(8,128)}, f32[2048,256]{1,0:T(8,128)}) custom-call(f32[2048,256]{1,0:T(8,128)S(1)} %get-tuple-element.88.shift_ref, f32[2048,256]{1,0:T(8,128)S(1)} %get-tuple-element.86.scale_ref, f32[2048,256]{1,0:T(8,128)S(1)} %get-tuple-element.89.rest_ref, f32[2048,256]{1,0:T(8,128)S(1)} %get-tuple-element.90.slip_rest_ref, ...), custom_call_target="tpu_custom_call" | custom-call | tf_op jit(solution)/shard_map/pallas_call | solution.py:32
  (19 shorter events, 0.2 us)
Async XLA Ops:
  1.6 12.8 %collective-permute-start.2 = (bf16[128,512]{1,0:T(8,128)(2,1)S(1)}, bf16[128,512]{1,0:T(8,128)(2,1)S(1)}, u32[]{:S(2)}, u32[]{:S(2)}) collective-permute-start(bf16[128,512]{1,0:T(8,128)(2,1)S(1)} %get-tuple-element.69.refs_0_), channel_id=1, source_target_pairs={{0,6},{1,7},{2,0},{3,1},{4,2},{5,3},{6,4},{7,5},{8,14},{9,15},{10,... | collective-permute-start | bytes 393224 | tf_op jit(solution)/shard_map/ppermute | solution.py:425
  6.7 12.0 %collective-permute-start.1 = (bf16[128,512]{1,0:T(8,128)(2,1)S(1)}, bf16[128,512]{1,0:T(8,128)(2,1)S(1)}, u32[]{:S(2)}, u32[]{:S(2)}) collective-permute-start(bf16[128,512]{1,0:T(8,128)(2,1)S(1)} %get-tuple-element.69.refs_0_), channel_id=1, source_target_pairs={{0,4},{1,5},{2,6},{3,7},{4,0},{5,1},{6,2},{7,3},{8,12},{9,13},{10,... | collective-permute-start | bytes 393224 | tf_op jit(solution)/shard_map/ppermute | solution.py:425
  6.7 12.0 %collective-permute-start = (bf16[128,512]{1,0:T(8,128)(2,1)S(1)}, bf16[128,512]{1,0:T(8,128)(2,1)S(1)}, u32[]{:S(2)}, u32[]{:S(2)}) collective-permute-start(bf16[128,512]{1,0:T(8,128)(2,1)S(1)} %get-tuple-element.69.refs_0_), channel_id=1, source_target_pairs={{0,2},{1,3},{2,4},{3,5},{4,6},{5,7},{6,0},{7,1},{8,10},{9,11},{10,... | collective-permute-start | bytes 393224 | tf_op jit(solution)/shard_map/ppermute | solution.py:425
  7.8 3.3 %copy-start = (f32[2048,256]{1,0:T(8,128)S(1)}, f32[2048,256]{1,0:T(8,128)}, u32[]{:S(2)}) copy-start(f32[2048,256]{1,0:T(8,128)} %slip_ref.3) | copy-start | bytes 6291460
  7.8 3.3 %copy-start.2 = (bf16[32,2048]{1,0:T(8,128)(2,1)S(1)}, bf16[32,2048]{1,0:T(8,128)(2,1)}, u32[]{:S(2)}) copy-start(bf16[32,2048]{1,0:T(8,128)(2,1)} %basis_in_ref.1) | copy-start | bytes 393220
  11.5 7.3 %collective-permute-start.5 = (bf16[256,256]{1,0:T(8,128)(2,1)S(1)}, bf16[256,256]{1,0:T(8,128)(2,1)S(1)}, u32[]{:S(2)}, u32[]{:S(2)}) collective-permute-start(bf16[256,256]{1,0:T(8,128)(2,1)S(1)} %get-tuple-element.58.refs_9_.refs_0_), channel_id=1, source_target_pairs={{0,24},{8,0},{16,8},{24,16},{1,25},{9,1},{17,9},{25,17},{2,26},{10... | collective-permute-start | bytes 393224 | tf_op jit(solution)/shard_map/ppermute | solution.py:421
  13.9 7.2 %collective-permute-start.4 = (bf16[256,256]{1,0:T(8,128)(2,1)S(1)}, bf16[256,256]{1,0:T(8,128)(2,1)S(1)}, u32[]{:S(2)}, u32[]{:S(2)}) collective-permute-start(bf16[256,256]{1,0:T(8,128)(2,1)S(1)} %get-tuple-element.58.refs_9_.refs_0_), channel_id=1, source_target_pairs={{0,16},{8,24},{16,0},{24,8},{1,17},{9,25},{17,1},{25,9},{2,18},{10... | collective-permute-start | bytes 393224 | tf_op jit(solution)/shard_map/ppermute | solution.py:421
  14.5 6.7 %collective-permute-start.3 = (bf16[256,256]{1,0:T(8,128)(2,1)S(1)}, bf16[256,256]{1,0:T(8,128)(2,1)S(1)}, u32[]{:S(2)}, u32[]{:S(2)}) collective-permute-start(bf16[256,256]{1,0:T(8,128)(2,1)S(1)} %get-tuple-element.58.refs_9_.refs_0_), channel_id=1, source_target_pairs={{0,8},{8,16},{16,24},{24,0},{1,9},{9,17},{17,25},{25,1},{2,10},{10... | collective-permute-start | bytes 393224 | tf_op jit(solution)/shard_map/ppermute | solution.py:421
  21.8 2.2 %collective-permute-start.6 = (bf16[1280,256]{1,0:T(8,128)(2,1)S(1)}, bf16[1280,256]{1,0:T(8,128)(2,1)S(1)}, u32[]{:S(2)}, u32[]{:S(2)}) collective-permute-start(bf16[1280,256]{1,0:T(8,128)(2,1)S(1)} %shard_map.189), channel_id=1, source_target_pairs={{0,1},{1,0},{2,3},{3,2},{4,5},{5,4},{6,7},{7,6},{8,9},{9,8},{10,11... | collective-permute-start | bytes 1966088 | tf_op jit(solution)/shard_map/ppermute | solution.py:428
  22.0 10.9 %collective-permute-start.8 = (bf16[512,512]{1,0:T(8,128)(2,1)S(1)}, bf16[512,512]{1,0:T(8,128)(2,1)S(1)}, u32[]{:S(2)}, u32[]{:S(2)}) collective-permute-start(bf16[512,512]{1,0:T(8,128)(2,1)S(1)} %shard_map.192.own_ref), channel_id=1, source_target_pairs={{0,1},{1,0},{2,3},{3,2},{4,5},{5,4},{6,7},{7,6},{8,9},{9,8},{10,11... | collective-permute-start | bytes 1572872 | tf_op jit(solution)/shard_map/ppermute | solution.py:428
  24.3 6.8 %collective-permute-start.7 = (bf16[256,256]{1,0:T(8,128)(2,1)S(1)}, bf16[256,256]{1,0:T(8,128)(2,1)S(1)}, u32[]{:S(2)}, u32[]{:S(2)}) collective-permute-start(bf16[256,256]{1,0:T(8,128)(2,1)S(1)} %get-tuple-element.66), channel_id=1, source_target_pairs={{0,2},{1,3},{2,0},{3,1},{4,6},{5,7},{6,4},{7,5},{8,10},{9,11},{10,... | collective-permute-start | bytes 393224 | tf_op jit(solution)/shard_map/ppermute | solution.py:440
  26.8 11.7 %collective-permute-start.10 = (bf16[256,256]{1,0:T(8,128)(2,1)S(1)}, bf16[256,256]{1,0:T(8,128)(2,1)S(1)}, u32[]{:S(2)}, u32[]{:S(2)}) collective-permute-start(bf16[256,256]{1,0:T(8,128)(2,1)S(1)} %get-tuple-element.82), channel_id=1, source_target_pairs={{0,2},{1,3},{2,0},{3,1},{4,6},{5,7},{6,4},{7,5},{8,10},{9,11},{10,... | collective-permute-start | bytes 393224 | tf_op jit(solution)/shard_map/ppermute | solution.py:440
  31.1 8.5 %collective-permute-start.9 = (bf16[256,256]{1,0:T(8,128)(2,1)S(1)}, bf16[256,256]{1,0:T(8,128)(2,1)S(1)}, u32[]{:S(2)}, u32[]{:S(2)}) collective-permute-start(bf16[256,256]{1,0:T(8,128)(2,1)S(1)} %shard_map.194), channel_id=1, source_target_pairs={{0,4},{1,5},{2,6},{3,7},{4,0},{5,1},{6,2},{7,3},{8,12},{9,13},{10,... | collective-permute-start | bytes 393224 | tf_op jit(solution)/shard_map/ppermute | solution.py:425
  32.9 6.8 %copy-start.1 = (bf16[32,2048]{1,0:T(8,128)(2,1)S(1)}, bf16[32,2048]{1,0:T(8,128)(2,1)}, u32[]{:S(2)}) copy-start(bf16[32,2048]{1,0:T(8,128)(2,1)} %basis_out_ref.3) | copy-start | bytes 393220
  37.8 1.9 %collective-permute-start.11 = (bf16[256,256]{1,0:T(8,128)(2,1)S(1)}, bf16[256,256]{1,0:T(8,128)(2,1)S(1)}, u32[]{:S(2)}, u32[]{:S(2)}) collective-permute-start(bf16[256,256]{1,0:T(8,128)(2,1)S(1)} %get-tuple-element.83), channel_id=1, source_target_pairs={{1,2},{3,4},{5,6},{7,8},{9,10},{11,12},{13,14},{15,16},{17,18},{19... | collective-permute-start | bytes 393224 | tf_op jit(solution)/shard_map/ppermute | solution.py:432
  41.5 11.5 %collective-permute-start.14 = (bf16[256,256]{1,0:T(8,128)(2,1)S(1)}, bf16[256,256]{1,0:T(8,128)(2,1)S(1)}, u32[]{:S(2)}, u32[]{:S(2)}) collective-permute-start(bf16[256,256]{1,0:T(8,128)(2,1)S(1)} %get-tuple-element.91.refs_0_), channel_id=1, source_target_pairs={{0,24},{8,0},{16,8},{24,16},{1,25},{9,1},{17,9},{25,17},{2,26},{10... | collective-permute-start | bytes 393224 | tf_op jit(solution)/shard_map/ppermute | solution.py:421
  50.3 5.0 %collective-permute-start.13 = (bf16[256,256]{1,0:T(8,128)(2,1)S(1)}, bf16[256,256]{1,0:T(8,128)(2,1)S(1)}, u32[]{:S(2)}, u32[]{:S(2)}) collective-permute-start(bf16[256,256]{1,0:T(8,128)(2,1)S(1)} %get-tuple-element.91.refs_0_), channel_id=1, source_target_pairs={{0,16},{8,24},{16,0},{24,8},{1,17},{9,25},{17,1},{25,9},{2,18},{10... | collective-permute-start | bytes 393224 | tf_op jit(solution)/shard_map/ppermute | solution.py:421
  51.6 5.9 %collective-permute-start.12 = (bf16[256,256]{1,0:T(8,128)(2,1)S(1)}, bf16[256,256]{1,0:T(8,128)(2,1)S(1)}, u32[]{:S(2)}, u32[]{:S(2)}) collective-permute-start(bf16[256,256]{1,0:T(8,128)(2,1)S(1)} %get-tuple-element.91.refs_0_), channel_id=1, source_target_pairs={{0,8},{8,16},{16,24},{24,0},{1,9},{9,17},{17,25},{25,1},{2,10},{10... | collective-permute-start | bytes 393224 | tf_op jit(solution)/shard_map/ppermute | solution.py:421
  58.2 2.2 %collective-permute-start.15 = (bf16[1280,256]{1,0:T(8,128)(2,1)S(1)}, bf16[1280,256]{1,0:T(8,128)(2,1)S(1)}, u32[]{:S(2)}, u32[]{:S(2)}) collective-permute-start(bf16[1280,256]{1,0:T(8,128)(2,1)S(1)} %shard_map.198), channel_id=1, source_target_pairs={{0,1},{1,0},{2,3},{3,2},{4,5},{5,4},{6,7},{7,6},{8,9},{9,8},{10,11... | collective-permute-start | bytes 1966088 | tf_op jit(solution)/shard_map/ppermute | solution.py:428
  60.6 5.6 %collective-permute-start.16 = (bf16[256,256]{1,0:T(8,128)(2,1)S(1)}, bf16[256,256]{1,0:T(8,128)(2,1)S(1)}, u32[]{:S(2)}, u32[]{:S(2)}) collective-permute-start(bf16[256,256]{1,0:T(8,128)(2,1)S(1)} %get-tuple-element.94), channel_id=1, source_target_pairs={{0,2},{1,3},{2,0},{3,1},{4,6},{5,7},{6,4},{7,5},{8,10},{9,11},{10,... | collective-permute-start | bytes 393224 | tf_op jit(solution)/shard_map/ppermute | solution.py:440
  60.7 8.7 %collective-permute-start.19 = (bf16[256,256]{1,0:T(8,128)(2,1)S(1)}, bf16[256,256]{1,0:T(8,128)(2,1)S(1)}, u32[]{:S(2)}, u32[]{:S(2)}) collective-permute-start(bf16[256,256]{1,0:T(8,128)(2,1)S(1)} %get-tuple-element.99), channel_id=1, source_target_pairs={{1,2},{3,4},{5,6},{7,8},{9,10},{11,12},{13,14},{15,16},{17,18},{19... | collective-permute-start | bytes 393224 | tf_op jit(solution)/shard_map/ppermute | solution.py:432
  61.4 13.0 %collective-permute-start.18 = (bf16[256,256]{1,0:T(8,128)(2,1)S(1)}, bf16[256,256]{1,0:T(8,128)(2,1)S(1)}, u32[]{:S(2)}, u32[]{:S(2)}) collective-permute-start(bf16[256,256]{1,0:T(8,128)(2,1)S(1)} %get-tuple-element.98), channel_id=1, source_target_pairs={{0,2},{1,3},{2,0},{3,1},{4,6},{5,7},{6,4},{7,5},{8,10},{9,11},{10,... | collective-permute-start | bytes 393224 | tf_op jit(solution)/shard_map/ppermute | solution.py:440
  66.3 9.1 %collective-permute-start.17 = (bf16[256,256]{1,0:T(8,128)(2,1)S(1)}, bf16[256,256]{1,0:T(8,128)(2,1)S(1)}, u32[]{:S(2)}, u32[]{:S(2)}) collective-permute-start(bf16[256,256]{1,0:T(8,128)(2,1)S(1)} %shard_map.200), channel_id=1, source_target_pairs={{0,4},{1,5},{2,6},{3,7},{4,0},{5,1},{6,2},{7,3},{8,12},{9,13},{10,... | collective-permute-start | bytes 393224 | tf_op jit(solution)/shard_map/ppermute | solution.py:425

commit v6 on v5

--- a/solution.py
+++ b/solution.py
@@ -447,8 +447,11 @@
             own, cross = lax.optimization_barrier((own, cross))
         return own, to_partner(passed), to_partner(direct), keep, sent, cross if later else to_chip(cross)
 
-    def second_step(own, came, direct, keep, sent, cross):
+    def second_step(own, came, direct, keep, sent, cross, later):
         sums = call(pair_sum_kernel, [jax.ShapeDtypeStruct((share, ens), BF16)] * (heights // 2 - 1), keep, came)
+        if later:
+            sums, cross = lax.optimization_barrier((sums, cross))
+            cross = to_chip(cross)
         return [to_height(part, 2 * (d + 1)) for d, part in enumerate(sums)] + [own, direct, sent, cross]
 
     def row_coeffs(coeff):
@@ -510,19 +513,17 @@
         scratch_shapes=scratch,
     )
     came, high = lax.optimization_barrier((came, high))
-    outer = second_step(own_part, came, direct, keep, sent, cross)
+    outer = second_step(own_part, came, direct, keep, sent, cross, True)
     shift, scale, rest, scale_mid = call(
         prepare_first_kernel, [full] * 4, low, high, own, other, slip, state, numbers, near, rounded
     )
-    shift, cross = lax.optimization_barrier((shift, cross))
-    outer[-1] = to_chip(cross)
     speed, rounded, coeff, pair, cross = call(
         functools.partial(finish_first_kernel, len(outer) - 2),
         [full, half, jax.ShapeDtypeStruct((patches // BS * R, ens), BF16), edge, edge],
         shift, scale, slip, basis_out, basis_in, near, *outer,
     )
     coeffs = row_coeffs(coeff)
-    outer = second_step(*first_step(coeffs, pair, cross, False))
+    outer = second_step(*first_step(coeffs, pair, cross, False), False)
     shift, slip_rest, rest = call(
         prepare_second_kernel, [full] * 3,
         slip, state, speed, rest, scale_mid, numbers, near, rounded,

time: 78.4 us -> 72.7 us (0.927)
  starting transfers between devices: 30.5 us -> 26.3 us
  waiting for transfers between devices: 18.7 us -> 17.2 us
    ppermute x6, starting transfers between devices: 14.6 us -> 8.98 us  [to_row(): lax.ppermute(array, 'row', [(i, (i + d) % row_count) for i in range(row_c...]
    ppermute x5, starting transfers between devices: 7.91 us -> 9.3 us  [to_height(): return lax.ppermute(array, 'col', pairs)]
    ppermute x4, waiting for transfers between devices: 7.03 us -> 5.9 us  [to_partner(): return lax.ppermute(array, 'col', pairs)]
  transfers between devices with their start and end apart: 20 -> 20, of which waited for: 11 -> 10; matrix products, arithmetic and copies ran while one was open for 4% -> 5% of each run, Pallas kernels for 22% -> 24%
where the time goes in v6:
time: 72.7 us; the launch traced here: 72.3 us
  starting transfers between devices  26.3 us (36%)
  Pallas kernels  24.5 us (34%)
  waiting for transfers between devices  17.2 us (24%)
  other arithmetic  3.28 us (5%)
  between operations  0.87 us (1%)
    pallas_call x17, Pallas kernels, call(): pl.pallas_call(kernel, in_specs=specs or [VMEM] * len(operands), out_shap...  24.5 us
    ppermute x5, starting transfers between devices, to_height(): return lax.ppermute(array, 'col', pairs)  9.3 us
    ppermute x6, starting transfers between devices, to_row(): lax.ppermute(array, 'row', [(i, (i + d) % row_count) for i in range(row_c...  8.98 us
    ppermute x6, waiting for transfers between devices, to_row(): lax.ppermute(array, 'row', [(i, (i + d) % row_count) for i in range(row_c...  7.31 us
    ppermute x4, starting transfers between devices, to_partner(): return lax.ppermute(array, 'col', pairs)  6.03 us
    ppermute x4, waiting for transfers between devices, to_partner(): return lax.ppermute(array, 'col', pairs)  5.9 us
    select_n x1, other arithmetic, masked_coupling(): jnp.where(keep, matrix, jnp.zeros((), BF16)).reshape(sources, rows, width)  3.28 us
    ppermute x3, waiting for transfers between devices, to_core(): lax.ppermute(array, 'col', [(2 * z + k, 2 * z + 1 - k) for z in range(hei...  2.16 us
  transfers between devices with their start and end apart: 20, of which 10 were waited for; matrix products, arithmetic and copies ran while one was open for 5% of the time, Pallas kernels for 24%

profile of v6, /device:TPU:0, one launch (start us, length us, event | category | flops | bytes accessed | tf_op | source)
XLA Modules:
  0.0 72.3 jit_solution(438866834908634247)
XLA Ops:
  0.6 1.0 %shard_map.185 = (f32[4,64,256]{2,1,0:T(8,128)S(1)}, bf16[128,512]{1,0:T(8,128)(2,1)S(1)}) custom-call(s32[4,8,64]{2,1,0:T(8,128)} %bitcast.28, bf16[128,256]{1,0:T(8,128)(2,1)} %now_hbm.1, bf16[128,256]{1,0:T(8,128)(2,1)} %rate_hbm.1), custom_call_target="tpu_custom_call" | custom-call | tf_op jit(solution)/shard_map/pallas_call | solution.py:32
  1.6 5.1 %collective-permute-start.2 = (bf16[128,512]{1,0:T(8,128)(2,1)S(1)}, bf16[128,512]{1,0:T(8,128)(2,1)S(1)}, u32[]{:S(2)}, u32[]{:S(2)}) collective-permute-start(bf16[128,512]{1,0:T(8,128)(2,1)S(1)} %get-tuple-element.69.refs_0_), channel_id=1, source_target_pairs={{0,6},{1,7},{2,0},{3,1},{4,2},{5,3},{6,4},{7,5},{8,14},{9,15},{10,... | collective-permute-start | bytes 393224 | tf_op jit(solution)/shard_map/ppermute | solution.py:425
  6.7 1.0 %collective-permute-start = (bf16[128,512]{1,0:T(8,128)(2,1)S(1)}, bf16[128,512]{1,0:T(8,128)(2,1)S(1)}, u32[]{:S(2)}, u32[]{:S(2)}) collective-permute-start(bf16[128,512]{1,0:T(8,128)(2,1)S(1)} %get-tuple-element.69.refs_0_), channel_id=1, source_target_pairs={{0,2},{1,3},{2,4},{3,5},{4,6},{5,7},{6,0},{7,1},{8,10},{9,11},{10,... | collective-permute-start | bytes 393224 | tf_op jit(solution)/shard_map/ppermute | solution.py:425
  7.7 0.1 lt.21
  7.8 3.3 %fusion.matrix_ref = bf16[4,2048,256]{2,1,0:T(8,128)(2,1)S(1)} fusion(bf16[2048,4,256]{2,1,0:T(4,128)(2,1)} %param.29, f32[4,64,256]{2,1,0:T(8,128)S(1)} %get-tuple-element.51, f32[2048]{0:T(1024)S(1)} %lt.21), kind=kLoop, calls=%fused_computation.1 | loop fusion | flops 4194304 | bytes 8658944 | tf_op jit(solution)/shard_map/jit(_where)/select_n | solution.py:387
  11.1 0.3 shard_map.186
  11.5 2.5 %collective-permute-start.5 = (bf16[256,256]{1,0:T(8,128)(2,1)S(1)}, bf16[256,256]{1,0:T(8,128)(2,1)S(1)}, u32[]{:S(2)}, u32[]{:S(2)}) collective-permute-start(bf16[256,256]{1,0:T(8,128)(2,1)S(1)} %get-tuple-element.58.refs_9_.refs_0_), channel_id=1, source_target_pairs={{0,24},{8,0},{16,8},{24,16},{1,25},{9,1},{17,9},{25,17},{2,26},{10... | collective-permute-start | bytes 393224 | tf_op jit(solution)/shard_map/ppermute | solution.py:421
  13.9 0.5 collective-permute-start.4
  14.5 0.0 collective-permute-done.2.refs_3_
  14.5 0.6 collective-permute-start.3
  15.1 3.7 %shard_map.187 = (f32[1024,8]{1,0:T(8,128)S(1)}, bf16[1024,1024]{1,0:T(8,128)(2,1)S(1)}) custom-call(f32[1,2048]{1,0:T(1,128)} %bitcast.14, f32[1,2048]{1,0:T(1,128)} %bitcast.16, f32[1,2048]{1,0:T(1,128)} %bitcast.18, f32[1,2048]{1,0:T(1,128)} %bitcast.20, f32[1,2048]{1,0:T(1,128)} %bitcast.22, f32[1,2048]{1,0:T(1,128)} %bitcast.24, s32[1,2048]{1,0:T(1,128)} %bitcast.26, ...), custom_call_target="tpu_custom_call" | custom-call | tf_op jit(solution)/shard_map/pallas_call | solution.py:32
  18.7 0.0 collective-permute-done.1.refs_2_
  18.8 2.3 %collective-permute-done.4.refs_2_ = bf16[256,256]{1,0:T(8,128)(2,1)S(1)} collective-permute-done((bf16[256,256]{1,0:T(8,128)(2,1)S(1)}, bf16[256,256]{1,0:T(8,128)(2,1)S(1)}, u32[]{:S(2)}, u32[]{:S(2)}) %collective-permute-start.4) | collective-permute-done | bytes 131104 | tf_op jit(solution)/shard_map/ppermute | solution.py:421
  21.1 0.7 shard_map.189
  21.8 0.1 collective-permute-start.6
  22.0 0.6 collective-permute-start.8
  22.5 0.7 shard_map.188.kept_ref
  23.2 0.8 %collective-permute-done.6.sent_ref.refs_3_ = bf16[1280,256]{1,0:T(8,128)(2,1)S(1)} collective-permute-done((bf16[1280,256]{1,0:T(8,128)(2,1)S(1)}, bf16[1280,256]{1,0:T(8,128)(2,1)S(1)}, u32[]{:S(2)}, u32[]{:S(2)}) %collective-permute-start.6) | collective-permute-done | bytes 655392 | tf_op jit(solution)/shard_map/ppermute | solution.py:428
  24.0 0.3 shard_map.190
  24.3 2.5 %collective-permute-start.7 = (bf16[256,256]{1,0:T(8,128)(2,1)S(1)}, bf16[256,256]{1,0:T(8,128)(2,1)S(1)}, u32[]{:S(2)}, u32[]{:S(2)}) collective-permute-start(bf16[256,256]{1,0:T(8,128)(2,1)S(1)} %get-tuple-element.66), channel_id=1, source_target_pairs={{0,2},{1,3},{2,0},{3,1},{4,6},{5,7},{6,4},{7,5},{8,10},{9,11},{10,... | collective-permute-start | bytes 393224 | tf_op jit(solution)/shard_map/ppermute | solution.py:440
  26.8 0.1 collective-permute-start.10
  26.9 3.7 %shard_map.191 = (f32[2048,8]{1,0:T(8,128)S(1)}, bf16[1024,1024]{1,0:T(8,128)(2,1)S(1)}, bf16[3,2048,256]{2,1,0:T(8,128)(2,1)S(1)}, f32[2048,256]{1,0:T(8,128)S(1)}) custom-call(f32[1,2048]{1,0:T(1,128)} %bitcast.15, f32[1,2048]{1,0:T(1,128)} %bitcast.17, f32[1,2048]{1,0:T(1,128)} %bitcast.19, f32[1,2048]{1,0:T(1,128)} %bitcast.21, f32[1,2048]{1,0:T(1,128)} %bitcast.23, ...), custom_call_target="tpu_custom_call" | custom-call | tf_op jit(solution)/shard_map/pallas_call | solution.py:32
  30.6 0.5 collective-permute-done.7.came_ref
  31.1 1.7 %collective-permute-start.9 = (bf16[256,256]{1,0:T(8,128)(2,1)S(1)}, bf16[256,256]{1,0:T(8,128)(2,1)S(1)}, u32[]{:S(2)}, u32[]{:S(2)}) collective-permute-start(bf16[256,256]{1,0:T(8,128)(2,1)S(1)} %shard_map.194), channel_id=1, source_target_pairs={{0,4},{1,5},{2,6},{3,7},{4,0},{5,1},{6,2},{7,3},{8,12},{9,13},{10,... | collective-permute-start | bytes 393224 | tf_op jit(solution)/shard_map/ppermute | solution.py:425
  32.9 0.7 collective-permute-start.11
  33.5 0.0 copy-start.1
  33.6 4.9 %shard_map.193 = (f32[2048,256]{1,0:T(8,128)S(1)}, f32[2048,256]{1,0:T(8,128)S(1)}, f32[2048,256]{1,0:T(8,128)S(1)}, f32[2048,256]{1,0:T(8,128)S(1)}) custom-call(bf16[1024,1024]{1,0:T(8,128)(2,1)S(1)} %get-tuple-element.65.low_ref, bf16[1024,1024]{1,0:T(8,128)(2,1)S(1)} %get-tuple-element.68.high_ref, bf16[512,512]{1,0:T(8,128)(2,1)S(1)} %shard_map.192.own_ref, ...), custom_call_target="tpu_custom_call" | custom-call | tf_op jit(solution)/shard_map/pallas_call | solution.py:32
  38.5 1.8 %collective-permute-done.9.refs_0_ = bf16[256,256]{1,0:T(8,128)(2,1)S(1)} collective-permute-done((bf16[256,256]{1,0:T(8,128)(2,1)S(1)}, bf16[256,256]{1,0:T(8,128)(2,1)S(1)}, u32[]{:S(2)}, u32[]{:S(2)}) %collective-permute-start.9) | collective-permute-done | bytes 131104 | tf_op jit(solution)/shard_map/ppermute | solution.py:425
  40.4 1.9 %shard_map.195 = (f32[2048,256]{1,0:T(8,128)S(1)}, bf16[2048,256]{1,0:T(8,128)(2,1)S(1)}, bf16[256,256]{1,0:T(8,128)(2,1)S(1)}, bf16[256,256]{1,0:T(8,128)(2,1)S(1)}, bf16[256,256]{1,0:T(8,128)(2,1)S(1)}) custom-call(f32[2048,256]{1,0:T(8,128)S(1)} %get-tuple-element.76.shift_ref, f32[2048,256]{1,0:T(8,128)S(1)} %get-tuple-element.77.scale_ref, ...), custom_call_target="tpu_custom_call" | custom-call | tf_op jit(solution)/shard_map/pallas_call | solution.py:32
  42.2 3.2 %collective-permute-start.14 = (bf16[256,256]{1,0:T(8,128)(2,1)S(1)}, bf16[256,256]{1,0:T(8,128)(2,1)S(1)}, u32[]{:S(2)}, u32[]{:S(2)}) collective-permute-start(bf16[256,256]{1,0:T(8,128)(2,1)S(1)} %get-tuple-element.91.refs_0_), channel_id=1, source_target_pairs={{0,24},{8,0},{16,8},{24,16},{1,25},{9,1},{17,9},{25,17},{2,26},{10... | collective-permute-start | bytes 393224 | tf_op jit(solution)/shard_map/ppermute | solution.py:421
  45.4 1.3 %collective-permute-start.13 = (bf16[256,256]{1,0:T(8,128)(2,1)S(1)}, bf16[256,256]{1,0:T(8,128)(2,1)S(1)}, u32[]{:S(2)}, u32[]{:S(2)}) collective-permute-start(bf16[256,256]{1,0:T(8,128)(2,1)S(1)} %get-tuple-element.91.refs_0_), channel_id=1, source_target_pairs={{0,16},{8,24},{16,0},{24,8},{1,17},{9,25},{17,1},{25,9},{2,18},{10... | collective-permute-start | bytes 393224 | tf_op jit(solution)/shard_map/ppermute | solution.py:421
  46.7 0.9 %collective-permute-start.12 = (bf16[256,256]{1,0:T(8,128)(2,1)S(1)}, bf16[256,256]{1,0:T(8,128)(2,1)S(1)}, u32[]{:S(2)}, u32[]{:S(2)}) collective-permute-start(bf16[256,256]{1,0:T(8,128)(2,1)S(1)} %get-tuple-element.91.refs_0_), channel_id=1, source_target_pairs={{0,8},{8,16},{16,24},{24,0},{1,9},{9,17},{17,25},{25,1},{2,10},{10... | collective-permute-start | bytes 393224 | tf_op jit(solution)/shard_map/ppermute | solution.py:421
  47.6 2.0 %collective-permute-done.14.refs_3_ = bf16[256,256]{1,0:T(8,128)(2,1)S(1)} collective-permute-done((bf16[256,256]{1,0:T(8,128)(2,1)S(1)}, bf16[256,256]{1,0:T(8,128)(2,1)S(1)}, u32[]{:S(2)}, u32[]{:S(2)}) %collective-permute-start.14) | collective-permute-done | bytes 131104 | tf_op jit(solution)/shard_map/ppermute | solution.py:421
  49.6 1.9 %collective-permute-done.13.refs_2_ = bf16[256,256]{1,0:T(8,128)(2,1)S(1)} collective-permute-done((bf16[256,256]{1,0:T(8,128)(2,1)S(1)}, bf16[256,256]{1,0:T(8,128)(2,1)S(1)}, u32[]{:S(2)}, u32[]{:S(2)}) %collective-permute-start.13) | collective-permute-done | bytes 131104 | tf_op jit(solution)/shard_map/ppermute | solution.py:421
  51.5 1.1 %collective-permute-done.12.refs_1_ = bf16[256,256]{1,0:T(8,128)(2,1)S(1)} collective-permute-done((bf16[256,256]{1,0:T(8,128)(2,1)S(1)}, bf16[256,256]{1,0:T(8,128)(2,1)S(1)}, u32[]{:S(2)}, u32[]{:S(2)}) %collective-permute-start.12) | collective-permute-done | bytes 131104 | tf_op jit(solution)/shard_map/ppermute | solution.py:421
  52.5 0.7 shard_map.198
  53.3 0.1 collective-permute-start.15
  53.3 0.7 shard_map.197.kept_ref
  54.1 1.4 %collective-permute-done.15.sent_ref.refs_3_ = bf16[1280,256]{1,0:T(8,128)(2,1)S(1)} collective-permute-done((bf16[1280,256]{1,0:T(8,128)(2,1)S(1)}, bf16[1280,256]{1,0:T(8,128)(2,1)S(1)}, u32[]{:S(2)}, u32[]{:S(2)}) %collective-permute-start.15) | collective-permute-done | bytes 655392 | tf_op jit(solution)/shard_map/ppermute | solution.py:428
  55.4 0.3 shard_map.199
  55.7 0.5 collective-permute-start.16
  56.2 0.7 collective-permute-start.19
  56.9 2.9 %collective-permute-start.18 = (bf16[256,256]{1,0:T(8,128)(2,1)S(1)}, bf16[256,256]{1,0:T(8,128)(2,1)S(1)}, u32[]{:S(2)}, u32[]{:S(2)}) collective-permute-start(bf16[256,256]{1,0:T(8,128)(2,1)S(1)} %get-tuple-element.98), channel_id=1, source_target_pairs={{0,2},{1,3},{2,0},{3,1},{4,6},{5,7},{6,4},{7,5},{8,10},{9,11},{10,... | collective-permute-start | bytes 393224 | tf_op jit(solution)/shard_map/ppermute | solution.py:440
  59.8 1.5 %collective-permute-done.16.came_ref = bf16[256,256]{1,0:T(8,128)(2,1)S(1)} collective-permute-done((bf16[256,256]{1,0:T(8,128)(2,1)S(1)}, bf16[256,256]{1,0:T(8,128)(2,1)S(1)}, u32[]{:S(2)}, u32[]{:S(2)}) %collective-permute-start.16) | collective-permute-done | bytes 131104 | tf_op jit(solution)/shard_map/ppermute | solution.py:440
  61.4 1.5 %collective-permute-start.17 = (bf16[256,256]{1,0:T(8,128)(2,1)S(1)}, bf16[256,256]{1,0:T(8,128)(2,1)S(1)}, u32[]{:S(2)}, u32[]{:S(2)}) collective-permute-start(bf16[256,256]{1,0:T(8,128)(2,1)S(1)} %shard_map.200), channel_id=1, source_target_pairs={{0,4},{1,5},{2,6},{3,7},{4,0},{5,1},{6,2},{7,3},{8,12},{9,13},{10,... | collective-permute-start | bytes 393224 | tf_op jit(solution)/shard_map/ppermute | solution.py:425
  62.8 3.0 %shard_map.196 = (f32[2048,256]{1,0:T(8,128)S(1)}, f32[2048,256]{1,0:T(8,128)S(1)}, f32[2048,256]{1,0:T(8,128)S(1)}) custom-call(f32[2048,256]{1,0:T(8,128)S(1)} %copy-done, f32[2048,256]{1,0:T(8,128)S(1)} %get-tuple-element.64.state_ref, f32[2048,256]{1,0:T(8,128)S(1)} %get-tuple-element.84.speed_ref, f32[2048,256]{1,0:T(8,128)S(1)} %get-tuple-element.85.part_ref, ...), custom_call_target="tpu_custom_call" | custom-call | tf_op jit(solution)/shard_map/pallas_call | solution.py:32
  65.9 3.9 %collective-permute-done.18.refs_2_ = bf16[256,256]{1,0:T(8,128)(2,1)S(1)} collective-permute-done((bf16[256,256]{1,0:T(8,128)(2,1)S(1)}, bf16[256,256]{1,0:T(8,128)(2,1)S(1)}, u32[]{:S(2)}, u32[]{:S(2)}) %collective-permute-start.18) | collective-permute-done | bytes 131104 | tf_op jit(solution)/shard_map/ppermute | solution.py:440
  69.7 2.6 %shard_map.201 = (f32[2048,256]{1,0:T(8,128)}, f32[2048,256]{1,0:T(8,128)}) custom-call(f32[2048,256]{1,0:T(8,128)S(1)} %get-tuple-element.88.shift_ref, f32[2048,256]{1,0:T(8,128)S(1)} %get-tuple-element.86.scale_ref, f32[2048,256]{1,0:T(8,128)S(1)} %get-tuple-element.89.rest_ref, f32[2048,256]{1,0:T(8,128)S(1)} %get-tuple-element.90.slip_rest_ref, ...), custom_call_target="tpu_custom_call" | custom-call | tf_op jit(solution)/shard_map/pallas_call | solution.py:32
  (19 shorter events, 0.2 us)
Async XLA Ops:
  1.6 12.8 %collective-permute-start.2 = (bf16[128,512]{1,0:T(8,128)(2,1)S(1)}, bf16[128,512]{1,0:T(8,128)(2,1)S(1)}, u32[]{:S(2)}, u32[]{:S(2)}) collective-permute-start(bf16[128,512]{1,0:T(8,128)(2,1)S(1)} %get-tuple-element.69.refs_0_), channel_id=1, source_target_pairs={{0,6},{1,7},{2,0},{3,1},{4,2},{5,3},{6,4},{7,5},{8,14},{9,15},{10,... | collective-permute-start | bytes 393224 | tf_op jit(solution)/shard_map/ppermute | solution.py:425
  6.7 12.0 %collective-permute-start.1 = (bf16[128,512]{1,0:T(8,128)(2,1)S(1)}, bf16[128,512]{1,0:T(8,128)(2,1)S(1)}, u32[]{:S(2)}, u32[]{:S(2)}) collective-permute-start(bf16[128,512]{1,0:T(8,128)(2,1)S(1)} %get-tuple-element.69.refs_0_), channel_id=1, source_target_pairs={{0,4},{1,5},{2,6},{3,7},{4,0},{5,1},{6,2},{7,3},{8,12},{9,13},{10,... | collective-permute-start | bytes 393224 | tf_op jit(solution)/shard_map/ppermute | solution.py:425
  6.7 12.0 %collective-permute-start = (bf16[128,512]{1,0:T(8,128)(2,1)S(1)}, bf16[128,512]{1,0:T(8,128)(2,1)S(1)}, u32[]{:S(2)}, u32[]{:S(2)}) collective-permute-start(bf16[128,512]{1,0:T(8,128)(2,1)S(1)} %get-tuple-element.69.refs_0_), channel_id=1, source_target_pairs={{0,2},{1,3},{2,4},{3,5},{4,6},{5,7},{6,0},{7,1},{8,10},{9,11},{10,... | collective-permute-start | bytes 393224 | tf_op jit(solution)/shard_map/ppermute | solution.py:425
  7.8 3.3 %copy-start = (f32[2048,256]{1,0:T(8,128)S(1)}, f32[2048,256]{1,0:T(8,128)}, u32[]{:S(2)}) copy-start(f32[2048,256]{1,0:T(8,128)} %slip_ref.3) | copy-start | bytes 6291460
  7.8 3.3 %copy-start.2 = (bf16[32,2048]{1,0:T(8,128)(2,1)S(1)}, bf16[32,2048]{1,0:T(8,128)(2,1)}, u32[]{:S(2)}) copy-start(bf16[32,2048]{1,0:T(8,128)(2,1)} %basis_in_ref.1) | copy-start | bytes 393220
  11.5 7.3 %collective-permute-start.5 = (bf16[256,256]{1,0:T(8,128)(2,1)S(1)}, bf16[256,256]{1,0:T(8,128)(2,1)S(1)}, u32[]{:S(2)}, u32[]{:S(2)}) collective-permute-start(bf16[256,256]{1,0:T(8,128)(2,1)S(1)} %get-tuple-element.58.refs_9_.refs_0_), channel_id=1, source_target_pairs={{0,24},{8,0},{16,8},{24,16},{1,25},{9,1},{17,9},{25,17},{2,26},{10... | collective-permute-start | bytes 393224 | tf_op jit(solution)/shard_map/ppermute | solution.py:421
  13.9 7.2 %collective-permute-start.4 = (bf16[256,256]{1,0:T(8,128)(2,1)S(1)}, bf16[256,256]{1,0:T(8,128)(2,1)S(1)}, u32[]{:S(2)}, u32[]{:S(2)}) collective-permute-start(bf16[256,256]{1,0:T(8,128)(2,1)S(1)} %get-tuple-element.58.refs_9_.refs_0_), channel_id=1, source_target_pairs={{0,16},{8,24},{16,0},{24,8},{1,17},{9,25},{17,1},{25,9},{2,18},{10... | collective-permute-start | bytes 393224 | tf_op jit(solution)/shard_map/ppermute | solution.py:421
  14.5 6.7 %collective-permute-start.3 = (bf16[256,256]{1,0:T(8,128)(2,1)S(1)}, bf16[256,256]{1,0:T(8,128)(2,1)S(1)}, u32[]{:S(2)}, u32[]{:S(2)}) collective-permute-start(bf16[256,256]{1,0:T(8,128)(2,1)S(1)} %get-tuple-element.58.refs_9_.refs_0_), channel_id=1, source_target_pairs={{0,8},{8,16},{16,24},{24,0},{1,9},{9,17},{17,25},{25,1},{2,10},{10... | collective-permute-start | bytes 393224 | tf_op jit(solution)/shard_map/ppermute | solution.py:421
  21.8 2.2 %collective-permute-start.6 = (bf16[1280,256]{1,0:T(8,128)(2,1)S(1)}, bf16[1280,256]{1,0:T(8,128)(2,1)S(1)}, u32[]{:S(2)}, u32[]{:S(2)}) collective-permute-start(bf16[1280,256]{1,0:T(8,128)(2,1)S(1)} %shard_map.189), channel_id=1, source_target_pairs={{0,1},{1,0},{2,3},{3,2},{4,5},{5,4},{6,7},{7,6},{8,9},{9,8},{10,11... | collective-permute-start | bytes 1966088 | tf_op jit(solution)/shard_map/ppermute | solution.py:428
  22.0 11.6 %collective-permute-start.8 = (bf16[512,512]{1,0:T(8,128)(2,1)S(1)}, bf16[512,512]{1,0:T(8,128)(2,1)S(1)}, u32[]{:S(2)}, u32[]{:S(2)}) collective-permute-start(bf16[512,512]{1,0:T(8,128)(2,1)S(1)} %shard_map.192.own_ref), channel_id=1, source_target_pairs={{0,1},{1,0},{2,3},{3,2},{4,5},{5,4},{6,7},{7,6},{8,9},{9,8},{10,11... | collective-permute-start | bytes 1572872 | tf_op jit(solution)/shard_map/ppermute | solution.py:428
  24.3 6.8 %collective-permute-start.7 = (bf16[256,256]{1,0:T(8,128)(2,1)S(1)}, bf16[256,256]{1,0:T(8,128)(2,1)S(1)}, u32[]{:S(2)}, u32[]{:S(2)}) collective-permute-start(bf16[256,256]{1,0:T(8,128)(2,1)S(1)} %get-tuple-element.66), channel_id=1, source_target_pairs={{0,2},{1,3},{2,0},{3,1},{4,6},{5,7},{6,4},{7,5},{8,10},{9,11},{10,... | collective-permute-start | bytes 393224 | tf_op jit(solution)/shard_map/ppermute | solution.py:440
  26.8 11.7 %collective-permute-start.10 = (bf16[256,256]{1,0:T(8,128)(2,1)S(1)}, bf16[256,256]{1,0:T(8,128)(2,1)S(1)}, u32[]{:S(2)}, u32[]{:S(2)}) collective-permute-start(bf16[256,256]{1,0:T(8,128)(2,1)S(1)} %get-tuple-element.82), channel_id=1, source_target_pairs={{0,2},{1,3},{2,0},{3,1},{4,6},{5,7},{6,4},{7,5},{8,10},{9,11},{10,... | collective-permute-start | bytes 393224 | tf_op jit(solution)/shard_map/ppermute | solution.py:440
  31.1 9.2 %collective-permute-start.9 = (bf16[256,256]{1,0:T(8,128)(2,1)S(1)}, bf16[256,256]{1,0:T(8,128)(2,1)S(1)}, u32[]{:S(2)}, u32[]{:S(2)}) collective-permute-start(bf16[256,256]{1,0:T(8,128)(2,1)S(1)} %shard_map.194), channel_id=1, source_target_pairs={{0,4},{1,5},{2,6},{3,7},{4,0},{5,1},{6,2},{7,3},{8,12},{9,13},{10,... | collective-permute-start | bytes 393224 | tf_op jit(solution)/shard_map/ppermute | solution.py:425
  32.9 7.5 %collective-permute-start.11 = (bf16[256,256]{1,0:T(8,128)(2,1)S(1)}, bf16[256,256]{1,0:T(8,128)(2,1)S(1)}, u32[]{:S(2)}, u32[]{:S(2)}) collective-permute-start(bf16[256,256]{1,0:T(8,128)(2,1)S(1)} %get-tuple-element.83), channel_id=1, source_target_pairs={{1,2},{3,4},{5,6},{7,8},{9,10},{11,12},{13,14},{15,16},{17,18},{19... | collective-permute-start | bytes 393224 | tf_op jit(solution)/shard_map/ppermute | solution.py:432
  33.5 6.8 %copy-start.1 = (bf16[32,2048]{1,0:T(8,128)(2,1)S(1)}, bf16[32,2048]{1,0:T(8,128)(2,1)}, u32[]{:S(2)}) copy-start(bf16[32,2048]{1,0:T(8,128)(2,1)} %basis_out_ref.3) | copy-start | bytes 393220
  42.2 7.4 %collective-permute-start.14 = (bf16[256,256]{1,0:T(8,128)(2,1)S(1)}, bf16[256,256]{1,0:T(8,128)(2,1)S(1)}, u32[]{:S(2)}, u32[]{:S(2)}) collective-permute-start(bf16[256,256]{1,0:T(8,128)(2,1)S(1)} %get-tuple-element.91.refs_0_), channel_id=1, source_target_pairs={{0,24},{8,0},{16,8},{24,16},{1,25},{9,1},{17,9},{25,17},{2,26},{10... | collective-permute-start | bytes 393224 | tf_op jit(solution)/shard_map/ppermute | solution.py:421
  45.4 6.1 %collective-permute-start.13 = (bf16[256,256]{1,0:T(8,128)(2,1)S(1)}, bf16[256,256]{1,0:T(8,128)(2,1)S(1)}, u32[]{:S(2)}, u32[]{:S(2)}) collective-permute-start(bf16[256,256]{1,0:T(8,128)(2,1)S(1)} %get-tuple-element.91.refs_0_), channel_id=1, source_target_pairs={{0,16},{8,24},{16,0},{24,8},{1,17},{9,25},{17,1},{25,9},{2,18},{10... | collective-permute-start | bytes 393224 | tf_op jit(solution)/shard_map/ppermute | solution.py:421
  46.7 5.9 %collective-permute-start.12 = (bf16[256,256]{1,0:T(8,128)(2,1)S(1)}, bf16[256,256]{1,0:T(8,128)(2,1)S(1)}, u32[]{:S(2)}, u32[]{:S(2)}) collective-permute-start(bf16[256,256]{1,0:T(8,128)(2,1)S(1)} %get-tuple-element.91.refs_0_), channel_id=1, source_target_pairs={{0,8},{8,16},{16,24},{24,0},{1,9},{9,17},{17,25},{25,1},{2,10},{10... | collective-permute-start | bytes 393224 | tf_op jit(solution)/shard_map/ppermute | solution.py:421
  53.3 2.2 %collective-permute-start.15 = (bf16[1280,256]{1,0:T(8,128)(2,1)S(1)}, bf16[1280,256]{1,0:T(8,128)(2,1)S(1)}, u32[]{:S(2)}, u32[]{:S(2)}) collective-permute-start(bf16[1280,256]{1,0:T(8,128)(2,1)S(1)} %shard_map.198), channel_id=1, source_target_pairs={{0,1},{1,0},{2,3},{3,2},{4,5},{5,4},{6,7},{7,6},{8,9},{9,8},{10,11... | collective-permute-start | bytes 1966088 | tf_op jit(solution)/shard_map/ppermute | solution.py:428
  55.7 5.6 %collective-permute-start.16 = (bf16[256,256]{1,0:T(8,128)(2,1)S(1)}, bf16[256,256]{1,0:T(8,128)(2,1)S(1)}, u32[]{:S(2)}, u32[]{:S(2)}) collective-permute-start(bf16[256,256]{1,0:T(8,128)(2,1)S(1)} %get-tuple-element.94), channel_id=1, source_target_pairs={{0,2},{1,3},{2,0},{3,1},{4,6},{5,7},{6,4},{7,5},{8,10},{9,11},{10,... | collective-permute-start | bytes 393224 | tf_op jit(solution)/shard_map/ppermute | solution.py:440
  56.2 9.6 %collective-permute-start.19 = (bf16[256,256]{1,0:T(8,128)(2,1)S(1)}, bf16[256,256]{1,0:T(8,128)(2,1)S(1)}, u32[]{:S(2)}, u32[]{:S(2)}) collective-permute-start(bf16[256,256]{1,0:T(8,128)(2,1)S(1)} %get-tuple-element.99), channel_id=1, source_target_pairs={{1,2},{3,4},{5,6},{7,8},{9,10},{11,12},{13,14},{15,16},{17,18},{19... | collective-permute-start | bytes 393224 | tf_op jit(solution)/shard_map/ppermute | solution.py:432
  56.9 12.8 %collective-permute-start.18 = (bf16[256,256]{1,0:T(8,128)(2,1)S(1)}, bf16[256,256]{1,0:T(8,128)(2,1)S(1)}, u32[]{:S(2)}, u32[]{:S(2)}) collective-permute-start(bf16[256,256]{1,0:T(8,128)(2,1)S(1)} %get-tuple-element.98), channel_id=1, source_target_pairs={{0,2},{1,3},{2,0},{3,1},{4,6},{5,7},{6,4},{7,5},{8,10},{9,11},{10,... | collective-permute-start | bytes 393224 | tf_op jit(solution)/shard_map/ppermute | solution.py:440
  61.4 8.4 %collective-permute-start.17 = (bf16[256,256]{1,0:T(8,128)(2,1)S(1)}, bf16[256,256]{1,0:T(8,128)(2,1)S(1)}, u32[]{:S(2)}, u32[]{:S(2)}) collective-permute-start(bf16[256,256]{1,0:T(8,128)(2,1)S(1)} %shard_map.200), channel_id=1, source_target_pairs={{0,4},{1,5},{2,6},{3,7},{4,0},{5,1},{6,2},{7,3},{8,12},{9,13},{10,... | collective-permute-start | bytes 393224 | tf_op jit(solution)/shard_map/ppermute | solution.py:425

commit v7 on v6

--- a/solution.py
+++ b/solution.py
@@ -283,11 +283,11 @@
         shift_ref[at, :] = tau * scale - state * inv_direct
         rest_ref[at, :] = state + (STEP_SIZE * ratio) * jnp.exp((REF_FRICTION - state) * inv_evolution)
 
-    @pl.loop(0, blocks)
+    @pl.loop(0, blocks, unroll=2)
     def _(m):
         block(low_ref, m, m)
 
-    @pl.loop(0, blocks)
+    @pl.loop(0, blocks, unroll=2)
     def _(m):
         block(high_ref, m, blocks + m)
 
@@ -335,7 +335,7 @@
     slip_ref, state_ref, speed_ref, part_ref, scale_ref, numbers_ref, near_ref, rounded_ref,
     shift_ref, slip_rest_ref, rest_ref,
 ):
-    @pl.loop(0, slip_ref.shape[0] // BS)
+    @pl.loop(0, slip_ref.shape[0] // BS, unroll=2)
     def _(n):
         at = rows_at(n, BS)
         numbers = numbers_ref[at, :]

time: 72.7 us -> 72.7 us (level)
  waiting for transfers between devices: 17.2 us -> 18.1 us
  Pallas kernels: 24.5 us -> 23.7 us
    pallas_call x17, Pallas kernels: 24.5 us -> 23.7 us  [call(): pl.pallas_call(kernel, in_specs=specs or [VMEM] * len(operands), out_shap...]
  transfers between devices with their start and end apart: 20 -> 20, of which waited for: 10 -> 10; matrix products, arithmetic and copies ran while one was open for 5% -> 5% of each run, Pallas kernels for 24% -> 23%
where the time goes in v7:
time: 72.7 us; the launch traced here: 72.3 us
  starting transfers between devices  26.3 us (36%)
  Pallas kernels  23.7 us (33%)
  waiting for transfers between devices  18.1 us (25%)
  other arithmetic  3.28 us (5%)
  between operations  0.87 us (1%)
    pallas_call x17, Pallas kernels, call(): pl.pallas_call(kernel, in_specs=specs or [VMEM] * len(operands), out_shap...  23.7 us
    ppermute x5, starting transfers between devices, to_height(): return lax.ppermute(array, 'col', pairs)  9.3 us
    ppermute x6, starting transfers between devices, to_row(): lax.ppermute(array, 'row', [(i, (i + d) % row_count) for i in range(row_c...  8.98 us
    ppermute x6, waiting for transfers between devices, to_row(): lax.ppermute(array, 'row', [(i, (i + d) % row_count) for i in range(row_c...  7.31 us
    ppermute x4, waiting for transfers between devices, to_partner(): return lax.ppermute(array, 'col', pairs)  6.04 us
    ppermute x4, starting transfers between devices, to_partner(): return lax.ppermute(array, 'col', pairs)  6.03 us
    select_n x1, other arithmetic, masked_coupling(): jnp.where(keep, matrix, jnp.zeros((), BF16)).reshape(sources, rows, width)  3.28 us
    ppermute x5, waiting for transfers between devices, to_height(): return lax.ppermute(array, 'col', pairs)  2.57 us
  transfers between devices with their start and end apart: 20, of which 10 were waited for; matrix products, arithmetic and copies ran while one was open for 5% of the time, Pallas kernels for 23%

profile of v7, /device:TPU:0, one launch (start us, length us, event | category | flops | bytes accessed | tf_op | source)
XLA Modules:
  0.0 72.3 jit_solution(17716905335991536808)
XLA Ops:
  0.6 1.0 %shard_map.185 = (f32[4,64,256]{2,1,0:T(8,128)S(1)}, bf16[128,512]{1,0:T(8,128)(2,1)S(1)}) custom-call(s32[4,8,64]{2,1,0:T(8,128)} %bitcast.28, bf16[128,256]{1,0:T(8,128)(2,1)} %now_hbm.1, bf16[128,256]{1,0:T(8,128)(2,1)} %rate_hbm.1), custom_call_target="tpu_custom_call" | custom-call | tf_op jit(solution)/shard_map/pallas_call | solution.py:32
  1.6 5.1 %collective-permute-start.2 = (bf16[128,512]{1,0:T(8,128)(2,1)S(1)}, bf16[128,512]{1,0:T(8,128)(2,1)S(1)}, u32[]{:S(2)}, u32[]{:S(2)}) collective-permute-start(bf16[128,512]{1,0:T(8,128)(2,1)S(1)} %get-tuple-element.69.refs_0_), channel_id=1, source_target_pairs={{0,6},{1,7},{2,0},{3,1},{4,2},{5,3},{6,4},{7,5},{8,14},{9,15},{10,... | collective-permute-start | bytes 393224 | tf_op jit(solution)/shard_map/ppermute | solution.py:425
  6.7 0.0 collective-permute-start.1
  6.7 1.0 %collective-permute-start = (bf16[128,512]{1,0:T(8,128)(2,1)S(1)}, bf16[128,512]{1,0:T(8,128)(2,1)S(1)}, u32[]{:S(2)}, u32[]{:S(2)}) collective-permute-start(bf16[128,512]{1,0:T(8,128)(2,1)S(1)} %get-tuple-element.69.refs_0_), channel_id=1, source_target_pairs={{0,2},{1,3},{2,4},{3,5},{4,6},{5,7},{6,0},{7,1},{8,10},{9,11},{10,... | collective-permute-start | bytes 393224 | tf_op jit(solution)/shard_map/ppermute | solution.py:425
  7.7 0.1 lt.21
  7.8 3.3 %fusion.matrix_ref = bf16[4,2048,256]{2,1,0:T(8,128)(2,1)S(1)} fusion(bf16[2048,4,256]{2,1,0:T(4,128)(2,1)} %param.29, f32[4,64,256]{2,1,0:T(8,128)S(1)} %get-tuple-element.51, f32[2048]{0:T(1024)S(1)} %lt.21), kind=kLoop, calls=%fused_computation.1 | loop fusion | flops 4194304 | bytes 8658944 | tf_op jit(solution)/shard_map/jit(_where)/select_n | solution.py:387
  11.1 0.3 shard_map.186
  11.5 2.5 %collective-permute-start.5 = (bf16[256,256]{1,0:T(8,128)(2,1)S(1)}, bf16[256,256]{1,0:T(8,128)(2,1)S(1)}, u32[]{:S(2)}, u32[]{:S(2)}) collective-permute-start(bf16[256,256]{1,0:T(8,128)(2,1)S(1)} %get-tuple-element.58.refs_9_.refs_0_), channel_id=1, source_target_pairs={{0,24},{8,0},{16,8},{24,16},{1,25},{9,1},{17,9},{25,17},{2,26},{10... | collective-permute-start | bytes 393224 | tf_op jit(solution)/shard_map/ppermute | solution.py:421
  13.9 0.5 collective-permute-start.4
  14.5 0.6 collective-permute-start.3
  15.1 3.7 %shard_map.187 = (f32[1024,8]{1,0:T(8,128)S(1)}, bf16[1024,1024]{1,0:T(8,128)(2,1)S(1)}) custom-call(f32[1,2048]{1,0:T(1,128)} %bitcast.14, f32[1,2048]{1,0:T(1,128)} %bitcast.16, f32[1,2048]{1,0:T(1,128)} %bitcast.18, f32[1,2048]{1,0:T(1,128)} %bitcast.20, f32[1,2048]{1,0:T(1,128)} %bitcast.22, f32[1,2048]{1,0:T(1,128)} %bitcast.24, s32[1,2048]{1,0:T(1,128)} %bitcast.26, ...), custom_call_target="tpu_custom_call" | custom-call | tf_op jit(solution)/shard_map/pallas_call | solution.py:32
  18.7 0.0 collective-permute-done.1.refs_2_
  18.8 2.3 %collective-permute-done.4.refs_2_ = bf16[256,256]{1,0:T(8,128)(2,1)S(1)} collective-permute-done((bf16[256,256]{1,0:T(8,128)(2,1)S(1)}, bf16[256,256]{1,0:T(8,128)(2,1)S(1)}, u32[]{:S(2)}, u32[]{:S(2)}) %collective-permute-start.4) | collective-permute-done | bytes 131104 | tf_op jit(solution)/shard_map/ppermute | solution.py:421
  21.1 0.7 shard_map.189
  21.8 0.1 collective-permute-start.6
  22.0 0.6 collective-permute-start.8
  22.5 0.7 shard_map.188.kept_ref
  23.2 0.8 %collective-permute-done.6.sent_ref.refs_3_ = bf16[1280,256]{1,0:T(8,128)(2,1)S(1)} collective-permute-done((bf16[1280,256]{1,0:T(8,128)(2,1)S(1)}, bf16[1280,256]{1,0:T(8,128)(2,1)S(1)}, u32[]{:S(2)}, u32[]{:S(2)}) %collective-permute-start.6) | collective-permute-done | bytes 655392 | tf_op jit(solution)/shard_map/ppermute | solution.py:428
  24.0 0.3 shard_map.190
  24.3 2.5 %collective-permute-start.7 = (bf16[256,256]{1,0:T(8,128)(2,1)S(1)}, bf16[256,256]{1,0:T(8,128)(2,1)S(1)}, u32[]{:S(2)}, u32[]{:S(2)}) collective-permute-start(bf16[256,256]{1,0:T(8,128)(2,1)S(1)} %get-tuple-element.66), channel_id=1, source_target_pairs={{0,2},{1,3},{2,0},{3,1},{4,6},{5,7},{6,4},{7,5},{8,10},{9,11},{10,... | collective-permute-start | bytes 393224 | tf_op jit(solution)/shard_map/ppermute | solution.py:440
  26.8 0.1 collective-permute-start.10
  26.9 3.7 %shard_map.191 = (f32[2048,8]{1,0:T(8,128)S(1)}, bf16[1024,1024]{1,0:T(8,128)(2,1)S(1)}, bf16[3,2048,256]{2,1,0:T(8,128)(2,1)S(1)}, f32[2048,256]{1,0:T(8,128)S(1)}) custom-call(f32[1,2048]{1,0:T(1,128)} %bitcast.15, f32[1,2048]{1,0:T(1,128)} %bitcast.17, f32[1,2048]{1,0:T(1,128)} %bitcast.19, f32[1,2048]{1,0:T(1,128)} %bitcast.21, f32[1,2048]{1,0:T(1,128)} %bitcast.23, ...), custom_call_target="tpu_custom_call" | custom-call | tf_op jit(solution)/shard_map/pallas_call | solution.py:32
  30.6 0.5 collective-permute-done.7.came_ref
  31.1 1.7 %collective-permute-start.9 = (bf16[256,256]{1,0:T(8,128)(2,1)S(1)}, bf16[256,256]{1,0:T(8,128)(2,1)S(1)}, u32[]{:S(2)}, u32[]{:S(2)}) collective-permute-start(bf16[256,256]{1,0:T(8,128)(2,1)S(1)} %shard_map.194), channel_id=1, source_target_pairs={{0,4},{1,5},{2,6},{3,7},{4,0},{5,1},{6,2},{7,3},{8,12},{9,13},{10,... | collective-permute-start | bytes 393224 | tf_op jit(solution)/shard_map/ppermute | solution.py:425
  32.9 0.7 collective-permute-start.11
  33.5 0.0 copy-start.1
  33.6 4.2 %shard_map.193 = (f32[2048,256]{1,0:T(8,128)S(1)}, f32[2048,256]{1,0:T(8,128)S(1)}, f32[2048,256]{1,0:T(8,128)S(1)}, f32[2048,256]{1,0:T(8,128)S(1)}) custom-call(bf16[1024,1024]{1,0:T(8,128)(2,1)S(1)} %get-tuple-element.65.low_ref, bf16[1024,1024]{1,0:T(8,128)(2,1)S(1)} %get-tuple-element.68.high_ref, bf16[512,512]{1,0:T(8,128)(2,1)S(1)} %shard_map.192.own_ref, ...), custom_call_target="tpu_custom_call" | custom-call | tf_op jit(solution)/shard_map/pallas_call | solution.py:32
  37.8 2.6 %collective-permute-done.9.refs_0_ = bf16[256,256]{1,0:T(8,128)(2,1)S(1)} collective-permute-done((bf16[256,256]{1,0:T(8,128)(2,1)S(1)}, bf16[256,256]{1,0:T(8,128)(2,1)S(1)}, u32[]{:S(2)}, u32[]{:S(2)}) %collective-permute-start.9) | collective-permute-done | bytes 131104 | tf_op jit(solution)/shard_map/ppermute | solution.py:425
  40.4 1.9 %shard_map.195 = (f32[2048,256]{1,0:T(8,128)S(1)}, bf16[2048,256]{1,0:T(8,128)(2,1)S(1)}, bf16[256,256]{1,0:T(8,128)(2,1)S(1)}, bf16[256,256]{1,0:T(8,128)(2,1)S(1)}, bf16[256,256]{1,0:T(8,128)(2,1)S(1)}) custom-call(f32[2048,256]{1,0:T(8,128)S(1)} %get-tuple-element.76.shift_ref, f32[2048,256]{1,0:T(8,128)S(1)} %get-tuple-element.77.scale_ref, ...), custom_call_target="tpu_custom_call" | custom-call | tf_op jit(solution)/shard_map/pallas_call | solution.py:32
  42.2 3.2 %collective-permute-start.14 = (bf16[256,256]{1,0:T(8,128)(2,1)S(1)}, bf16[256,256]{1,0:T(8,128)(2,1)S(1)}, u32[]{:S(2)}, u32[]{:S(2)}) collective-permute-start(bf16[256,256]{1,0:T(8,128)(2,1)S(1)} %get-tuple-element.91.refs_0_), channel_id=1, source_target_pairs={{0,24},{8,0},{16,8},{24,16},{1,25},{9,1},{17,9},{25,17},{2,26},{10... | collective-permute-start | bytes 393224 | tf_op jit(solution)/shard_map/ppermute | solution.py:421
  45.4 1.3 %collective-permute-start.13 = (bf16[256,256]{1,0:T(8,128)(2,1)S(1)}, bf16[256,256]{1,0:T(8,128)(2,1)S(1)}, u32[]{:S(2)}, u32[]{:S(2)}) collective-permute-start(bf16[256,256]{1,0:T(8,128)(2,1)S(1)} %get-tuple-element.91.refs_0_), channel_id=1, source_target_pairs={{0,16},{8,24},{16,0},{24,8},{1,17},{9,25},{17,1},{25,9},{2,18},{10... | collective-permute-start | bytes 393224 | tf_op jit(solution)/shard_map/ppermute | solution.py:421
  46.7 0.9 %collective-permute-start.12 = (bf16[256,256]{1,0:T(8,128)(2,1)S(1)}, bf16[256,256]{1,0:T(8,128)(2,1)S(1)}, u32[]{:S(2)}, u32[]{:S(2)}) collective-permute-start(bf16[256,256]{1,0:T(8,128)(2,1)S(1)} %get-tuple-element.91.refs_0_), channel_id=1, source_target_pairs={{0,8},{8,16},{16,24},{24,0},{1,9},{9,17},{17,25},{25,1},{2,10},{10... | collective-permute-start | bytes 393224 | tf_op jit(solution)/shard_map/ppermute | solution.py:421
  47.6 2.0 %collective-permute-done.14.refs_3_ = bf16[256,256]{1,0:T(8,128)(2,1)S(1)} collective-permute-done((bf16[256,256]{1,0:T(8,128)(2,1)S(1)}, bf16[256,256]{1,0:T(8,128)(2,1)S(1)}, u32[]{:S(2)}, u32[]{:S(2)}) %collective-permute-start.14) | collective-permute-done | bytes 131104 | tf_op jit(solution)/shard_map/ppermute | solution.py:421
  49.6 1.2 %collective-permute-done.13.refs_2_ = bf16[256,256]{1,0:T(8,128)(2,1)S(1)} collective-permute-done((bf16[256,256]{1,0:T(8,128)(2,1)S(1)}, bf16[256,256]{1,0:T(8,128)(2,1)S(1)}, u32[]{:S(2)}, u32[]{:S(2)}) %collective-permute-start.13) | collective-permute-done | bytes 131104 | tf_op jit(solution)/shard_map/ppermute | solution.py:421
  50.8 1.7 %collective-permute-done.12.refs_1_ = bf16[256,256]{1,0:T(8,128)(2,1)S(1)} collective-permute-done((bf16[256,256]{1,0:T(8,128)(2,1)S(1)}, bf16[256,256]{1,0:T(8,128)(2,1)S(1)}, u32[]{:S(2)}, u32[]{:S(2)}) %collective-permute-start.12) | collective-permute-done | bytes 131104 | tf_op jit(solution)/shard_map/ppermute | solution.py:421
  52.5 0.7 shard_map.198
  53.3 0.1 collective-permute-start.15
  53.3 0.7 shard_map.197.kept_ref
  54.1 1.4 %collective-permute-done.15.sent_ref.refs_3_ = bf16[1280,256]{1,0:T(8,128)(2,1)S(1)} collective-permute-done((bf16[1280,256]{1,0:T(8,128)(2,1)S(1)}, bf16[1280,256]{1,0:T(8,128)(2,1)S(1)}, u32[]{:S(2)}, u32[]{:S(2)}) %collective-permute-start.15) | collective-permute-done | bytes 655392 | tf_op jit(solution)/shard_map/ppermute | solution.py:428
  55.4 0.3 shard_map.199
  55.7 0.5 collective-permute-start.16
  56.2 0.7 collective-permute-start.19
  56.9 2.9 %collective-permute-start.18 = (bf16[256,256]{1,0:T(8,128)(2,1)S(1)}, bf16[256,256]{1,0:T(8,128)(2,1)S(1)}, u32[]{:S(2)}, u32[]{:S(2)}) collective-permute-start(bf16[256,256]{1,0:T(8,128)(2,1)S(1)} %get-tuple-element.98), channel_id=1, source_target_pairs={{0,2},{1,3},{2,0},{3,1},{4,6},{5,7},{6,4},{7,5},{8,10},{9,11},{10,... | collective-permute-start | bytes 393224 | tf_op jit(solution)/shard_map/ppermute | solution.py:440
  59.8 1.5 %collective-permute-done.16.came_ref = bf16[256,256]{1,0:T(8,128)(2,1)S(1)} collective-permute-done((bf16[256,256]{1,0:T(8,128)(2,1)S(1)}, bf16[256,256]{1,0:T(8,128)(2,1)S(1)}, u32[]{:S(2)}, u32[]{:S(2)}) %collective-permute-start.16) | collective-permute-done | bytes 131104 | tf_op jit(solution)/shard_map/ppermute | solution.py:440
  61.4 1.5 %collective-permute-start.17 = (bf16[256,256]{1,0:T(8,128)(2,1)S(1)}, bf16[256,256]{1,0:T(8,128)(2,1)S(1)}, u32[]{:S(2)}, u32[]{:S(2)}) collective-permute-start(bf16[256,256]{1,0:T(8,128)(2,1)S(1)} %shard_map.200), channel_id=1, source_target_pairs={{0,4},{1,5},{2,6},{3,7},{4,0},{5,1},{6,2},{7,3},{8,12},{9,13},{10,... | collective-permute-start | bytes 393224 | tf_op jit(solution)/shard_map/ppermute | solution.py:425
  62.8 2.9 %shard_map.196 = (f32[2048,256]{1,0:T(8,128)S(1)}, f32[2048,256]{1,0:T(8,128)S(1)}, f32[2048,256]{1,0:T(8,128)S(1)}) custom-call(f32[2048,256]{1,0:T(8,128)S(1)} %copy-done, f32[2048,256]{1,0:T(8,128)S(1)} %get-tuple-element.64.state_ref, f32[2048,256]{1,0:T(8,128)S(1)} %get-tuple-element.84.speed_ref, f32[2048,256]{1,0:T(8,128)S(1)} %get-tuple-element.85.part_ref, ...), custom_call_target="tpu_custom_call" | custom-call | tf_op jit(solution)/shard_map/pallas_call | solution.py:32
  65.7 4.0 %collective-permute-done.18.refs_2_ = bf16[256,256]{1,0:T(8,128)(2,1)S(1)} collective-permute-done((bf16[256,256]{1,0:T(8,128)(2,1)S(1)}, bf16[256,256]{1,0:T(8,128)(2,1)S(1)}, u32[]{:S(2)}, u32[]{:S(2)}) %collective-permute-start.18) | collective-permute-done | bytes 131104 | tf_op jit(solution)/shard_map/ppermute | solution.py:440
  69.7 2.6 %shard_map.201 = (f32[2048,256]{1,0:T(8,128)}, f32[2048,256]{1,0:T(8,128)}) custom-call(f32[2048,256]{1,0:T(8,128)S(1)} %get-tuple-element.88.shift_ref, f32[2048,256]{1,0:T(8,128)S(1)} %get-tuple-element.86.scale_ref, f32[2048,256]{1,0:T(8,128)S(1)} %get-tuple-element.89.rest_ref, f32[2048,256]{1,0:T(8,128)S(1)} %get-tuple-element.90.slip_rest_ref, ...), custom_call_target="tpu_custom_call" | custom-call | tf_op jit(solution)/shard_map/pallas_call | solution.py:32
  (19 shorter events, 0.2 us)
Async XLA Ops:
  1.6 12.8 %collective-permute-start.2 = (bf16[128,512]{1,0:T(8,128)(2,1)S(1)}, bf16[128,512]{1,0:T(8,128)(2,1)S(1)}, u32[]{:S(2)}, u32[]{:S(2)}) collective-permute-start(bf16[128,512]{1,0:T(8,128)(2,1)S(1)} %get-tuple-element.69.refs_0_), channel_id=1, source_target_pairs={{0,6},{1,7},{2,0},{3,1},{4,2},{5,3},{6,4},{7,5},{8,14},{9,15},{10,... | collective-permute-start | bytes 393224 | tf_op jit(solution)/shard_map/ppermute | solution.py:425
  6.7 12.0 %collective-permute-start.1 = (bf16[128,512]{1,0:T(8,128)(2,1)S(1)}, bf16[128,512]{1,0:T(8,128)(2,1)S(1)}, u32[]{:S(2)}, u32[]{:S(2)}) collective-permute-start(bf16[128,512]{1,0:T(8,128)(2,1)S(1)} %get-tuple-element.69.refs_0_), channel_id=1, source_target_pairs={{0,4},{1,5},{2,6},{3,7},{4,0},{5,1},{6,2},{7,3},{8,12},{9,13},{10,... | collective-permute-start | bytes 393224 | tf_op jit(solution)/shard_map/ppermute | solution.py:425
  6.7 12.0 %collective-permute-start = (bf16[128,512]{1,0:T(8,128)(2,1)S(1)}, bf16[128,512]{1,0:T(8,128)(2,1)S(1)}, u32[]{:S(2)}, u32[]{:S(2)}) collective-permute-start(bf16[128,512]{1,0:T(8,128)(2,1)S(1)} %get-tuple-element.69.refs_0_), channel_id=1, source_target_pairs={{0,2},{1,3},{2,4},{3,5},{4,6},{5,7},{6,0},{7,1},{8,10},{9,11},{10,... | collective-permute-start | bytes 393224 | tf_op jit(solution)/shard_map/ppermute | solution.py:425
  7.8 3.3 %copy-start = (f32[2048,256]{1,0:T(8,128)S(1)}, f32[2048,256]{1,0:T(8,128)}, u32[]{:S(2)}) copy-start(f32[2048,256]{1,0:T(8,128)} %slip_ref.3) | copy-start | bytes 6291460
  7.8 3.3 %copy-start.2 = (bf16[32,2048]{1,0:T(8,128)(2,1)S(1)}, bf16[32,2048]{1,0:T(8,128)(2,1)}, u32[]{:S(2)}) copy-start(bf16[32,2048]{1,0:T(8,128)(2,1)} %basis_in_ref.1) | copy-start | bytes 393220
  11.5 7.3 %collective-permute-start.5 = (bf16[256,256]{1,0:T(8,128)(2,1)S(1)}, bf16[256,256]{1,0:T(8,128)(2,1)S(1)}, u32[]{:S(2)}, u32[]{:S(2)}) collective-permute-start(bf16[256,256]{1,0:T(8,128)(2,1)S(1)} %get-tuple-element.58.refs_9_.refs_0_), channel_id=1, source_target_pairs={{0,24},{8,0},{16,8},{24,16},{1,25},{9,1},{17,9},{25,17},{2,26},{10... | collective-permute-start | bytes 393224 | tf_op jit(solution)/shard_map/ppermute | solution.py:421
  13.9 7.2 %collective-permute-start.4 = (bf16[256,256]{1,0:T(8,128)(2,1)S(1)}, bf16[256,256]{1,0:T(8,128)(2,1)S(1)}, u32[]{:S(2)}, u32[]{:S(2)}) collective-permute-start(bf16[256,256]{1,0:T(8,128)(2,1)S(1)} %get-tuple-element.58.refs_9_.refs_0_), channel_id=1, source_target_pairs={{0,16},{8,24},{16,0},{24,8},{1,17},{9,25},{17,1},{25,9},{2,18},{10... | collective-permute-start | bytes 393224 | tf_op jit(solution)/shard_map/ppermute | solution.py:421
  14.5 6.7 %collective-permute-start.3 = (bf16[256,256]{1,0:T(8,128)(2,1)S(1)}, bf16[256,256]{1,0:T(8,128)(2,1)S(1)}, u32[]{:S(2)}, u32[]{:S(2)}) collective-permute-start(bf16[256,256]{1,0:T(8,128)(2,1)S(1)} %get-tuple-element.58.refs_9_.refs_0_), channel_id=1, source_target_pairs={{0,8},{8,16},{16,24},{24,0},{1,9},{9,17},{17,25},{25,1},{2,10},{10... | collective-permute-start | bytes 393224 | tf_op jit(solution)/shard_map/ppermute | solution.py:421
  21.8 2.2 %collective-permute-start.6 = (bf16[1280,256]{1,0:T(8,128)(2,1)S(1)}, bf16[1280,256]{1,0:T(8,128)(2,1)S(1)}, u32[]{:S(2)}, u32[]{:S(2)}) collective-permute-start(bf16[1280,256]{1,0:T(8,128)(2,1)S(1)} %shard_map.189), channel_id=1, source_target_pairs={{0,1},{1,0},{2,3},{3,2},{4,5},{5,4},{6,7},{7,6},{8,9},{9,8},{10,11... | collective-permute-start | bytes 1966088 | tf_op jit(solution)/shard_map/ppermute | solution.py:428
  22.0 11.6 %collective-permute-start.8 = (bf16[512,512]{1,0:T(8,128)(2,1)S(1)}, bf16[512,512]{1,0:T(8,128)(2,1)S(1)}, u32[]{:S(2)}, u32[]{:S(2)}) collective-permute-start(bf16[512,512]{1,0:T(8,128)(2,1)S(1)} %shard_map.192.own_ref), channel_id=1, source_target_pairs={{0,1},{1,0},{2,3},{3,2},{4,5},{5,4},{6,7},{7,6},{8,9},{9,8},{10,11... | collective-permute-start | bytes 1572872 | tf_op jit(solution)/shard_map/ppermute | solution.py:428
  24.3 6.8 %collective-permute-start.7 = (bf16[256,256]{1,0:T(8,128)(2,1)S(1)}, bf16[256,256]{1,0:T(8,128)(2,1)S(1)}, u32[]{:S(2)}, u32[]{:S(2)}) collective-permute-start(bf16[256,256]{1,0:T(8,128)(2,1)S(1)} %get-tuple-element.66), channel_id=1, source_target_pairs={{0,2},{1,3},{2,0},{3,1},{4,6},{5,7},{6,4},{7,5},{8,10},{9,11},{10,... | collective-permute-start | bytes 393224 | tf_op jit(solution)/shard_map/ppermute | solution.py:440
  26.8 11.0 %collective-permute-start.10 = (bf16[256,256]{1,0:T(8,128)(2,1)S(1)}, bf16[256,256]{1,0:T(8,128)(2,1)S(1)}, u32[]{:S(2)}, u32[]{:S(2)}) collective-permute-start(bf16[256,256]{1,0:T(8,128)(2,1)S(1)} %get-tuple-element.82), channel_id=1, source_target_pairs={{0,2},{1,3},{2,0},{3,1},{4,6},{5,7},{6,4},{7,5},{8,10},{9,11},{10,... | collective-permute-start | bytes 393224 | tf_op jit(solution)/shard_map/ppermute | solution.py:440
  31.1 9.2 %collective-permute-start.9 = (bf16[256,256]{1,0:T(8,128)(2,1)S(1)}, bf16[256,256]{1,0:T(8,128)(2,1)S(1)}, u32[]{:S(2)}, u32[]{:S(2)}) collective-permute-start(bf16[256,256]{1,0:T(8,128)(2,1)S(1)} %shard_map.194), channel_id=1, source_target_pairs={{0,4},{1,5},{2,6},{3,7},{4,0},{5,1},{6,2},{7,3},{8,12},{9,13},{10,... | collective-permute-start | bytes 393224 | tf_op jit(solution)/shard_map/ppermute | solution.py:425
  32.9 7.5 %collective-permute-start.11 = (bf16[256,256]{1,0:T(8,128)(2,1)S(1)}, bf16[256,256]{1,0:T(8,128)(2,1)S(1)}, u32[]{:S(2)}, u32[]{:S(2)}) collective-permute-start(bf16[256,256]{1,0:T(8,128)(2,1)S(1)} %get-tuple-element.83), channel_id=1, source_target_pairs={{1,2},{3,4},{5,6},{7,8},{9,10},{11,12},{13,14},{15,16},{17,18},{19... | collective-permute-start | bytes 393224 | tf_op jit(solution)/shard_map/ppermute | solution.py:432
  33.5 6.8 %copy-start.1 = (bf16[32,2048]{1,0:T(8,128)(2,1)S(1)}, bf16[32,2048]{1,0:T(8,128)(2,1)}, u32[]{:S(2)}) copy-start(bf16[32,2048]{1,0:T(8,128)(2,1)} %basis_out_ref.3) | copy-start | bytes 393220
  42.2 7.4 %collective-permute-start.14 = (bf16[256,256]{1,0:T(8,128)(2,1)S(1)}, bf16[256,256]{1,0:T(8,128)(2,1)S(1)}, u32[]{:S(2)}, u32[]{:S(2)}) collective-permute-start(bf16[256,256]{1,0:T(8,128)(2,1)S(1)} %get-tuple-element.91.refs_0_), channel_id=1, source_target_pairs={{0,24},{8,0},{16,8},{24,16},{1,25},{9,1},{17,9},{25,17},{2,26},{10... | collective-permute-start | bytes 393224 | tf_op jit(solution)/shard_map/ppermute | solution.py:421
  45.4 5.5 %collective-permute-start.13 = (bf16[256,256]{1,0:T(8,128)(2,1)S(1)}, bf16[256,256]{1,0:T(8,128)(2,1)S(1)}, u32[]{:S(2)}, u32[]{:S(2)}) collective-permute-start(bf16[256,256]{1,0:T(8,128)(2,1)S(1)} %get-tuple-element.91.refs_0_), channel_id=1, source_target_pairs={{0,16},{8,24},{16,0},{24,8},{1,17},{9,25},{17,1},{25,9},{2,18},{10... | collective-permute-start | bytes 393224 | tf_op jit(solution)/shard_map/ppermute | solution.py:421
  46.7 5.9 %collective-permute-start.12 = (bf16[256,256]{1,0:T(8,128)(2,1)S(1)}, bf16[256,256]{1,0:T(8,128)(2,1)S(1)}, u32[]{:S(2)}, u32[]{:S(2)}) collective-permute-start(bf16[256,256]{1,0:T(8,128)(2,1)S(1)} %get-tuple-element.91.refs_0_), channel_id=1, source_target_pairs={{0,8},{8,16},{16,24},{24,0},{1,9},{9,17},{17,25},{25,1},{2,10},{10... | collective-permute-start | bytes 393224 | tf_op jit(solution)/shard_map/ppermute | solution.py:421
  53.3 2.2 %collective-permute-start.15 = (bf16[1280,256]{1,0:T(8,128)(2,1)S(1)}, bf16[1280,256]{1,0:T(8,128)(2,1)S(1)}, u32[]{:S(2)}, u32[]{:S(2)}) collective-permute-start(bf16[1280,256]{1,0:T(8,128)(2,1)S(1)} %shard_map.198), channel_id=1, source_target_pairs={{0,1},{1,0},{2,3},{3,2},{4,5},{5,4},{6,7},{7,6},{8,9},{9,8},{10,11... | collective-permute-start | bytes 1966088 | tf_op jit(solution)/shard_map/ppermute | solution.py:428
  55.7 5.6 %collective-permute-start.16 = (bf16[256,256]{1,0:T(8,128)(2,1)S(1)}, bf16[256,256]{1,0:T(8,128)(2,1)S(1)}, u32[]{:S(2)}, u32[]{:S(2)}) collective-permute-start(bf16[256,256]{1,0:T(8,128)(2,1)S(1)} %get-tuple-element.94), channel_id=1, source_target_pairs={{0,2},{1,3},{2,0},{3,1},{4,6},{5,7},{6,4},{7,5},{8,10},{9,11},{10,... | collective-permute-start | bytes 393224 | tf_op jit(solution)/shard_map/ppermute | solution.py:440
  56.2 9.5 %collective-permute-start.19 = (bf16[256,256]{1,0:T(8,128)(2,1)S(1)}, bf16[256,256]{1,0:T(8,128)(2,1)S(1)}, u32[]{:S(2)}, u32[]{:S(2)}) collective-permute-start(bf16[256,256]{1,0:T(8,128)(2,1)S(1)} %get-tuple-element.99), channel_id=1, source_target_pairs={{1,2},{3,4},{5,6},{7,8},{9,10},{11,12},{13,14},{15,16},{17,18},{19... | collective-permute-start | bytes 393224 | tf_op jit(solution)/shard_map/ppermute | solution.py:432
  56.9 12.8 %collective-permute-start.18 = (bf16[256,256]{1,0:T(8,128)(2,1)S(1)}, bf16[256,256]{1,0:T(8,128)(2,1)S(1)}, u32[]{:S(2)}, u32[]{:S(2)}) collective-permute-start(bf16[256,256]{1,0:T(8,128)(2,1)S(1)} %get-tuple-element.98), channel_id=1, source_target_pairs={{0,2},{1,3},{2,0},{3,1},{4,6},{5,7},{6,4},{7,5},{8,10},{9,11},{10,... | collective-permute-start | bytes 393224 | tf_op jit(solution)/shard_map/ppermute | solution.py:440
  61.4 8.4 %collective-permute-start.17 = (bf16[256,256]{1,0:T(8,128)(2,1)S(1)}, bf16[256,256]{1,0:T(8,128)(2,1)S(1)}, u32[]{:S(2)}, u32[]{:S(2)}) collective-permute-start(bf16[256,256]{1,0:T(8,128)(2,1)S(1)} %shard_map.200), channel_id=1, source_target_pairs={{0,4},{1,5},{2,6},{3,7},{4,0},{5,1},{6,2},{7,3},{8,12},{9,13},{10,... | collective-permute-start | bytes 393224 | tf_op jit(solution)/shard_map/ppermute | solution.py:425

commit v8 on v7

--- a/solution.py
+++ b/solution.py
@@ -287,7 +287,7 @@
     def _(m):
         block(low_ref, m, m)
 
-    @pl.loop(0, blocks, unroll=2)
+    @pl.loop(0, high_ref.shape[1] // BS, unroll=2)
     def _(m):
         block(high_ref, m, blocks + m)
 
@@ -480,8 +480,10 @@
     coeffs = row_coeffs(coeff)
     brick_lists = [adj_count[None], adj_bricks, adj_weight]
     columns = [array[None] for array in per_patch] + brick_lists
-    start = patches // 2
-    part = jax.ShapeDtypeStruct((2 * heights * size, start), BF16)
+    start = (5 * (patches // BS) // 8) * BS
+    part, last_part = (
+        jax.ShapeDtypeStruct((2 * heights * size, n), BF16) for n in (start, patches - start)
+    )
     scratch = [
         pltpu.VMEM((6, 1, patches), F32),
         pltpu.VMEM((1, patches), jnp.int32),
@@ -505,7 +507,7 @@
     own_part, came, direct, keep, sent, cross = first_step(coeffs, pair, cross, True)
     numbers, high, near, state = call(
         functools.partial(weights_kernel, heights, size, start),
-        [jax.ShapeDtypeStruct((patches, 8), F32), part, jax.ShapeDtypeStruct(near_blocks.shape, BF16), full],
+        [jax.ShapeDtypeStruct((patches, 8), F32), last_part, jax.ShapeDtypeStruct(near_blocks.shape, BF16), full],
         *in_hbm(*columns, near_blocks, state),
         numbers,
         own_part,

time: 72.7 us -> 72.8 us (level)
  starting transfers between devices: 26.3 us -> 27.1 us
    ppermute x6, starting transfers between devices: 8.98 us -> 9.86 us  [to_row(): lax.ppermute(array, 'row', [(i, (i + d) % row_count) for i in range(row_c...]
    ppermute x6, waiting for transfers between devices: 7.31 us -> 6.54 us  [to_row(): lax.ppermute(array, 'row', [(i, (i + d) % row_count) for i in range(row_c...]
where the time goes in v8:
time: 72.8 us; the launch traced here: 72.4 us
  starting transfers between devices  27.1 us (37%)
  Pallas kernels  23.5 us (32%)
  waiting for transfers between devices  17.5 us (24%)
  other arithmetic  3.28 us (5%)
  between operations  0.87 us (1%)
    pallas_call x17, Pallas kernels, call(): pl.pallas_call(kernel, in_specs=specs or [VMEM] * len(operands), out_shap...  23.5 us
    ppermute x6, starting transfers between devices, to_row(): lax.ppermute(array, 'row', [(i, (i + d) % row_count) for i in range(row_c...  9.86 us
    ppermute x5, starting transfers between devices, to_height(): return lax.ppermute(array, 'col', pairs)  9.2 us
    ppermute x4, waiting for transfers between devices, to_partner(): return lax.ppermute(array, 'col', pairs)  6.76 us
    ppermute x6, waiting for transfers between devices, to_row(): lax.ppermute(array, 'row', [(i, (i + d) % row_count) for i in range(row_c...  6.54 us
    ppermute x4, starting transfers between devices, to_partner(): return lax.ppermute(array, 'col', pairs)  6.03 us
    select_n x1, other arithmetic, masked_coupling(): jnp.where(keep, matrix, jnp.zeros((), BF16)).reshape(sources, rows, width)  3.28 us
    ppermute x3, waiting for transfers between devices, to_core(): lax.ppermute(array, 'col', [(2 * z + k, 2 * z + 1 - k) for z in range(hei...  2.16 us
  transfers between devices with their start and end apart: 20, of which 10 were waited for; matrix products, arithmetic and copies ran while one was open for 5% of the time, Pallas kernels for 23%

profile of v8, /device:TPU:0, one launch (start us, length us, event | category | flops | bytes accessed | tf_op | source)
XLA Modules:
  0.0 72.4 jit_solution(2062759617737687157)
XLA Ops:
  0.6 1.0 %shard_map.185 = (f32[4,64,256]{2,1,0:T(8,128)S(1)}, bf16[128,512]{1,0:T(8,128)(2,1)S(1)}) custom-call(s32[4,8,64]{2,1,0:T(8,128)} %bitcast.28, bf16[128,256]{1,0:T(8,128)(2,1)} %now_hbm.1, bf16[128,256]{1,0:T(8,128)(2,1)} %rate_hbm.1), custom_call_target="tpu_custom_call" | custom-call | tf_op jit(solution)/shard_map/pallas_call | solution.py:32
  1.6 5.1 %collective-permute-start.2 = (bf16[128,512]{1,0:T(8,128)(2,1)S(1)}, bf16[128,512]{1,0:T(8,128)(2,1)S(1)}, u32[]{:S(2)}, u32[]{:S(2)}) collective-permute-start(bf16[128,512]{1,0:T(8,128)(2,1)S(1)} %get-tuple-element.69.refs_0_), channel_id=1, source_target_pairs={{0,6},{1,7},{2,0},{3,1},{4,2},{5,3},{6,4},{7,5},{8,14},{9,15},{10,... | collective-permute-start | bytes 393224 | tf_op jit(solution)/shard_map/ppermute | solution.py:425
  6.7 0.0 collective-permute-start.1
  6.7 1.0 %collective-permute-start = (bf16[128,512]{1,0:T(8,128)(2,1)S(1)}, bf16[128,512]{1,0:T(8,128)(2,1)S(1)}, u32[]{:S(2)}, u32[]{:S(2)}) collective-permute-start(bf16[128,512]{1,0:T(8,128)(2,1)S(1)} %get-tuple-element.69.refs_0_), channel_id=1, source_target_pairs={{0,2},{1,3},{2,4},{3,5},{4,6},{5,7},{6,0},{7,1},{8,10},{9,11},{10,... | collective-permute-start | bytes 393224 | tf_op jit(solution)/shard_map/ppermute | solution.py:425
  7.7 0.1 lt.21
  7.8 3.3 %fusion.matrix_ref = bf16[4,2048,256]{2,1,0:T(8,128)(2,1)S(1)} fusion(bf16[2048,4,256]{2,1,0:T(4,128)(2,1)} %param.29, f32[4,64,256]{2,1,0:T(8,128)S(1)} %get-tuple-element.51, f32[2048]{0:T(1024)S(1)} %lt.21), kind=kLoop, calls=%fused_computation.1 | loop fusion | flops 4194304 | bytes 8658944 | tf_op jit(solution)/shard_map/jit(_where)/select_n | solution.py:387
  11.1 0.3 shard_map.186
  11.5 2.5 %collective-permute-start.5 = (bf16[256,256]{1,0:T(8,128)(2,1)S(1)}, bf16[256,256]{1,0:T(8,128)(2,1)S(1)}, u32[]{:S(2)}, u32[]{:S(2)}) collective-permute-start(bf16[256,256]{1,0:T(8,128)(2,1)S(1)} %get-tuple-element.58.refs_9_.refs_0_), channel_id=1, source_target_pairs={{0,24},{8,0},{16,8},{24,16},{1,25},{9,1},{17,9},{25,17},{2,26},{10... | collective-permute-start | bytes 393224 | tf_op jit(solution)/shard_map/ppermute | solution.py:421
  13.9 0.5 collective-permute-start.4
  14.5 0.6 collective-permute-start.3
  15.1 4.4 %shard_map.187 = (f32[1280,8]{1,0:T(8,128)S(1)}, bf16[1024,1280]{1,0:T(8,128)(2,1)S(1)}) custom-call(f32[1,2048]{1,0:T(1,128)} %bitcast.14, f32[1,2048]{1,0:T(1,128)} %bitcast.16, f32[1,2048]{1,0:T(1,128)} %bitcast.18, f32[1,2048]{1,0:T(1,128)} %bitcast.20, f32[1,2048]{1,0:T(1,128)} %bitcast.22, f32[1,2048]{1,0:T(1,128)} %bitcast.24, s32[1,2048]{1,0:T(1,128)} %bitcast.26, ...), custom_call_target="tpu_custom_call" | custom-call | tf_op jit(solution)/shard_map/pallas_call | solution.py:32
  19.4 0.0 collective-permute-done.1.refs_2_
  19.5 1.7 %collective-permute-done.4.refs_2_ = bf16[256,256]{1,0:T(8,128)(2,1)S(1)} collective-permute-done((bf16[256,256]{1,0:T(8,128)(2,1)S(1)}, bf16[256,256]{1,0:T(8,128)(2,1)S(1)}, u32[]{:S(2)}, u32[]{:S(2)}) %collective-permute-start.4) | collective-permute-done | bytes 131104 | tf_op jit(solution)/shard_map/ppermute | solution.py:421
  21.1 0.7 shard_map.189
  21.8 0.1 collective-permute-start.6
  22.0 0.6 collective-permute-start.8
  22.5 0.7 shard_map.188.kept_ref
  23.2 0.8 %collective-permute-done.6.sent_ref.refs_3_ = bf16[1280,256]{1,0:T(8,128)(2,1)S(1)} collective-permute-done((bf16[1280,256]{1,0:T(8,128)(2,1)S(1)}, bf16[1280,256]{1,0:T(8,128)(2,1)S(1)}, u32[]{:S(2)}, u32[]{:S(2)}) %collective-permute-start.6) | collective-permute-done | bytes 655392 | tf_op jit(solution)/shard_map/ppermute | solution.py:428
  24.0 0.3 shard_map.190
  24.3 2.5 %collective-permute-start.7 = (bf16[256,256]{1,0:T(8,128)(2,1)S(1)}, bf16[256,256]{1,0:T(8,128)(2,1)S(1)}, u32[]{:S(2)}, u32[]{:S(2)}) collective-permute-start(bf16[256,256]{1,0:T(8,128)(2,1)S(1)} %get-tuple-element.66), channel_id=1, source_target_pairs={{0,2},{1,3},{2,0},{3,1},{4,6},{5,7},{6,4},{7,5},{8,10},{9,11},{10,... | collective-permute-start | bytes 393224 | tf_op jit(solution)/shard_map/ppermute | solution.py:440
  26.8 0.1 collective-permute-start.10
  26.9 3.1 %shard_map.191 = (f32[2048,8]{1,0:T(8,128)S(1)}, bf16[1024,768]{1,0:T(8,128)(2,1)S(1)}, bf16[3,2048,256]{2,1,0:T(8,128)(2,1)S(1)}, f32[2048,256]{1,0:T(8,128)S(1)}) custom-call(f32[1,2048]{1,0:T(1,128)} %bitcast.15, f32[1,2048]{1,0:T(1,128)} %bitcast.17, f32[1,2048]{1,0:T(1,128)} %bitcast.19, f32[1,2048]{1,0:T(1,128)} %bitcast.21, f32[1,2048]{1,0:T(1,128)} %bitcast.23, ...), custom_call_target="tpu_custom_call" | custom-call | tf_op jit(solution)/shard_map/pallas_call | solution.py:32
  30.0 1.1 %collective-permute-done.7.came_ref = bf16[256,256]{1,0:T(8,128)(2,1)S(1)} collective-permute-done((bf16[256,256]{1,0:T(8,128)(2,1)S(1)}, bf16[256,256]{1,0:T(8,128)(2,1)S(1)}, u32[]{:S(2)}, u32[]{:S(2)}) %collective-permute-start.7) | collective-permute-done | bytes 131104 | tf_op jit(solution)/shard_map/ppermute | solution.py:440
  31.1 1.7 %collective-permute-start.9 = (bf16[256,256]{1,0:T(8,128)(2,1)S(1)}, bf16[256,256]{1,0:T(8,128)(2,1)S(1)}, u32[]{:S(2)}, u32[]{:S(2)}) collective-permute-start(bf16[256,256]{1,0:T(8,128)(2,1)S(1)} %shard_map.194), channel_id=1, source_target_pairs={{0,4},{1,5},{2,6},{3,7},{4,0},{5,1},{6,2},{7,3},{8,12},{9,13},{10,... | collective-permute-start | bytes 393224 | tf_op jit(solution)/shard_map/ppermute | solution.py:425
  32.9 0.7 collective-permute-start.11
  33.5 0.0 copy-start.1
  33.6 4.0 %shard_map.193 = (f32[2048,256]{1,0:T(8,128)S(1)}, f32[2048,256]{1,0:T(8,128)S(1)}, f32[2048,256]{1,0:T(8,128)S(1)}, f32[2048,256]{1,0:T(8,128)S(1)}) custom-call(bf16[1024,1280]{1,0:T(8,128)(2,1)S(1)} %get-tuple-element.65.low_ref, bf16[1024,768]{1,0:T(8,128)(2,1)S(1)} %get-tuple-element.68.high_ref, bf16[512,512]{1,0:T(8,128)(2,1)S(1)} %shard_map.192.own_ref, ...), custom_call_target="tpu_custom_call" | custom-call | tf_op jit(solution)/shard_map/pallas_call | solution.py:32
  37.6 2.0 %collective-permute-done.9.refs_0_ = bf16[256,256]{1,0:T(8,128)(2,1)S(1)} collective-permute-done((bf16[256,256]{1,0:T(8,128)(2,1)S(1)}, bf16[256,256]{1,0:T(8,128)(2,1)S(1)}, u32[]{:S(2)}, u32[]{:S(2)}) %collective-permute-start.9) | collective-permute-done | bytes 131104 | tf_op jit(solution)/shard_map/ppermute | solution.py:425
  39.6 1.8 %shard_map.195 = (f32[2048,256]{1,0:T(8,128)S(1)}, bf16[2048,256]{1,0:T(8,128)(2,1)S(1)}, bf16[256,256]{1,0:T(8,128)(2,1)S(1)}, bf16[256,256]{1,0:T(8,128)(2,1)S(1)}, bf16[256,256]{1,0:T(8,128)(2,1)S(1)}) custom-call(f32[2048,256]{1,0:T(8,128)S(1)} %get-tuple-element.76.shift_ref, f32[2048,256]{1,0:T(8,128)S(1)} %get-tuple-element.77.scale_ref, ...), custom_call_target="tpu_custom_call" | custom-call | tf_op jit(solution)/shard_map/pallas_call | solution.py:32
  41.4 4.2 %collective-permute-start.14 = (bf16[256,256]{1,0:T(8,128)(2,1)S(1)}, bf16[256,256]{1,0:T(8,128)(2,1)S(1)}, u32[]{:S(2)}, u32[]{:S(2)}) collective-permute-start(bf16[256,256]{1,0:T(8,128)(2,1)S(1)} %get-tuple-element.91.refs_0_), channel_id=1, source_target_pairs={{0,24},{8,0},{16,8},{24,16},{1,25},{9,1},{17,9},{25,17},{2,26},{10... | collective-permute-start | bytes 393224 | tf_op jit(solution)/shard_map/ppermute | solution.py:421
  45.6 1.1 %collective-permute-start.13 = (bf16[256,256]{1,0:T(8,128)(2,1)S(1)}, bf16[256,256]{1,0:T(8,128)(2,1)S(1)}, u32[]{:S(2)}, u32[]{:S(2)}) collective-permute-start(bf16[256,256]{1,0:T(8,128)(2,1)S(1)} %get-tuple-element.91.refs_0_), channel_id=1, source_target_pairs={{0,16},{8,24},{16,0},{24,8},{1,17},{9,25},{17,1},{25,9},{2,18},{10... | collective-permute-start | bytes 393224 | tf_op jit(solution)/shard_map/ppermute | solution.py:421
  46.7 1.0 %collective-permute-start.12 = (bf16[256,256]{1,0:T(8,128)(2,1)S(1)}, bf16[256,256]{1,0:T(8,128)(2,1)S(1)}, u32[]{:S(2)}, u32[]{:S(2)}) collective-permute-start(bf16[256,256]{1,0:T(8,128)(2,1)S(1)} %get-tuple-element.91.refs_0_), channel_id=1, source_target_pairs={{0,8},{8,16},{16,24},{24,0},{1,9},{9,17},{17,25},{25,1},{2,10},{10... | collective-permute-start | bytes 393224 | tf_op jit(solution)/shard_map/ppermute | solution.py:421
  47.7 1.4 %collective-permute-done.14.refs_3_ = bf16[256,256]{1,0:T(8,128)(2,1)S(1)} collective-permute-done((bf16[256,256]{1,0:T(8,128)(2,1)S(1)}, bf16[256,256]{1,0:T(8,128)(2,1)S(1)}, u32[]{:S(2)}, u32[]{:S(2)}) %collective-permute-start.14) | collective-permute-done | bytes 131104 | tf_op jit(solution)/shard_map/ppermute | solution.py:421
  49.1 1.5 %collective-permute-done.13.refs_2_ = bf16[256,256]{1,0:T(8,128)(2,1)S(1)} collective-permute-done((bf16[256,256]{1,0:T(8,128)(2,1)S(1)}, bf16[256,256]{1,0:T(8,128)(2,1)S(1)}, u32[]{:S(2)}, u32[]{:S(2)}) %collective-permute-start.13) | collective-permute-done | bytes 131104 | tf_op jit(solution)/shard_map/ppermute | solution.py:421
  50.6 2.0 %collective-permute-done.12.refs_1_ = bf16[256,256]{1,0:T(8,128)(2,1)S(1)} collective-permute-done((bf16[256,256]{1,0:T(8,128)(2,1)S(1)}, bf16[256,256]{1,0:T(8,128)(2,1)S(1)}, u32[]{:S(2)}, u32[]{:S(2)}) %collective-permute-start.12) | collective-permute-done | bytes 131104 | tf_op jit(solution)/shard_map/ppermute | solution.py:421
  52.6 0.7 shard_map.198
  53.3 0.1 collective-permute-start.15
  53.4 0.7 shard_map.197.kept_ref
  54.1 1.4 %collective-permute-done.15.sent_ref.refs_3_ = bf16[1280,256]{1,0:T(8,128)(2,1)S(1)} collective-permute-done((bf16[1280,256]{1,0:T(8,128)(2,1)S(1)}, bf16[1280,256]{1,0:T(8,128)(2,1)S(1)}, u32[]{:S(2)}, u32[]{:S(2)}) %collective-permute-start.15) | collective-permute-done | bytes 655392 | tf_op jit(solution)/shard_map/ppermute | solution.py:428
  55.5 0.3 shard_map.199
  55.7 0.5 collective-permute-start.16
  56.2 0.7 collective-permute-start.19
  56.9 2.9 %collective-permute-start.18 = (bf16[256,256]{1,0:T(8,128)(2,1)S(1)}, bf16[256,256]{1,0:T(8,128)(2,1)S(1)}, u32[]{:S(2)}, u32[]{:S(2)}) collective-permute-start(bf16[256,256]{1,0:T(8,128)(2,1)S(1)} %get-tuple-element.98), channel_id=1, source_target_pairs={{0,2},{1,3},{2,0},{3,1},{4,6},{5,7},{6,4},{7,5},{8,10},{9,11},{10,... | collective-permute-start | bytes 393224 | tf_op jit(solution)/shard_map/ppermute | solution.py:440
  59.8 1.5 %collective-permute-done.16.came_ref = bf16[256,256]{1,0:T(8,128)(2,1)S(1)} collective-permute-done((bf16[256,256]{1,0:T(8,128)(2,1)S(1)}, bf16[256,256]{1,0:T(8,128)(2,1)S(1)}, u32[]{:S(2)}, u32[]{:S(2)}) %collective-permute-start.16) | collective-permute-done | bytes 131104 | tf_op jit(solution)/shard_map/ppermute | solution.py:440
  61.4 1.4 %collective-permute-start.17 = (bf16[256,256]{1,0:T(8,128)(2,1)S(1)}, bf16[256,256]{1,0:T(8,128)(2,1)S(1)}, u32[]{:S(2)}, u32[]{:S(2)}) collective-permute-start(bf16[256,256]{1,0:T(8,128)(2,1)S(1)} %shard_map.200), channel_id=1, source_target_pairs={{0,4},{1,5},{2,6},{3,7},{4,0},{5,1},{6,2},{7,3},{8,12},{9,13},{10,... | collective-permute-start | bytes 393224 | tf_op jit(solution)/shard_map/ppermute | solution.py:425
  62.7 2.9 %shard_map.196 = (f32[2048,256]{1,0:T(8,128)S(1)}, f32[2048,256]{1,0:T(8,128)S(1)}, f32[2048,256]{1,0:T(8,128)S(1)}) custom-call(f32[2048,256]{1,0:T(8,128)S(1)} %copy-done, f32[2048,256]{1,0:T(8,128)S(1)} %get-tuple-element.64.state_ref, f32[2048,256]{1,0:T(8,128)S(1)} %get-tuple-element.84.speed_ref, f32[2048,256]{1,0:T(8,128)S(1)} %get-tuple-element.85.part_ref, ...), custom_call_target="tpu_custom_call" | custom-call | tf_op jit(solution)/shard_map/pallas_call | solution.py:32
  65.7 4.1 %collective-permute-done.18.refs_2_ = bf16[256,256]{1,0:T(8,128)(2,1)S(1)} collective-permute-done((bf16[256,256]{1,0:T(8,128)(2,1)S(1)}, bf16[256,256]{1,0:T(8,128)(2,1)S(1)}, u32[]{:S(2)}, u32[]{:S(2)}) %collective-permute-start.18) | collective-permute-done | bytes 131104 | tf_op jit(solution)/shard_map/ppermute | solution.py:440
  69.8 2.6 %shard_map.201 = (f32[2048,256]{1,0:T(8,128)}, f32[2048,256]{1,0:T(8,128)}) custom-call(f32[2048,256]{1,0:T(8,128)S(1)} %get-tuple-element.88.shift_ref, f32[2048,256]{1,0:T(8,128)S(1)} %get-tuple-element.86.scale_ref, f32[2048,256]{1,0:T(8,128)S(1)} %get-tuple-element.89.rest_ref, f32[2048,256]{1,0:T(8,128)S(1)} %get-tuple-element.90.slip_rest_ref, ...), custom_call_target="tpu_custom_call" | custom-call | tf_op jit(solution)/shard_map/pallas_call | solution.py:32
  (19 shorter events, 0.2 us)
Async XLA Ops:
  1.6 12.8 %collective-permute-start.2 = (bf16[128,512]{1,0:T(8,128)(2,1)S(1)}, bf16[128,512]{1,0:T(8,128)(2,1)S(1)}, u32[]{:S(2)}, u32[]{:S(2)}) collective-permute-start(bf16[128,512]{1,0:T(8,128)(2,1)S(1)} %get-tuple-element.69.refs_0_), channel_id=1, source_target_pairs={{0,6},{1,7},{2,0},{3,1},{4,2},{5,3},{6,4},{7,5},{8,14},{9,15},{10,... | collective-permute-start | bytes 393224 | tf_op jit(solution)/shard_map/ppermute | solution.py:425
  6.7 12.7 %collective-permute-start.1 = (bf16[128,512]{1,0:T(8,128)(2,1)S(1)}, bf16[128,512]{1,0:T(8,128)(2,1)S(1)}, u32[]{:S(2)}, u32[]{:S(2)}) collective-permute-start(bf16[128,512]{1,0:T(8,128)(2,1)S(1)} %get-tuple-element.69.refs_0_), channel_id=1, source_target_pairs={{0,4},{1,5},{2,6},{3,7},{4,0},{5,1},{6,2},{7,3},{8,12},{9,13},{10,... | collective-permute-start | bytes 393224 | tf_op jit(solution)/shard_map/ppermute | solution.py:425
  6.7 12.7 %collective-permute-start = (bf16[128,512]{1,0:T(8,128)(2,1)S(1)}, bf16[128,512]{1,0:T(8,128)(2,1)S(1)}, u32[]{:S(2)}, u32[]{:S(2)}) collective-permute-start(bf16[128,512]{1,0:T(8,128)(2,1)S(1)} %get-tuple-element.69.refs_0_), channel_id=1, source_target_pairs={{0,2},{1,3},{2,4},{3,5},{4,6},{5,7},{6,0},{7,1},{8,10},{9,11},{10,... | collective-permute-start | bytes 393224 | tf_op jit(solution)/shard_map/ppermute | solution.py:425
  7.8 3.3 %copy-start = (f32[2048,256]{1,0:T(8,128)S(1)}, f32[2048,256]{1,0:T(8,128)}, u32[]{:S(2)}) copy-start(f32[2048,256]{1,0:T(8,128)} %slip_ref.3) | copy-start | bytes 6291460
  7.8 3.3 %copy-start.2 = (bf16[32,2048]{1,0:T(8,128)(2,1)S(1)}, bf16[32,2048]{1,0:T(8,128)(2,1)}, u32[]{:S(2)}) copy-start(bf16[32,2048]{1,0:T(8,128)(2,1)} %basis_in_ref.1) | copy-start | bytes 393220
  11.5 8.0 %collective-permute-start.5 = (bf16[256,256]{1,0:T(8,128)(2,1)S(1)}, bf16[256,256]{1,0:T(8,128)(2,1)S(1)}, u32[]{:S(2)}, u32[]{:S(2)}) collective-permute-start(bf16[256,256]{1,0:T(8,128)(2,1)S(1)} %get-tuple-element.58.refs_9_.refs_0_), channel_id=1, source_target_pairs={{0,24},{8,0},{16,8},{24,16},{1,25},{9,1},{17,9},{25,17},{2,26},{10... | collective-permute-start | bytes 393224 | tf_op jit(solution)/shard_map/ppermute | solution.py:421
  13.9 7.2 %collective-permute-start.4 = (bf16[256,256]{1,0:T(8,128)(2,1)S(1)}, bf16[256,256]{1,0:T(8,128)(2,1)S(1)}, u32[]{:S(2)}, u32[]{:S(2)}) collective-permute-start(bf16[256,256]{1,0:T(8,128)(2,1)S(1)} %get-tuple-element.58.refs_9_.refs_0_), channel_id=1, source_target_pairs={{0,16},{8,24},{16,0},{24,8},{1,17},{9,25},{17,1},{25,9},{2,18},{10... | collective-permute-start | bytes 393224 | tf_op jit(solution)/shard_map/ppermute | solution.py:421
  14.5 6.7 %collective-permute-start.3 = (bf16[256,256]{1,0:T(8,128)(2,1)S(1)}, bf16[256,256]{1,0:T(8,128)(2,1)S(1)}, u32[]{:S(2)}, u32[]{:S(2)}) collective-permute-start(bf16[256,256]{1,0:T(8,128)(2,1)S(1)} %get-tuple-element.58.refs_9_.refs_0_), channel_id=1, source_target_pairs={{0,8},{8,16},{16,24},{24,0},{1,9},{9,17},{17,25},{25,1},{2,10},{10... | collective-permute-start | bytes 393224 | tf_op jit(solution)/shard_map/ppermute | solution.py:421
  21.8 2.2 %collective-permute-start.6 = (bf16[1280,256]{1,0:T(8,128)(2,1)S(1)}, bf16[1280,256]{1,0:T(8,128)(2,1)S(1)}, u32[]{:S(2)}, u32[]{:S(2)}) collective-permute-start(bf16[1280,256]{1,0:T(8,128)(2,1)S(1)} %shard_map.189), channel_id=1, source_target_pairs={{0,1},{1,0},{2,3},{3,2},{4,5},{5,4},{6,7},{7,6},{8,9},{9,8},{10,11... | collective-permute-start | bytes 1966088 | tf_op jit(solution)/shard_map/ppermute | solution.py:428
  22.0 11.6 %collective-permute-start.8 = (bf16[512,512]{1,0:T(8,128)(2,1)S(1)}, bf16[512,512]{1,0:T(8,128)(2,1)S(1)}, u32[]{:S(2)}, u32[]{:S(2)}) collective-permute-start(bf16[512,512]{1,0:T(8,128)(2,1)S(1)} %shard_map.192.own_ref), channel_id=1, source_target_pairs={{0,1},{1,0},{2,3},{3,2},{4,5},{5,4},{6,7},{7,6},{8,9},{9,8},{10,11... | collective-permute-start | bytes 1572872 | tf_op jit(solution)/shard_map/ppermute | solution.py:428
  24.3 6.8 %collective-permute-start.7 = (bf16[256,256]{1,0:T(8,128)(2,1)S(1)}, bf16[256,256]{1,0:T(8,128)(2,1)S(1)}, u32[]{:S(2)}, u32[]{:S(2)}) collective-permute-start(bf16[256,256]{1,0:T(8,128)(2,1)S(1)} %get-tuple-element.66), channel_id=1, source_target_pairs={{0,2},{1,3},{2,0},{3,1},{4,6},{5,7},{6,4},{7,5},{8,10},{9,11},{10,... | collective-permute-start | bytes 393224 | tf_op jit(solution)/shard_map/ppermute | solution.py:440
  26.8 10.7 %collective-permute-start.10 = (bf16[256,256]{1,0:T(8,128)(2,1)S(1)}, bf16[256,256]{1,0:T(8,128)(2,1)S(1)}, u32[]{:S(2)}, u32[]{:S(2)}) collective-permute-start(bf16[256,256]{1,0:T(8,128)(2,1)S(1)} %get-tuple-element.82), channel_id=1, source_target_pairs={{0,2},{1,3},{2,0},{3,1},{4,6},{5,7},{6,4},{7,5},{8,10},{9,11},{10,... | collective-permute-start | bytes 393224 | tf_op jit(solution)/shard_map/ppermute | solution.py:440
  31.1 8.4 %collective-permute-start.9 = (bf16[256,256]{1,0:T(8,128)(2,1)S(1)}, bf16[256,256]{1,0:T(8,128)(2,1)S(1)}, u32[]{:S(2)}, u32[]{:S(2)}) collective-permute-start(bf16[256,256]{1,0:T(8,128)(2,1)S(1)} %shard_map.194), channel_id=1, source_target_pairs={{0,4},{1,5},{2,6},{3,7},{4,0},{5,1},{6,2},{7,3},{8,12},{9,13},{10,... | collective-permute-start | bytes 393224 | tf_op jit(solution)/shard_map/ppermute | solution.py:425
  32.9 6.7 %collective-permute-start.11 = (bf16[256,256]{1,0:T(8,128)(2,1)S(1)}, bf16[256,256]{1,0:T(8,128)(2,1)S(1)}, u32[]{:S(2)}, u32[]{:S(2)}) collective-permute-start(bf16[256,256]{1,0:T(8,128)(2,1)S(1)} %get-tuple-element.83), channel_id=1, source_target_pairs={{1,2},{3,4},{5,6},{7,8},{9,10},{11,12},{13,14},{15,16},{17,18},{19... | collective-permute-start | bytes 393224 | tf_op jit(solution)/shard_map/ppermute | solution.py:432
  33.5 6.0 %copy-start.1 = (bf16[32,2048]{1,0:T(8,128)(2,1)S(1)}, bf16[32,2048]{1,0:T(8,128)(2,1)}, u32[]{:S(2)}) copy-start(bf16[32,2048]{1,0:T(8,128)(2,1)} %basis_out_ref.3) | copy-start | bytes 393220
  41.4 7.7 %collective-permute-start.14 = (bf16[256,256]{1,0:T(8,128)(2,1)S(1)}, bf16[256,256]{1,0:T(8,128)(2,1)S(1)}, u32[]{:S(2)}, u32[]{:S(2)}) collective-permute-start(bf16[256,256]{1,0:T(8,128)(2,1)S(1)} %get-tuple-element.91.refs_0_), channel_id=1, source_target_pairs={{0,24},{8,0},{16,8},{24,16},{1,25},{9,1},{17,9},{25,17},{2,26},{10... | collective-permute-start | bytes 393224 | tf_op jit(solution)/shard_map/ppermute | solution.py:421
  45.6 5.0 %collective-permute-start.13 = (bf16[256,256]{1,0:T(8,128)(2,1)S(1)}, bf16[256,256]{1,0:T(8,128)(2,1)S(1)}, u32[]{:S(2)}, u32[]{:S(2)}) collective-permute-start(bf16[256,256]{1,0:T(8,128)(2,1)S(1)} %get-tuple-element.91.refs_0_), channel_id=1, source_target_pairs={{0,16},{8,24},{16,0},{24,8},{1,17},{9,25},{17,1},{25,9},{2,18},{10... | collective-permute-start | bytes 393224 | tf_op jit(solution)/shard_map/ppermute | solution.py:421
  46.7 5.9 %collective-permute-start.12 = (bf16[256,256]{1,0:T(8,128)(2,1)S(1)}, bf16[256,256]{1,0:T(8,128)(2,1)S(1)}, u32[]{:S(2)}, u32[]{:S(2)}) collective-permute-start(bf16[256,256]{1,0:T(8,128)(2,1)S(1)} %get-tuple-element.91.refs_0_), channel_id=1, source_target_pairs={{0,8},{8,16},{16,24},{24,0},{1,9},{9,17},{17,25},{25,1},{2,10},{10... | collective-permute-start | bytes 393224 | tf_op jit(solution)/shard_map/ppermute | solution.py:421
  53.3 2.2 %collective-permute-start.15 = (bf16[1280,256]{1,0:T(8,128)(2,1)S(1)}, bf16[1280,256]{1,0:T(8,128)(2,1)S(1)}, u32[]{:S(2)}, u32[]{:S(2)}) collective-permute-start(bf16[1280,256]{1,0:T(8,128)(2,1)S(1)} %shard_map.198), channel_id=1, source_target_pairs={{0,1},{1,0},{2,3},{3,2},{4,5},{5,4},{6,7},{7,6},{8,9},{9,8},{10,11... | collective-permute-start | bytes 1966088 | tf_op jit(solution)/shard_map/ppermute | solution.py:428
  55.7 5.6 %collective-permute-start.16 = (bf16[256,256]{1,0:T(8,128)(2,1)S(1)}, bf16[256,256]{1,0:T(8,128)(2,1)S(1)}, u32[]{:S(2)}, u32[]{:S(2)}) collective-permute-start(bf16[256,256]{1,0:T(8,128)(2,1)S(1)} %get-tuple-element.94), channel_id=1, source_target_pairs={{0,2},{1,3},{2,0},{3,1},{4,6},{5,7},{6,4},{7,5},{8,10},{9,11},{10,... | collective-permute-start | bytes 393224 | tf_op jit(solution)/shard_map/ppermute | solution.py:440
  56.2 9.4 %collective-permute-start.19 = (bf16[256,256]{1,0:T(8,128)(2,1)S(1)}, bf16[256,256]{1,0:T(8,128)(2,1)S(1)}, u32[]{:S(2)}, u32[]{:S(2)}) collective-permute-start(bf16[256,256]{1,0:T(8,128)(2,1)S(1)} %get-tuple-element.99), channel_id=1, source_target_pairs={{1,2},{3,4},{5,6},{7,8},{9,10},{11,12},{13,14},{15,16},{17,18},{19... | collective-permute-start | bytes 393224 | tf_op jit(solution)/shard_map/ppermute | solution.py:432
  56.9 12.9 %collective-permute-start.18 = (bf16[256,256]{1,0:T(8,128)(2,1)S(1)}, bf16[256,256]{1,0:T(8,128)(2,1)S(1)}, u32[]{:S(2)}, u32[]{:S(2)}) collective-permute-start(bf16[256,256]{1,0:T(8,128)(2,1)S(1)} %get-tuple-element.98), channel_id=1, source_target_pairs={{0,2},{1,3},{2,0},{3,1},{4,6},{5,7},{6,4},{7,5},{8,10},{9,11},{10,... | collective-permute-start | bytes 393224 | tf_op jit(solution)/shard_map/ppermute | solution.py:440
  61.4 8.4 %collective-permute-start.17 = (bf16[256,256]{1,0:T(8,128)(2,1)S(1)}, bf16[256,256]{1,0:T(8,128)(2,1)S(1)}, u32[]{:S(2)}, u32[]{:S(2)}) collective-permute-start(bf16[256,256]{1,0:T(8,128)(2,1)S(1)} %shard_map.200), channel_id=1, source_target_pairs={{0,4},{1,5},{2,6},{3,7},{4,0},{5,1},{6,2},{7,3},{8,12},{9,13},{10,... | collective-permute-start | bytes 393224 | tf_op jit(solution)/shard_map/ppermute | solution.py:425

commit v9 on v7

--- a/solution.py
+++ b/solution.py
@@ -140,7 +140,7 @@
     slots = bricks_ref.shape[0]
     col = lax.axis_index("col")
     height, core = lax.div(col, 2).astype(F32), lax.rem(col, 2).astype(F32)
-    group, lanes, unrolled = 16, 128, 8
+    group, lanes, unrolled = 16, 128, 16
     for copy in copies:
         copy.wait()
 

time: 72.7 us -> 72.8 us (level)
  transfers between devices with their start and end apart: 20 -> 20, of which waited for: 10 -> 10; matrix products, arithmetic and copies ran while one was open for 5% -> 5% of each run, Pallas kernels for 23% -> 22%
where the time goes in v9:
time: 72.8 us; the launch traced here: 72.4 us
  starting transfers between devices  27 us (37%)
  Pallas kernels  23.3 us (32%)
  waiting for transfers between devices  17.9 us (25%)
  other arithmetic  3.28 us (5%)
  between operations  0.87 us (1%)
    pallas_call x17, Pallas kernels, call(): pl.pallas_call(kernel, in_specs=specs or [VMEM] * len(operands), out_shap...  23.3 us
    ppermute x6, starting transfers between devices, to_row(): lax.ppermute(array, 'row', [(i, (i + d) % row_count) for i in range(row_c...  9.48 us
    ppermute x5, starting transfers between devices, to_height(): return lax.ppermute(array, 'col', pairs)  9.29 us
    ppermute x6, waiting for transfers between devices, to_row(): lax.ppermute(array, 'row', [(i, (i + d) % row_count) for i in range(row_c...  7.49 us
    ppermute x4, starting transfers between devices, to_partner(): return lax.ppermute(array, 'col', pairs)  6.22 us
    ppermute x4, waiting for transfers between devices, to_partner(): return lax.ppermute(array, 'col', pairs)  6.15 us
    select_n x1, other arithmetic, masked_coupling(): jnp.where(keep, matrix, jnp.zeros((), BF16)).reshape(sources, rows, width)  3.28 us
    ppermute x3, waiting for transfers between devices, to_core(): lax.ppermute(array, 'col', [(2 * z + k, 2 * z + 1 - k) for z in range(hei...  2.16 us
  transfers between devices with their start and end apart: 20, of which 10 were waited for; matrix products, arithmetic and copies ran while one was open for 5% of the time, Pallas kernels for 22%

profile of v9, /device:TPU:0, one launch (start us, length us, event | category | flops | bytes accessed | tf_op | source)
XLA Modules:
  0.0 72.4 jit_solution(10398618476552319937)
XLA Ops:
  0.6 1.0 %shard_map.185 = (f32[4,64,256]{2,1,0:T(8,128)S(1)}, bf16[128,512]{1,0:T(8,128)(2,1)S(1)}) custom-call(s32[4,8,64]{2,1,0:T(8,128)} %bitcast.28, bf16[128,256]{1,0:T(8,128)(2,1)} %now_hbm.1, bf16[128,256]{1,0:T(8,128)(2,1)} %rate_hbm.1), custom_call_target="tpu_custom_call" | custom-call | tf_op jit(solution)/shard_map/pallas_call | solution.py:32
  1.6 5.1 %collective-permute-start.2 = (bf16[128,512]{1,0:T(8,128)(2,1)S(1)}, bf16[128,512]{1,0:T(8,128)(2,1)S(1)}, u32[]{:S(2)}, u32[]{:S(2)}) collective-permute-start(bf16[128,512]{1,0:T(8,128)(2,1)S(1)} %get-tuple-element.69.refs_0_), channel_id=1, source_target_pairs={{0,6},{1,7},{2,0},{3,1},{4,2},{5,3},{6,4},{7,5},{8,14},{9,15},{10,... | collective-permute-start | bytes 393224 | tf_op jit(solution)/shard_map/ppermute | solution.py:425
  6.7 1.0 %collective-permute-start = (bf16[128,512]{1,0:T(8,128)(2,1)S(1)}, bf16[128,512]{1,0:T(8,128)(2,1)S(1)}, u32[]{:S(2)}, u32[]{:S(2)}) collective-permute-start(bf16[128,512]{1,0:T(8,128)(2,1)S(1)} %get-tuple-element.69.refs_0_), channel_id=1, source_target_pairs={{0,2},{1,3},{2,4},{3,5},{4,6},{5,7},{6,0},{7,1},{8,10},{9,11},{10,... | collective-permute-start | bytes 393224 | tf_op jit(solution)/shard_map/ppermute | solution.py:425
  7.7 0.1 lt.21
  7.8 3.3 %fusion.matrix_ref = bf16[4,2048,256]{2,1,0:T(8,128)(2,1)S(1)} fusion(bf16[2048,4,256]{2,1,0:T(4,128)(2,1)} %param.29, f32[4,64,256]{2,1,0:T(8,128)S(1)} %get-tuple-element.51, f32[2048]{0:T(1024)S(1)} %lt.21), kind=kLoop, calls=%fused_computation.1 | loop fusion | flops 4194304 | bytes 8658944 | tf_op jit(solution)/shard_map/jit(_where)/select_n | solution.py:387
  11.1 0.3 shard_map.186
  11.5 2.5 %collective-permute-start.5 = (bf16[256,256]{1,0:T(8,128)(2,1)S(1)}, bf16[256,256]{1,0:T(8,128)(2,1)S(1)}, u32[]{:S(2)}, u32[]{:S(2)}) collective-permute-start(bf16[256,256]{1,0:T(8,128)(2,1)S(1)} %get-tuple-element.58.refs_9_.refs_0_), channel_id=1, source_target_pairs={{0,24},{8,0},{16,8},{24,16},{1,25},{9,1},{17,9},{25,17},{2,26},{10... | collective-permute-start | bytes 393224 | tf_op jit(solution)/shard_map/ppermute | solution.py:421
  13.9 0.5 collective-permute-start.4
  14.5 0.0 collective-permute-done.2.refs_3_
  14.5 0.6 collective-permute-start.3
  15.1 3.5 %shard_map.187 = (f32[1024,8]{1,0:T(8,128)S(1)}, bf16[1024,1024]{1,0:T(8,128)(2,1)S(1)}) custom-call(f32[1,2048]{1,0:T(1,128)} %bitcast.14, f32[1,2048]{1,0:T(1,128)} %bitcast.16, f32[1,2048]{1,0:T(1,128)} %bitcast.18, f32[1,2048]{1,0:T(1,128)} %bitcast.20, f32[1,2048]{1,0:T(1,128)} %bitcast.22, f32[1,2048]{1,0:T(1,128)} %bitcast.24, s32[1,2048]{1,0:T(1,128)} %bitcast.26, ...), custom_call_target="tpu_custom_call" | custom-call | tf_op jit(solution)/shard_map/pallas_call | solution.py:32
  18.6 0.0 collective-permute-done.refs_1_
  18.6 2.5 %collective-permute-done.4.refs_2_ = bf16[256,256]{1,0:T(8,128)(2,1)S(1)} collective-permute-done((bf16[256,256]{1,0:T(8,128)(2,1)S(1)}, bf16[256,256]{1,0:T(8,128)(2,1)S(1)}, u32[]{:S(2)}, u32[]{:S(2)}) %collective-permute-start.4) | collective-permute-done | bytes 131104 | tf_op jit(solution)/shard_map/ppermute | solution.py:421
  21.1 0.7 shard_map.189
  21.8 0.1 collective-permute-start.6
  22.0 0.6 collective-permute-start.8
  22.5 0.7 shard_map.188.kept_ref
  23.2 0.8 %collective-permute-done.6.sent_ref.refs_3_ = bf16[1280,256]{1,0:T(8,128)(2,1)S(1)} collective-permute-done((bf16[1280,256]{1,0:T(8,128)(2,1)S(1)}, bf16[1280,256]{1,0:T(8,128)(2,1)S(1)}, u32[]{:S(2)}, u32[]{:S(2)}) %collective-permute-start.6) | collective-permute-done | bytes 655392 | tf_op jit(solution)/shard_map/ppermute | solution.py:428
  24.0 0.3 shard_map.190
  24.3 2.5 %collective-permute-start.7 = (bf16[256,256]{1,0:T(8,128)(2,1)S(1)}, bf16[256,256]{1,0:T(8,128)(2,1)S(1)}, u32[]{:S(2)}, u32[]{:S(2)}) collective-permute-start(bf16[256,256]{1,0:T(8,128)(2,1)S(1)} %get-tuple-element.66), channel_id=1, source_target_pairs={{0,2},{1,3},{2,0},{3,1},{4,6},{5,7},{6,4},{7,5},{8,10},{9,11},{10,... | collective-permute-start | bytes 393224 | tf_op jit(solution)/shard_map/ppermute | solution.py:440
  26.8 0.1 collective-permute-start.10
  26.9 3.5 %shard_map.191 = (f32[2048,8]{1,0:T(8,128)S(1)}, bf16[1024,1024]{1,0:T(8,128)(2,1)S(1)}, bf16[3,2048,256]{2,1,0:T(8,128)(2,1)S(1)}, f32[2048,256]{1,0:T(8,128)S(1)}) custom-call(f32[1,2048]{1,0:T(1,128)} %bitcast.15, f32[1,2048]{1,0:T(1,128)} %bitcast.17, f32[1,2048]{1,0:T(1,128)} %bitcast.19, f32[1,2048]{1,0:T(1,128)} %bitcast.21, f32[1,2048]{1,0:T(1,128)} %bitcast.23, ...), custom_call_target="tpu_custom_call" | custom-call | tf_op jit(solution)/shard_map/pallas_call | solution.py:32
  30.4 0.7 collective-permute-done.7.came_ref
  31.1 1.7 %collective-permute-start.9 = (bf16[256,256]{1,0:T(8,128)(2,1)S(1)}, bf16[256,256]{1,0:T(8,128)(2,1)S(1)}, u32[]{:S(2)}, u32[]{:S(2)}) collective-permute-start(bf16[256,256]{1,0:T(8,128)(2,1)S(1)} %shard_map.194), channel_id=1, source_target_pairs={{0,4},{1,5},{2,6},{3,7},{4,0},{5,1},{6,2},{7,3},{8,12},{9,13},{10,... | collective-permute-start | bytes 393224 | tf_op jit(solution)/shard_map/ppermute | solution.py:425
  32.9 0.7 collective-permute-start.11
  33.5 0.0 copy-start.1
  33.6 4.2 %shard_map.193 = (f32[2048,256]{1,0:T(8,128)S(1)}, f32[2048,256]{1,0:T(8,128)S(1)}, f32[2048,256]{1,0:T(8,128)S(1)}, f32[2048,256]{1,0:T(8,128)S(1)}) custom-call(bf16[1024,1024]{1,0:T(8,128)(2,1)S(1)} %get-tuple-element.65.low_ref, bf16[1024,1024]{1,0:T(8,128)(2,1)S(1)} %get-tuple-element.68.high_ref, bf16[512,512]{1,0:T(8,128)(2,1)S(1)} %shard_map.192.own_ref, ...), custom_call_target="tpu_custom_call" | custom-call | tf_op jit(solution)/shard_map/pallas_call | solution.py:32
  37.8 2.1 %collective-permute-done.9.refs_0_ = bf16[256,256]{1,0:T(8,128)(2,1)S(1)} collective-permute-done((bf16[256,256]{1,0:T(8,128)(2,1)S(1)}, bf16[256,256]{1,0:T(8,128)(2,1)S(1)}, u32[]{:S(2)}, u32[]{:S(2)}) %collective-permute-start.9) | collective-permute-done | bytes 131104 | tf_op jit(solution)/shard_map/ppermute | solution.py:425
  39.8 1.9 %shard_map.195 = (f32[2048,256]{1,0:T(8,128)S(1)}, bf16[2048,256]{1,0:T(8,128)(2,1)S(1)}, bf16[256,256]{1,0:T(8,128)(2,1)S(1)}, bf16[256,256]{1,0:T(8,128)(2,1)S(1)}, bf16[256,256]{1,0:T(8,128)(2,1)S(1)}) custom-call(f32[2048,256]{1,0:T(8,128)S(1)} %get-tuple-element.76.shift_ref, f32[2048,256]{1,0:T(8,128)S(1)} %get-tuple-element.77.scale_ref, ...), custom_call_target="tpu_custom_call" | custom-call | tf_op jit(solution)/shard_map/pallas_call | solution.py:32
  41.7 3.7 %collective-permute-start.14 = (bf16[256,256]{1,0:T(8,128)(2,1)S(1)}, bf16[256,256]{1,0:T(8,128)(2,1)S(1)}, u32[]{:S(2)}, u32[]{:S(2)}) collective-permute-start(bf16[256,256]{1,0:T(8,128)(2,1)S(1)} %get-tuple-element.91.refs_0_), channel_id=1, source_target_pairs={{0,24},{8,0},{16,8},{24,16},{1,25},{9,1},{17,9},{25,17},{2,26},{10... | collective-permute-start | bytes 393224 | tf_op jit(solution)/shard_map/ppermute | solution.py:421
  45.4 1.3 %collective-permute-start.13 = (bf16[256,256]{1,0:T(8,128)(2,1)S(1)}, bf16[256,256]{1,0:T(8,128)(2,1)S(1)}, u32[]{:S(2)}, u32[]{:S(2)}) collective-permute-start(bf16[256,256]{1,0:T(8,128)(2,1)S(1)} %get-tuple-element.91.refs_0_), channel_id=1, source_target_pairs={{0,16},{8,24},{16,0},{24,8},{1,17},{9,25},{17,1},{25,9},{2,18},{10... | collective-permute-start | bytes 393224 | tf_op jit(solution)/shard_map/ppermute | solution.py:421
  46.7 0.9 %collective-permute-start.12 = (bf16[256,256]{1,0:T(8,128)(2,1)S(1)}, bf16[256,256]{1,0:T(8,128)(2,1)S(1)}, u32[]{:S(2)}, u32[]{:S(2)}) collective-permute-start(bf16[256,256]{1,0:T(8,128)(2,1)S(1)} %get-tuple-element.91.refs_0_), channel_id=1, source_target_pairs={{0,8},{8,16},{16,24},{24,0},{1,9},{9,17},{17,25},{25,1},{2,10},{10... | collective-permute-start | bytes 393224 | tf_op jit(solution)/shard_map/ppermute | solution.py:421
  47.6 1.7 %collective-permute-done.14.refs_3_ = bf16[256,256]{1,0:T(8,128)(2,1)S(1)} collective-permute-done((bf16[256,256]{1,0:T(8,128)(2,1)S(1)}, bf16[256,256]{1,0:T(8,128)(2,1)S(1)}, u32[]{:S(2)}, u32[]{:S(2)}) %collective-permute-start.14) | collective-permute-done | bytes 131104 | tf_op jit(solution)/shard_map/ppermute | solution.py:421
  49.3 1.2 %collective-permute-done.13.refs_2_ = bf16[256,256]{1,0:T(8,128)(2,1)S(1)} collective-permute-done((bf16[256,256]{1,0:T(8,128)(2,1)S(1)}, bf16[256,256]{1,0:T(8,128)(2,1)S(1)}, u32[]{:S(2)}, u32[]{:S(2)}) %collective-permute-start.13) | collective-permute-done | bytes 131104 | tf_op jit(solution)/shard_map/ppermute | solution.py:421
  50.5 2.1 %collective-permute-done.12.refs_1_ = bf16[256,256]{1,0:T(8,128)(2,1)S(1)} collective-permute-done((bf16[256,256]{1,0:T(8,128)(2,1)S(1)}, bf16[256,256]{1,0:T(8,128)(2,1)S(1)}, u32[]{:S(2)}, u32[]{:S(2)}) %collective-permute-start.12) | collective-permute-done | bytes 131104 | tf_op jit(solution)/shard_map/ppermute | solution.py:421
  52.5 0.7 shard_map.198
  53.3 0.1 collective-permute-start.15
  53.3 0.7 shard_map.197.kept_ref
  54.1 1.4 %collective-permute-done.15.sent_ref.refs_3_ = bf16[1280,256]{1,0:T(8,128)(2,1)S(1)} collective-permute-done((bf16[1280,256]{1,0:T(8,128)(2,1)S(1)}, bf16[1280,256]{1,0:T(8,128)(2,1)S(1)}, u32[]{:S(2)}, u32[]{:S(2)}) %collective-permute-start.15) | collective-permute-done | bytes 655392 | tf_op jit(solution)/shard_map/ppermute | solution.py:428
  55.4 0.3 shard_map.199
  55.7 0.8 %collective-permute-start.16 = (bf16[256,256]{1,0:T(8,128)(2,1)S(1)}, bf16[256,256]{1,0:T(8,128)(2,1)S(1)}, u32[]{:S(2)}, u32[]{:S(2)}) collective-permute-start(bf16[256,256]{1,0:T(8,128)(2,1)S(1)} %get-tuple-element.94), channel_id=1, source_target_pairs={{0,2},{1,3},{2,0},{3,1},{4,6},{5,7},{6,4},{7,5},{8,10},{9,11},{10,... | collective-permute-start | bytes 393224 | tf_op jit(solution)/shard_map/ppermute | solution.py:440
  56.5 0.7 collective-permute-start.19
  57.2 2.8 %collective-permute-start.18 = (bf16[256,256]{1,0:T(8,128)(2,1)S(1)}, bf16[256,256]{1,0:T(8,128)(2,1)S(1)}, u32[]{:S(2)}, u32[]{:S(2)}) collective-permute-start(bf16[256,256]{1,0:T(8,128)(2,1)S(1)} %get-tuple-element.98), channel_id=1, source_target_pairs={{0,2},{1,3},{2,0},{3,1},{4,6},{5,7},{6,4},{7,5},{8,10},{9,11},{10,... | collective-permute-start | bytes 393224 | tf_op jit(solution)/shard_map/ppermute | solution.py:440
  60.0 1.3 %collective-permute-done.16.came_ref = bf16[256,256]{1,0:T(8,128)(2,1)S(1)} collective-permute-done((bf16[256,256]{1,0:T(8,128)(2,1)S(1)}, bf16[256,256]{1,0:T(8,128)(2,1)S(1)}, u32[]{:S(2)}, u32[]{:S(2)}) %collective-permute-start.16) | collective-permute-done | bytes 131104 | tf_op jit(solution)/shard_map/ppermute | solution.py:440
  61.4 1.5 %collective-permute-start.17 = (bf16[256,256]{1,0:T(8,128)(2,1)S(1)}, bf16[256,256]{1,0:T(8,128)(2,1)S(1)}, u32[]{:S(2)}, u32[]{:S(2)}) collective-permute-start(bf16[256,256]{1,0:T(8,128)(2,1)S(1)} %shard_map.200), channel_id=1, source_target_pairs={{0,4},{1,5},{2,6},{3,7},{4,0},{5,1},{6,2},{7,3},{8,12},{9,13},{10,... | collective-permute-start | bytes 393224 | tf_op jit(solution)/shard_map/ppermute | solution.py:425
  62.8 2.9 %shard_map.196 = (f32[2048,256]{1,0:T(8,128)S(1)}, f32[2048,256]{1,0:T(8,128)S(1)}, f32[2048,256]{1,0:T(8,128)S(1)}) custom-call(f32[2048,256]{1,0:T(8,128)S(1)} %copy-done, f32[2048,256]{1,0:T(8,128)S(1)} %get-tuple-element.64.state_ref, f32[2048,256]{1,0:T(8,128)S(1)} %get-tuple-element.84.speed_ref, f32[2048,256]{1,0:T(8,128)S(1)} %get-tuple-element.85.part_ref, ...), custom_call_target="tpu_custom_call" | custom-call | tf_op jit(solution)/shard_map/pallas_call | solution.py:32
  65.7 4.1 %collective-permute-done.18.refs_2_ = bf16[256,256]{1,0:T(8,128)(2,1)S(1)} collective-permute-done((bf16[256,256]{1,0:T(8,128)(2,1)S(1)}, bf16[256,256]{1,0:T(8,128)(2,1)S(1)}, u32[]{:S(2)}, u32[]{:S(2)}) %collective-permute-start.18) | collective-permute-done | bytes 131104 | tf_op jit(solution)/shard_map/ppermute | solution.py:440
  69.8 2.6 %shard_map.201 = (f32[2048,256]{1,0:T(8,128)}, f32[2048,256]{1,0:T(8,128)}) custom-call(f32[2048,256]{1,0:T(8,128)S(1)} %get-tuple-element.88.shift_ref, f32[2048,256]{1,0:T(8,128)S(1)} %get-tuple-element.86.scale_ref, f32[2048,256]{1,0:T(8,128)S(1)} %get-tuple-element.89.rest_ref, f32[2048,256]{1,0:T(8,128)S(1)} %get-tuple-element.90.slip_rest_ref, ...), custom_call_target="tpu_custom_call" | custom-call | tf_op jit(solution)/shard_map/pallas_call | solution.py:32
  (19 shorter events, 0.2 us)
Async XLA Ops:
  1.6 12.8 %collective-permute-start.2 = (bf16[128,512]{1,0:T(8,128)(2,1)S(1)}, bf16[128,512]{1,0:T(8,128)(2,1)S(1)}, u32[]{:S(2)}, u32[]{:S(2)}) collective-permute-start(bf16[128,512]{1,0:T(8,128)(2,1)S(1)} %get-tuple-element.69.refs_0_), channel_id=1, source_target_pairs={{0,6},{1,7},{2,0},{3,1},{4,2},{5,3},{6,4},{7,5},{8,14},{9,15},{10,... | collective-permute-start | bytes 393224 | tf_op jit(solution)/shard_map/ppermute | solution.py:425
  6.7 11.8 %collective-permute-start.1 = (bf16[128,512]{1,0:T(8,128)(2,1)S(1)}, bf16[128,512]{1,0:T(8,128)(2,1)S(1)}, u32[]{:S(2)}, u32[]{:S(2)}) collective-permute-start(bf16[128,512]{1,0:T(8,128)(2,1)S(1)} %get-tuple-element.69.refs_0_), channel_id=1, source_target_pairs={{0,4},{1,5},{2,6},{3,7},{4,0},{5,1},{6,2},{7,3},{8,12},{9,13},{10,... | collective-permute-start | bytes 393224 | tf_op jit(solution)/shard_map/ppermute | solution.py:425
  6.7 11.9 %collective-permute-start = (bf16[128,512]{1,0:T(8,128)(2,1)S(1)}, bf16[128,512]{1,0:T(8,128)(2,1)S(1)}, u32[]{:S(2)}, u32[]{:S(2)}) collective-permute-start(bf16[128,512]{1,0:T(8,128)(2,1)S(1)} %get-tuple-element.69.refs_0_), channel_id=1, source_target_pairs={{0,2},{1,3},{2,4},{3,5},{4,6},{5,7},{6,0},{7,1},{8,10},{9,11},{10,... | collective-permute-start | bytes 393224 | tf_op jit(solution)/shard_map/ppermute | solution.py:425
  7.8 3.3 %copy-start = (f32[2048,256]{1,0:T(8,128)S(1)}, f32[2048,256]{1,0:T(8,128)}, u32[]{:S(2)}) copy-start(f32[2048,256]{1,0:T(8,128)} %slip_ref.3) | copy-start | bytes 6291460
  7.8 3.3 %copy-start.2 = (bf16[32,2048]{1,0:T(8,128)(2,1)S(1)}, bf16[32,2048]{1,0:T(8,128)(2,1)}, u32[]{:S(2)}) copy-start(bf16[32,2048]{1,0:T(8,128)(2,1)} %basis_in_ref.1) | copy-start | bytes 393220
  11.5 7.1 %collective-permute-start.5 = (bf16[256,256]{1,0:T(8,128)(2,1)S(1)}, bf16[256,256]{1,0:T(8,128)(2,1)S(1)}, u32[]{:S(2)}, u32[]{:S(2)}) collective-permute-start(bf16[256,256]{1,0:T(8,128)(2,1)S(1)} %get-tuple-element.58.refs_9_.refs_0_), channel_id=1, source_target_pairs={{0,24},{8,0},{16,8},{24,16},{1,25},{9,1},{17,9},{25,17},{2,26},{10... | collective-permute-start | bytes 393224 | tf_op jit(solution)/shard_map/ppermute | solution.py:421
  13.9 7.2 %collective-permute-start.4 = (bf16[256,256]{1,0:T(8,128)(2,1)S(1)}, bf16[256,256]{1,0:T(8,128)(2,1)S(1)}, u32[]{:S(2)}, u32[]{:S(2)}) collective-permute-start(bf16[256,256]{1,0:T(8,128)(2,1)S(1)} %get-tuple-element.58.refs_9_.refs_0_), channel_id=1, source_target_pairs={{0,16},{8,24},{16,0},{24,8},{1,17},{9,25},{17,1},{25,9},{2,18},{10... | collective-permute-start | bytes 393224 | tf_op jit(solution)/shard_map/ppermute | solution.py:421
  14.5 6.7 %collective-permute-start.3 = (bf16[256,256]{1,0:T(8,128)(2,1)S(1)}, bf16[256,256]{1,0:T(8,128)(2,1)S(1)}, u32[]{:S(2)}, u32[]{:S(2)}) collective-permute-start(bf16[256,256]{1,0:T(8,128)(2,1)S(1)} %get-tuple-element.58.refs_9_.refs_0_), channel_id=1, source_target_pairs={{0,8},{8,16},{16,24},{24,0},{1,9},{9,17},{17,25},{25,1},{2,10},{10... | collective-permute-start | bytes 393224 | tf_op jit(solution)/shard_map/ppermute | solution.py:421
  21.8 2.2 %collective-permute-start.6 = (bf16[1280,256]{1,0:T(8,128)(2,1)S(1)}, bf16[1280,256]{1,0:T(8,128)(2,1)S(1)}, u32[]{:S(2)}, u32[]{:S(2)}) collective-permute-start(bf16[1280,256]{1,0:T(8,128)(2,1)S(1)} %shard_map.189), channel_id=1, source_target_pairs={{0,1},{1,0},{2,3},{3,2},{4,5},{5,4},{6,7},{7,6},{8,9},{9,8},{10,11... | collective-permute-start | bytes 1966088 | tf_op jit(solution)/shard_map/ppermute | solution.py:428
  22.0 11.6 %collective-permute-start.8 = (bf16[512,512]{1,0:T(8,128)(2,1)S(1)}, bf16[512,512]{1,0:T(8,128)(2,1)S(1)}, u32[]{:S(2)}, u32[]{:S(2)}) collective-permute-start(bf16[512,512]{1,0:T(8,128)(2,1)S(1)} %shard_map.192.own_ref), channel_id=1, source_target_pairs={{0,1},{1,0},{2,3},{3,2},{4,5},{5,4},{6,7},{7,6},{8,9},{9,8},{10,11... | collective-permute-start | bytes 1572872 | tf_op jit(solution)/shard_map/ppermute | solution.py:428
  24.3 6.8 %collective-permute-start.7 = (bf16[256,256]{1,0:T(8,128)(2,1)S(1)}, bf16[256,256]{1,0:T(8,128)(2,1)S(1)}, u32[]{:S(2)}, u32[]{:S(2)}) collective-permute-start(bf16[256,256]{1,0:T(8,128)(2,1)S(1)} %get-tuple-element.66), channel_id=1, source_target_pairs={{0,2},{1,3},{2,0},{3,1},{4,6},{5,7},{6,4},{7,5},{8,10},{9,11},{10,... | collective-permute-start | bytes 393224 | tf_op jit(solution)/shard_map/ppermute | solution.py:440
  26.8 11.0 %collective-permute-start.10 = (bf16[256,256]{1,0:T(8,128)(2,1)S(1)}, bf16[256,256]{1,0:T(8,128)(2,1)S(1)}, u32[]{:S(2)}, u32[]{:S(2)}) collective-permute-start(bf16[256,256]{1,0:T(8,128)(2,1)S(1)} %get-tuple-element.82), channel_id=1, source_target_pairs={{0,2},{1,3},{2,0},{3,1},{4,6},{5,7},{6,4},{7,5},{8,10},{9,11},{10,... | collective-permute-start | bytes 393224 | tf_op jit(solution)/shard_map/ppermute | solution.py:440
  31.1 8.7 %collective-permute-start.9 = (bf16[256,256]{1,0:T(8,128)(2,1)S(1)}, bf16[256,256]{1,0:T(8,128)(2,1)S(1)}, u32[]{:S(2)}, u32[]{:S(2)}) collective-permute-start(bf16[256,256]{1,0:T(8,128)(2,1)S(1)} %shard_map.194), channel_id=1, source_target_pairs={{0,4},{1,5},{2,6},{3,7},{4,0},{5,1},{6,2},{7,3},{8,12},{9,13},{10,... | collective-permute-start | bytes 393224 | tf_op jit(solution)/shard_map/ppermute | solution.py:425
  32.9 7.0 %collective-permute-start.11 = (bf16[256,256]{1,0:T(8,128)(2,1)S(1)}, bf16[256,256]{1,0:T(8,128)(2,1)S(1)}, u32[]{:S(2)}, u32[]{:S(2)}) collective-permute-start(bf16[256,256]{1,0:T(8,128)(2,1)S(1)} %get-tuple-element.83), channel_id=1, source_target_pairs={{1,2},{3,4},{5,6},{7,8},{9,10},{11,12},{13,14},{15,16},{17,18},{19... | collective-permute-start | bytes 393224 | tf_op jit(solution)/shard_map/ppermute | solution.py:432
  33.5 6.3 %copy-start.1 = (bf16[32,2048]{1,0:T(8,128)(2,1)S(1)}, bf16[32,2048]{1,0:T(8,128)(2,1)}, u32[]{:S(2)}) copy-start(bf16[32,2048]{1,0:T(8,128)(2,1)} %basis_out_ref.3) | copy-start | bytes 393220
  41.7 7.6 %collective-permute-start.14 = (bf16[256,256]{1,0:T(8,128)(2,1)S(1)}, bf16[256,256]{1,0:T(8,128)(2,1)S(1)}, u32[]{:S(2)}, u32[]{:S(2)}) collective-permute-start(bf16[256,256]{1,0:T(8,128)(2,1)S(1)} %get-tuple-element.91.refs_0_), channel_id=1, source_target_pairs={{0,24},{8,0},{16,8},{24,16},{1,25},{9,1},{17,9},{25,17},{2,26},{10... | collective-permute-start | bytes 393224 | tf_op jit(solution)/shard_map/ppermute | solution.py:421
  45.4 5.1 %collective-permute-start.13 = (bf16[256,256]{1,0:T(8,128)(2,1)S(1)}, bf16[256,256]{1,0:T(8,128)(2,1)S(1)}, u32[]{:S(2)}, u32[]{:S(2)}) collective-permute-start(bf16[256,256]{1,0:T(8,128)(2,1)S(1)} %get-tuple-element.91.refs_0_), channel_id=1, source_target_pairs={{0,16},{8,24},{16,0},{24,8},{1,17},{9,25},{17,1},{25,9},{2,18},{10... | collective-permute-start | bytes 393224 | tf_op jit(solution)/shard_map/ppermute | solution.py:421
  46.7 5.9 %collective-permute-start.12 = (bf16[256,256]{1,0:T(8,128)(2,1)S(1)}, bf16[256,256]{1,0:T(8,128)(2,1)S(1)}, u32[]{:S(2)}, u32[]{:S(2)}) collective-permute-start(bf16[256,256]{1,0:T(8,128)(2,1)S(1)} %get-tuple-element.91.refs_0_), channel_id=1, source_target_pairs={{0,8},{8,16},{16,24},{24,0},{1,9},{9,17},{17,25},{25,1},{2,10},{10... | collective-permute-start | bytes 393224 | tf_op jit(solution)/shard_map/ppermute | solution.py:421
  53.3 2.2 %collective-permute-start.15 = (bf16[1280,256]{1,0:T(8,128)(2,1)S(1)}, bf16[1280,256]{1,0:T(8,128)(2,1)S(1)}, u32[]{:S(2)}, u32[]{:S(2)}) collective-permute-start(bf16[1280,256]{1,0:T(8,128)(2,1)S(1)} %shard_map.198), channel_id=1, source_target_pairs={{0,1},{1,0},{2,3},{3,2},{4,5},{5,4},{6,7},{7,6},{8,9},{9,8},{10,11... | collective-permute-start | bytes 1966088 | tf_op jit(solution)/shard_map/ppermute | solution.py:428
  55.7 5.6 %collective-permute-start.16 = (bf16[256,256]{1,0:T(8,128)(2,1)S(1)}, bf16[256,256]{1,0:T(8,128)(2,1)S(1)}, u32[]{:S(2)}, u32[]{:S(2)}) collective-permute-start(bf16[256,256]{1,0:T(8,128)(2,1)S(1)} %get-tuple-element.94), channel_id=1, source_target_pairs={{0,2},{1,3},{2,0},{3,1},{4,6},{5,7},{6,4},{7,5},{8,10},{9,11},{10,... | collective-permute-start | bytes 393224 | tf_op jit(solution)/shard_map/ppermute | solution.py:440
  56.5 9.2 %collective-permute-start.19 = (bf16[256,256]{1,0:T(8,128)(2,1)S(1)}, bf16[256,256]{1,0:T(8,128)(2,1)S(1)}, u32[]{:S(2)}, u32[]{:S(2)}) collective-permute-start(bf16[256,256]{1,0:T(8,128)(2,1)S(1)} %get-tuple-element.99), channel_id=1, source_target_pairs={{1,2},{3,4},{5,6},{7,8},{9,10},{11,12},{13,14},{15,16},{17,18},{19... | collective-permute-start | bytes 393224 | tf_op jit(solution)/shard_map/ppermute | solution.py:432
  57.2 12.7 %collective-permute-start.18 = (bf16[256,256]{1,0:T(8,128)(2,1)S(1)}, bf16[256,256]{1,0:T(8,128)(2,1)S(1)}, u32[]{:S(2)}, u32[]{:S(2)}) collective-permute-start(bf16[256,256]{1,0:T(8,128)(2,1)S(1)} %get-tuple-element.98), channel_id=1, source_target_pairs={{0,2},{1,3},{2,0},{3,1},{4,6},{5,7},{6,4},{7,5},{8,10},{9,11},{10,... | collective-permute-start | bytes 393224 | tf_op jit(solution)/shard_map/ppermute | solution.py:440
  61.4 8.5 %collective-permute-start.17 = (bf16[256,256]{1,0:T(8,128)(2,1)S(1)}, bf16[256,256]{1,0:T(8,128)(2,1)S(1)}, u32[]{:S(2)}, u32[]{:S(2)}) collective-permute-start(bf16[256,256]{1,0:T(8,128)(2,1)S(1)} %shard_map.200), channel_id=1, source_target_pairs={{0,4},{1,5},{2,6},{3,7},{4,0},{5,1},{6,2},{7,3},{8,12},{9,13},{10,... | collective-permute-start | bytes 393224 | tf_op jit(solution)/shard_map/ppermute | solution.py:425
